TPU v7x, 128 devices: a whole 4x4x4 slice. The times are simulated.
128 devices in a mesh: lon: 16 (over y, z_lo, core), lat: 8 (over x, z_hi).
Axes of the slice: x: 4, y: 4, z: 4 (z_hi: 2, z_lo: 2; z = z_hi * 2 + z_lo), core: 2. Of those that a mesh axis runs over, the one named last changes fastest.
Arguments:
- initial_kelvin_map: float32 [1024, 512, 128], P('lon', 'lat'), may hold values from -6 to 6
- thermal_diffusivity_map: float32 [1024, 512, 128], P('lon', 'lat'), may hold values from 0.1 to 1
- interior_power_source: float32 [1024, 512, 128], P('lon', 'lat'), may hold values from -6 to 6
- earlier_east_west_basis: float32 [1024, 32], P('lon'), may hold values from -0.1875 to 0.1875
- earlier_north_south_basis: float32 [512, 32], P('lat'), may hold values from -0.25 to 0.25
- earlier_depthwise_basis: float32 [128, 32], replicated, may hold values from -0.5 to 0.5
Outputs:
- final_kelvin_map: float32 [1024, 512, 128], P('lon', 'lat')
- error: float32 [1024, 512, 128], P('lon', 'lat')
- new_lon: float32 [1024, 32], P('lon')
- new_lat: float32 [512, 32], P('lat')
- new_rad: float32 [128, 32], replicated
- core: float32 [32, 32, 32], replicated
All inputs are finite; a program needn't handle non-finite values.
Results may differ from a plain program's by a relative error of at most 0.02.
Values sent between devices are 32-bit elements; how exact they have to be, the bound alone decides.
No kernel may reach another device: no remote copies, remote signals or barrier semaphores. Data moves between devices by JAX's collectives and lax.ppermute only.
A program may use at most 64 MiB of HBM per device.

v0:
```python
import jax
import jax.numpy as jnp
from jax import lax
from jax.sharding import PartitionSpec as P

SHELL_LAYERS = 128
R = 32
STEPS = 4


highest = lax.Precision.HIGHEST
time_step = 0.15


def extended(x, sides, width, wrap):
    for axis, dim in sides:
        count, length = (lax.axis_size(axis), x.shape[dim])
        up = [(i, (i + 1) % count) for i in range(count if wrap else count - 1)]
        down = [(j, i) for i, j in up]
        last = lax.slice_in_dim(x, length - width, length, axis=dim)
        initial = lax.slice_in_dim(x, 0, width, axis=dim)
        before = lax.ppermute(last, axis, up)
        after = lax.ppermute(initial, axis, down)
        x = jnp.concatenate([before, x, after], axis=dim)
    return x


def harmonic(cond_a, cond_b):
    summed = cond_a + cond_b
    return 2.0 * cond_a * cond_b / jnp.where(summed > 0.0, summed, 1.0)


def advance(padded, cond_pad, interior_power_source):
    centre = padded[1:-1, 1:-1]
    kcentre = cond_pad[1:-1, 1:-1]
    change = interior_power_source
    pairs = (
        (padded[2:, 1:-1], cond_pad[2:, 1:-1]),
        (padded[:-2, 1:-1], cond_pad[:-2, 1:-1]),
        (padded[1:-1, 2:], cond_pad[1:-1, 2:]),
        (padded[1:-1, :-2], cond_pad[1:-1, :-2]),
    )
    for near_t, near_k in pairs:
        change = change + harmonic(kcentre, near_k) * (near_t - centre)
    radial_t = jnp.pad(centre, ((0, 0), (0, 0), (1, 1)))
    radial_k = jnp.pad(kcentre, ((0, 0), (0, 0), (1, 1)))
    change = change + harmonic(kcentre, radial_k[:, :, 2:]) * (radial_t[:, :, 2:] - centre)
    change = change + harmonic(kcentre, radial_k[:, :, :-2]) * (radial_t[:, :, :-2] - centre)
    return centre + time_step * change


def orthonormal(block, gram):
    factor_l = jnp.linalg.cholesky(gram)
    return lax.linalg.triangular_solve(
        factor_l, block, left_side=False, lower=True, transpose_a=True
    )


def local(
    initial_kelvin_map,
    thermal_diffusivity_map,
    interior_power_source,
    earlier_east_west_basis,
    earlier_north_south_basis,
    earlier_depthwise_basis,
):
    east_west_entries = initial_kelvin_map.shape[0]
    north_south_entries = initial_kelvin_map.shape[1]
    cond_lon = extended(thermal_diffusivity_map, (("lon", 0),), 1, True)
    cond_pad = extended(cond_lon, (("lat", 1),), 1, False)
    final_kelvin_map = initial_kelvin_map
    for step_index in range(STEPS):
        temp_lon = extended(final_kelvin_map, (("lon", 0),), 1, True)
        padded = extended(temp_lon, (("lat", 1),), 1, False)
        final_kelvin_map = advance(padded, cond_pad, interior_power_source)
    rad_proj = jnp.dot(
        final_kelvin_map.reshape(east_west_entries * north_south_entries, SHELL_LAYERS),
        earlier_depthwise_basis,
        precision=highest,
    ).reshape(east_west_entries, north_south_entries, R)
    modes = jnp.einsum(
        "ijb,ja->iab", rad_proj, earlier_north_south_basis, precision=highest
    ).reshape(east_west_entries, R * R)
    modes = lax.psum(modes, "lat")
    proj = lax.psum(jnp.dot(modes.T, earlier_east_west_basis, precision=highest), "lon")
    block = jnp.dot(modes, proj, precision=highest)
    gram = lax.psum(jnp.dot(block.T, block, precision=highest), "lon")
    new_lon = orthonormal(block, gram)
    modes = jnp.einsum("ijb,ia->jab", rad_proj, new_lon, precision=highest).reshape(
        north_south_entries, R * R
    )
    modes = lax.psum(modes, "lon")
    proj = lax.psum(jnp.dot(modes.T, earlier_north_south_basis, precision=highest), "lat")
    block = jnp.dot(modes, proj, precision=highest)
    gram = lax.psum(jnp.dot(block.T, block, precision=highest), "lat")
    new_lat = orthonormal(block, gram)
    lon_proj = jnp.dot(
        new_lon.T,
        final_kelvin_map.reshape(east_west_entries, north_south_entries * SHELL_LAYERS),
        precision=highest,
    ).reshape(R, north_south_entries, SHELL_LAYERS)
    local_modes = jnp.einsum("ajr,jb->rab", lon_proj, new_lat, precision=highest)
    modes = lax.psum(local_modes.reshape(SHELL_LAYERS, R * R), ("lon", "lat"))
    proj = jnp.dot(modes.T, earlier_depthwise_basis, precision=highest)
    block = jnp.dot(modes, proj, precision=highest)
    gram = jnp.dot(block.T, block, precision=highest)
    new_rad = orthonormal(block, gram)
    core = jnp.einsum("rab,rc->abc", modes.reshape(SHELL_LAYERS, R, R), new_rad, precision=highest)
    first = jnp.einsum("abc,rc->abr", core, new_rad, precision=highest)
    second = jnp.einsum("abr,jb->ajr", first, new_lat, precision=highest)
    recon = jnp.dot(
        new_lon, second.reshape(R, north_south_entries * SHELL_LAYERS), precision=highest
    ).reshape(east_west_entries, north_south_entries, SHELL_LAYERS)
    return (final_kelvin_map, final_kelvin_map - recon, new_lon, new_lat, new_rad, core)


def solution(mesh):
    in_specs = (
        P("lon", "lat", None),
        P("lon", "lat", None),
        P("lon", "lat", None),
        P("lon", None),
        P("lat", None),
        P(),
    )
    out_specs = (
        P("lon", "lat", None),
        P("lon", "lat", None),
        P("lon", None),
        P("lat", None),
        P(),
        P(),
    )
    return jax.shard_map(local, mesh=mesh, in_specs=in_specs, out_specs=out_specs, check_vma=False)
```

profile of v0, /device:TPU:1, one launch (start us, length us, event | category | flops | bytes accessed | tf_op | source)
XLA Modules:
  0.0 830.4 jit_solution(1771202771691080442)
XLA Ops:
  8.0 3.0 collective-permute-start.2
  11.8 2.4 collective-permute-start.1
  14.2 3.0 copy.52
  17.2 1.2 copy.78
  18.4 1.4 collective-permute-start.4
  19.9 6.1 collective-permute-start.6
  26.0 1.3 collective-permute-start.5
  27.3 6.4 collective-permute-start.7
  34.8 8.6 %fusion.5 = (f32[64,64,128]{2,0,1:T(8,128)S(1)}, f32[64,64,128]{2,0,1:T(8,128)S(1)}, f32[64,64,128]{2,0,1:T(8,128)S(1)}) fusion(f32[64,64,128]{2,0,1:T(8,128)S(1)} %copy.78, f32[66,1,128]{2,0,1:T(8,128)S(1)} %collective-permute-done.7, f32[1,64,128]{2,0,1:T(1,128)S(1)} %collective-permute-done.1, f32[1,64,128]{2,0,1:T(1,128)S(1)} %collective-permute-done.3, ...), kind=kLoop, calls=%fused_computation.21 | loop fusion | flops 35127296 | bytes 12849152 | tf_op jit(solution)/shard_map/add | solution.py:49
  43.9 1.6 collective-permute-start.8
  47.3 1.3 collective-permute-start.10
  48.6 7.4 collective-permute-start.11
  57.1 7.8 fusion.13
  65.3 3.5 collective-permute-start.12
  69.7 1.3 collective-permute-start.14
  71.0 7.7 collective-permute-start.15
  79.7 7.7 fusion.21
  87.8 4.7 collective-permute-start.16
  93.4 1.3 collective-permute-start.18
  94.7 7.0 collective-permute-start.19
  102.8 7.8 fusion.29
  110.6 6.7 fusion.124
  117.4 1.8 copy.83
  119.2 2.9 convolution_bitcast_fusion.1
  123.3 92.9 %all-reduce.11.cloned.1.call-done = f32[64,1024]{0,1:T(8,128)} async-done(((f32[64,1024]{0,1:T(8,128)}), f32[64,1024]{0,1:T(8,128)}) %all-reduce.11.cloned.1.call-update) | async-done | bytes 262160 | tf_op jit(solution)/shard_map/psum | solution.py:84
  216.2 2.4 fusion.133
  218.6 121.4 %all-reduce.13.cloned.1.call-done = f32[1024,32]{1,0:T(8,128)} async-done(((f32[1024,32]{1,0:T(8,128)}), f32[1024,32]{1,0:T(8,128)}) %all-reduce.13.cloned.1.call-update) | async-done | bytes 131088 | tf_op jit(solution)/shard_map/psum | solution.py:85
  340.0 2.2 fusion.134
  342.4 52.8 %psum.51 = f32[32,32]{0,1:T(8,128)S(1)} all-reduce(f32[32,32]{0,1:T(8,128)S(1)} %fusion.135), channel_id=1, replica_groups=mesh['lon'=16,'lat'=8] {'lon'}, use_global_device_ids=true, to_apply=%region_2.3 | all-reduce | flops 1024 | bytes 8192 | tf_op jit(solution)/shard_map/psum | solution.py:87
  395.2 2.9 cholesky.59
  399.5 2.4 custom-call.10
  403.9 10.0 %all-reduce.17.cloned.1.call-start = ((), (), s32[]{:S(2)}) async-start(), calls=%async_computation.3 | async-start | bytes 1048576 | tf_op jit(solution)/shard_map/psum | solution.py:93
  413.9 110.3 %all-reduce.15.cloned.1.call-done = f32[64,1024]{0,1:T(8,128)} async-done(((f32[64,1024]{0,1:T(8,128)}), f32[64,1024]{0,1:T(8,128)}) %all-reduce.15.cloned.1.call-update) | async-done | bytes 262160 | tf_op jit(solution)/shard_map/psum | solution.py:92
  524.2 2.4 fusion.136
  527.8 80.6 %all-reduce.17.cloned.1.call-done = f32[1024,32]{1,0:T(8,128)} async-done(((f32[1024,32]{1,0:T(8,128)}), f32[1024,32]{1,0:T(8,128)}) %all-reduce.17.cloned.1.call-update) | async-done | bytes 131088 | tf_op jit(solution)/shard_map/psum | solution.py:93
  608.4 2.2 fusion.137
  610.8 31.1 %psum.54 = f32[32,32]{0,1:T(8,128)S(1)} all-reduce(f32[32,32]{0,1:T(8,128)S(1)} %fusion.138), channel_id=1, replica_groups=mesh['lon'=16,'lat'=8] {'lat'}, use_global_device_ids=true, to_apply=%region_7.10 | all-reduce | flops 1024 | bytes 8192 | tf_op jit(solution)/shard_map/psum | solution.py:95
  642.0 2.9 cholesky.70
  646.2 2.4 custom-call.11
  648.9 2.0 fusion.99
  651.0 2.5 copy.94
  653.5 152.1 %all-reduce.19.cloned.1.call-done = f32[128,1024]{0,1:T(8,128)} async-done(((f32[128,1024]{0,1:T(8,128)}), f32[128,1024]{0,1:T(8,128)}) %all-reduce.19.cloned.1.call-update) | async-done | bytes 524304 | tf_op jit(solution)/shard_map/psum | solution.py:103
  805.6 1.7 fusion.139
  807.3 2.0 fusion.140
  809.6 2.9 cholesky.81
  813.8 2.4 custom-call.8
  818.7 2.4 convolution_subtract_fusion
  821.1 2.5 copy.95
  (92 shorter events, 22.3 us)
Async XLA Ops:
  7.2 103.4 %copy-start = (f32[128,32]{0,1:T(8,128)S(1)}, f32[128,32]{0,1:T(8,128)}, u32[]{:S(2)}) copy-start(f32[128,32]{0,1:T(8,128)} %param.14) | copy-start | bytes 49156
  7.2 209.0 %all-reduce.11.cloned.1.call-start = ((), (), s32[]{:S(2)}) async-start(), calls=%async_computation | async-start | bytes 1048576 | tf_op jit(solution)/shard_map/psum | solution.py:84
  8.0 10.4 %collective-permute-start.2 = (f32[1,64,128]{2,0,1:T(1,128)S(1)}, f32[1,64,128]{2,0,1:T(1,128)S(1)}, u32[]{:S(2)}, u32[]{:S(2)}) collective-permute-start(f32[1,64,128]{2,0,1:T(1,128)S(1)} %bitcast.136), channel_id=1, source_target_pairs={{0,8},{8,16},{16,24},{24,32},{32,40},{40,48},{48,56},{56,64},{64,7... | collective-permute-start | bytes 98312 | tf_op jit(solution)/shard_map/ppermute | solution.py:22
  11.0 7.4 collective-permute-start
  11.8 14.2 %collective-permute-start.1 = (f32[1,64,128]{2,0,1:T(1,128)S(1)}, f32[1,64,128]{2,0,1:T(1,128)S(1)}, u32[]{:S(2)}, u32[]{:S(2)}) collective-permute-start(f32[1,64,128]{2,0,1:T(1,128)S(1)} %bitcast.134), channel_id=1, source_target_pairs={{8,0},{16,8},{24,16},{32,24},{40,32},{48,40},{56,48},{64,56},{72,6... | collective-permute-start | bytes 98312 | tf_op jit(solution)/shard_map/ppermute | solution.py:23
  14.2 3.0 copy-start.3
  14.2 11.8 %collective-permute-start.3 = (f32[1,64,128]{2,0,1:T(1,128)S(1)}, f32[1,64,128]{2,0,1:T(1,128)S(1)}, u32[]{:S(2)}, u32[]{:S(2)}) collective-permute-start(f32[1,64,128]{2,0,1:T(1,128)S(1)} %bitcast.133), channel_id=1, source_target_pairs={{0,8},{8,16},{16,24},{24,32},{32,40},{40,48},{48,56},{56,64},{64,7... | collective-permute-start | bytes 98312 | tf_op jit(solution)/shard_map/ppermute | solution.py:22
  18.4 16.4 %copy-start.1 = (f32[64,64,128]{2,1,0:T(8,128)S(1)}, f32[64,64,128]{2,1,0:T(8,128)}, u32[]{:S(2)}) copy-start(f32[64,64,128]{2,1,0:T(8,128)} %param.11) | copy-start | bytes 6291460
  18.4 15.3 %collective-permute-start.4 = (f32[66,1,128]{2,0,1:T(8,128)S(1)}, f32[66,1,128]{2,0,1:T(8,128)S(1)}, u32[]{:S(2)}, u32[]{:S(2)}) collective-permute-start(f32[66,1,128]{2,0,1:T(8,128)S(1)} %get-tuple-element.29), channel_id=1, source_target_pairs={{1,0},{2,1},{3,2},{4,3},{5,4},{6,5},{7,6},{9,8},{10,9},{11,10},{12... | collective-permute-start | bytes 101384 | tf_op jit(solution)/shard_map/ppermute | solution.py:23
  19.9 13.9 %collective-permute-start.6 = (f32[66,1,128]{2,0,1:T(8,128)S(1)}, f32[66,1,128]{2,0,1:T(8,128)S(1)}, u32[]{:S(2)}, u32[]{:S(2)}) collective-permute-start(f32[66,1,128]{2,0,1:T(8,128)S(1)} %get-tuple-element.30), channel_id=1, source_target_pairs={{0,1},{1,2},{2,3},{3,4},{4,5},{5,6},{6,7},{8,9},{9,10},{10,11},{11... | collective-permute-start | bytes 101384 | tf_op jit(solution)/shard_map/ppermute | solution.py:22
  26.0 7.7 collective-permute-start.5
  27.3 7.4 collective-permute-start.7
  43.4 2.7 collective-permute-start.9
  43.9 3.3 collective-permute-start.8
  47.3 8.8 %collective-permute-start.10 = (f32[66,1,128]{2,0,1:T(8,128)S(1)}, f32[66,1,128]{2,0,1:T(8,128)S(1)}, u32[]{:S(2)}, u32[]{:S(2)}) collective-permute-start(f32[66,1,128]{2,0,1:T(8,128)S(1)} %get-tuple-element.27), channel_id=1, source_target_pairs={{1,0},{2,1},{3,2},{4,3},{5,4},{6,5},{7,6},{9,8},{10,9},{11,10},{12... | collective-permute-start | bytes 101384 | tf_op jit(solution)/shard_map/ppermute | solution.py:23
  48.6 8.5 %collective-permute-start.11 = (f32[66,1,128]{2,0,1:T(8,128)S(1)}, f32[66,1,128]{2,0,1:T(8,128)S(1)}, u32[]{:S(2)}, u32[]{:S(2)}) collective-permute-start(f32[66,1,128]{2,0,1:T(8,128)S(1)} %get-tuple-element.28), channel_id=1, source_target_pairs={{0,1},{1,2},{2,3},{3,4},{4,5},{5,6},{6,7},{8,9},{9,10},{10,11},{11... | collective-permute-start | bytes 101384 | tf_op jit(solution)/shard_map/ppermute | solution.py:22
  64.9 4.5 collective-permute-start.13
  65.3 4.4 collective-permute-start.12
  69.7 9.0 %collective-permute-start.14 = (f32[66,1,128]{2,0,1:T(8,128)S(1)}, f32[66,1,128]{2,0,1:T(8,128)S(1)}, u32[]{:S(2)}, u32[]{:S(2)}) collective-permute-start(f32[66,1,128]{2,0,1:T(8,128)S(1)} %get-tuple-element.25), channel_id=1, source_target_pairs={{1,0},{2,1},{3,2},{4,3},{5,4},{6,5},{7,6},{9,8},{10,9},{11,10},{12... | collective-permute-start | bytes 101384 | tf_op jit(solution)/shard_map/ppermute | solution.py:23
  71.0 8.8 %collective-permute-start.15 = (f32[66,1,128]{2,0,1:T(8,128)S(1)}, f32[66,1,128]{2,0,1:T(8,128)S(1)}, u32[]{:S(2)}, u32[]{:S(2)}) collective-permute-start(f32[66,1,128]{2,0,1:T(8,128)S(1)} %get-tuple-element.26), channel_id=1, source_target_pairs={{0,1},{1,2},{2,3},{3,4},{4,5},{5,6},{6,7},{8,9},{9,10},{10,11},{11... | collective-permute-start | bytes 101384 | tf_op jit(solution)/shard_map/ppermute | solution.py:22
  87.5 5.4 collective-permute-start.17
  87.8 5.6 collective-permute-start.16
  93.4 8.3 collective-permute-start.18
  94.7 8.0 collective-permute-start.19
  110.6 8.5 %copy-start.7 = (f32[64,32]{0,1:T(8,128)S(1)}, f32[64,32]{0,1:T(8,128)}, u32[]{:S(2)}) copy-start(f32[64,32]{0,1:T(8,128)} %param.13) | copy-start | bytes 24580
  119.1 97.0 %copy-start.9 = (f32[64,32]{0,1:T(8,128)S(1)}, f32[64,32]{0,1:T(8,128)}, u32[]{:S(2)}) copy-start(f32[64,32]{0,1:T(8,128)} %param.12) | copy-start | bytes 24580
  123.2 216.8 %all-reduce.13.cloned.1.call-start = ((), (), s32[]{:S(2)}) async-start(), calls=%async_computation.1 | async-start | bytes 1048576 | tf_op jit(solution)/shard_map/psum | solution.py:85
  218.6 305.6 %all-reduce.15.cloned.1.call-start = ((), (), s32[]{:S(2)}) async-start(), calls=%async_computation.2 | async-start | bytes 1048576 | tf_op jit(solution)/shard_map/psum | solution.py:92
  402.2 416.5 %copy-start.5 = (f32[32,64]{1,0:T(8,128)}, f32[32,64]{1,0:T(8,128)S(1)}, u32[]{:S(2)}) copy-start(f32[32,64]{1,0:T(8,128)S(1)} %fusion.120) | copy-start | bytes 24580
  403.9 204.5 %all-reduce.17.cloned.1.call-start = ((), (), s32[]{:S(2)}) async-start(), calls=%async_computation.3 | async-start | bytes 1048576 | tf_op jit(solution)/shard_map/psum | solution.py:93
  526.6 279.0 %all-reduce.19.cloned.1.call-start = ((), (), s32[]{:S(2)}) async-start(), calls=%async_computation.4 | async-start | bytes 1048576 | tf_op jit(solution)/shard_map/psum | solution.py:103
  648.9 168.7 %copy-start.6 = (f32[32,64]{1,0:T(8,128)}, f32[32,64]{1,0:T(8,128)S(1)}, u32[]{:S(2)}) copy-start(f32[32,64]{1,0:T(8,128)S(1)} %fusion.114) | copy-start | bytes 24580
  805.6 10.9 %copy-start.2 = (f32[128,1024]{0,1:T(8,128)S(1)}, f32[128,1024]{0,1:T(8,128)}, u32[]{:S(2)}) copy-start(f32[128,1024]{0,1:T(8,128)} %all-reduce.19.cloned.1.call-done) | copy-start | bytes 1572868
  816.5 4.6 copy-start.8
  817.1 4.0 copy-start.4
Sparse Core Ops, SparseCore 0:
  123.3 92.7 all-reduce.10
  219.3 120.6 all-reduce.12
  404.1 120.0 all-reduce.14
  527.3 81.1 all-reduce.16
  651.1 154.4 all-reduce.18
where the time goes:
time: 840 us; the launch traced here: 830 us
  waiting for transfers between devices  565 us (67%)
  blocking collectives  83.9 us (10%)
  starting transfers between devices  67.7 us (8%)
  other arithmetic  52.1 us (6%)
  matrix products  32 us (4%)
  local copies, waits for them, and re-layouts  15.2 us (2%)
  between operations  14.5 us (2%)
    psum x1, waiting for transfers between devices, local(): modes = lax.psum(local_modes.reshape(SHELL_LAYERS, R * R), ('lon', 'lat'))  152 us
    psum x1, waiting for transfers between devices, local(): lax.psum(jnp.dot(modes.T, earlier_east_west_basis, precision=highest), 'l...  121 us
    psum x1, waiting for transfers between devices, local(): modes = lax.psum(modes, 'lon')  110 us
    psum x1, waiting for transfers between devices, local(): modes = lax.psum(modes, 'lat')  92.9 us
    psum x1, waiting for transfers between devices, local(): lax.psum(jnp.dot(modes.T, earlier_north_south_basis, precision=highest),...  80.6 us
    psum x1, blocking collectives, local(): gram = lax.psum(jnp.dot(block.T, block, precision=highest), 'lon')  52.8 us
    ppermute x10, starting transfers between devices, extended(): before = lax.ppermute(last, axis, up)  38.8 us
    add x4, other arithmetic, advance(): return centre + time_step * change  32 us
  transfers between devices with their start and end apart: 25, of which 15 were waited for; matrix products, arithmetic and copies ran while one was open for 1% of the time, Pallas kernels for 0%

commit v1 on v0

v1 whole, which is shorter than its diff:
```python
import functools

import jax
import jax.numpy as jnp
from jax import lax
from jax.experimental import pallas as pl
from jax.experimental.pallas import tpu as pltpu
from jax.sharding import PartitionSpec as P

SHELL_LAYERS = 128
R = 32
STEPS = 4
time_step = 0.15
highest = lax.Precision.HIGHEST
W = STEPS


def dot(a, b, ca, cb):
    return lax.dot_general(
        a, b, (((ca,), (cb,)), ((), ())), precision=highest, preferred_element_type=jnp.float32
    )


def face(p, q):
    summed = p + q
    return (2.0 * time_step) * p * q / jnp.where(summed > 0.0, summed, 1.0)


def conduct_kernel(n, m, t_ref, k_ref, s_ref, below_ref, above_ref, south_ref, north_ref,
                   ssouth_ref, snorth_ref, out_ref, t, k, s, hx, hy, hz):
    rows = m + 2 * W
    layers = t_ref.shape[2]
    tile = (2 * W, layers)
    first = lax.broadcasted_iota(jnp.int32, tile, 0) < W
    half = (n + 2 * W) // 2

    def inner(i, c):
        t[i + W, 0:m, :] = t_ref[i]
        k[i + W, 0:m, :] = k_ref[i]
        s[i + W, 0:m, :] = s_ref[i] * time_step
        return c

    lax.fori_loop(0, n, inner, 0, unroll=2)
    for i in range(W):
        t[i, 0:m, :] = below_ref[i]
        k[i, 0:m, :] = below_ref[W + i]
        t[n + W + i, 0:m, :] = above_ref[i]
        k[n + W + i, 0:m, :] = above_ref[W + i]
        s[i, 0:m, :] = below_ref[2 * W + i] * time_step
        s[n + W + i, 0:m, :] = above_ref[2 * W + i] * time_step

    def edge(i, c):
        south, north = south_ref[i], north_ref[i]
        t[i, m:rows, :] = jnp.where(first, north, south)
        k[i, m:rows, :] = pltpu.roll(jnp.where(first, south, north), W, 0)
        return c

    lax.fori_loop(0, n + 2 * W, edge, 0, unroll=2)

    def edge_s(i, c):
        south, north = ssouth_ref[i] * time_step, snorth_ref[i] * time_step
        s[i, m:rows, :] = jnp.where(first, north, pltpu.roll(south, W, 0))
        s[i + half, m:rows, :] = jnp.where(first, pltpu.roll(north, W, 0), south)
        return c

    lax.fori_loop(0, half, edge_s, 0, unroll=2)

    inside = lax.broadcasted_iota(jnp.int32, (rows, layers), 1) < layers - 1

    def faces(i, c):
        kc = k[i]
        hx[i] = face(kc, k[jnp.minimum(i + 1, n + 2 * W - 1)])
        hy[i] = face(kc, pltpu.roll(kc, rows - 1, 0))
        hz[i] = jnp.where(inside, face(kc, pltpu.roll(kc, layers - 1, 1)), 0.0)
        return c

    lax.fori_loop(0, n + 2 * W, faces, 0)

    for step in range(STEPS):
        last = step == STEPS - 1

        def body(p, carry):
            tc, fprev = carry
            tn = t[p + 1]
            fx = hx[p] * (tn - tc)
            fy = hy[p] * (pltpu.roll(tc, rows - 1, 0) - tc)
            fz = hz[p] * (pltpu.roll(tc, layers - 1, 1) - tc)
            new = tc + (
                (s[p] + (fx - fprev))
                + ((fy - pltpu.roll(fy, 1, 0)) + (fz - pltpu.roll(fz, 1, 1)))
            )
            if last:
                out_ref[p - W] = new[0:m]
            else:
                t[p] = new
            return tn, fx

        tc = t[step + 1]
        lax.fori_loop(
            step + 1, n + 2 * W - 1 - step, body, (tc, hx[step] * (tc - t[step])), unroll=2
        )


def conduct(t, k, s):
    n, m, layers = t.shape
    lon, lat = lax.axis_size("lon"), lax.axis_size("lat")
    up = [(i, (i + 1) % lon) for i in range(lon)]
    down = [(j, i) for i, j in up]
    below = lax.ppermute(jnp.concatenate([t[n - W:], k[n - W:], s[n - W:]], 0), "lon", up)
    above = lax.ppermute(jnp.concatenate([t[:W], k[:W], s[:W]], 0), "lon", down)

    def ext(x, q, lo):
        rows = slice(0, W) if lo else slice(m - W, m)
        return jnp.concatenate(
            [below[q * W:q * W + W, rows], x[:, rows], above[q * W:q * W + W, rows]], 0
        )

    north_to = [(i, i + 1) for i in range(lat - 1)]
    south_to = [(j, i) for i, j in north_to]
    half = (n + 2 * W) // 2
    low_s, high_s = ext(s, 2, True), ext(s, 2, False)
    south = lax.ppermute(jnp.concatenate([ext(k, 1, False), ext(t, 0, False)], 1), "lat", north_to)
    north = lax.ppermute(jnp.concatenate([ext(t, 0, True), ext(k, 1, True)], 1), "lat", south_to)
    ssouth = lax.ppermute(jnp.concatenate([high_s[:half], high_s[half:]], 1), "lat", north_to)
    snorth = lax.ppermute(jnp.concatenate([low_s[:half], low_s[half:]], 1), "lat", south_to)
    big = pltpu.VMEM((n + 2 * W, m + 2 * W, layers), jnp.float32)
    return pl.pallas_call(
        functools.partial(conduct_kernel, n, m),
        out_shape=jax.ShapeDtypeStruct(t.shape, jnp.float32),
        in_specs=[pl.BlockSpec(memory_space=pltpu.VMEM)] * 9,
        out_specs=pl.BlockSpec(memory_space=pltpu.VMEM),
        scratch_shapes=[big] * 6,
        compiler_params=pltpu.CompilerParams(vmem_limit_bytes=48 * 2**20),
        name="conduct",
    )(t, k, s, below, above, south, north, ssouth, snorth)


def inverse_factor(gram):
    n = gram.shape[0]
    row = lax.broadcasted_iota(jnp.int32, (n, n), 0)
    col = lax.broadcasted_iota(jnp.int32, (n, n), 1)
    a = gram
    inv = jnp.where(row == col, 1.0, 0.0).astype(jnp.float32)
    scale = jnp.zeros((n, 1), jnp.float32)
    r1 = lax.broadcasted_iota(jnp.int32, (n, 1), 0)
    for j in range(n):
        column = a[:, j:j + 1]
        pivot = a[j:j + 1, j:j + 1]
        factor = jnp.where(r1 > j, column / pivot, 0.0)
        scale = jnp.where(r1 == j, lax.rsqrt(pivot), scale)
        a = a - factor * a[j:j + 1, :]
        inv = inv - factor * inv[j:j + 1, :]
    return inv * scale


def inverse_kernel(g_ref, o_ref):
    o_ref[...] = inverse_factor(g_ref[...])


def inverse(gram):
    return pl.pallas_call(
        inverse_kernel, out_shape=jax.ShapeDtypeStruct(gram.shape, jnp.float32), name="inverse"
    )(gram)


def scatter_sum(parts, axis):
    return jnp.sum(lax.all_to_all(parts, axis, 0, 0, tiled=True), axis=0)


def gather(part, axis):
    count = lax.axis_size(axis)
    return lax.all_to_all(
        jnp.broadcast_to(part[None], (count,) + part.shape), axis, 0, 0, tiled=True
    )


def total(part, axis):
    return jnp.sum(gather(part, axis), axis=0)


def local(t0, k, s, u, v, w):
    n, m, layers = t0.shape
    lon, lat = lax.axis_size("lon"), lax.axis_size("lat")
    t = conduct(t0, k, s)
    rad = dot(t.reshape(n * m, layers), w, 1, 0).reshape(n, m, R)
    parts = jnp.einsum("ijb,ja->iab", rad, v, precision=highest)
    parts = parts.reshape(n, lat, R // lat * R).transpose(1, 0, 2)
    y1 = scatter_sum(parts, "lat")
    proj = total(dot(u, y1, 0, 0), "lon")
    b1 = total(dot(proj, y1, 1, 1), "lat")
    g1 = dot(b1, b1, 1, 1)
    bs = R // lon
    parts = jnp.einsum("ijb,ci->bjc", rad, b1, precision=highest).reshape(lon, bs * m * R // 128, 128)
    parts = jnp.concatenate(
        [parts, jnp.broadcast_to(g1.reshape(1, R * R // 128, 128), (lon, R * R // 128, 128))], 1
    )
    got = scatter_sum(parts, "lon")
    y2 = got[: bs * m * R // 128].reshape(bs * m, R)
    inv1 = inverse(got[bs * m * R // 128:].reshape(R, R))
    new_lon = dot(b1, inv1, 0, 1)
    y2 = dot(y2, inv1, 1, 1).reshape(bs, m, R)
    proj = total(jnp.einsum("jc,bja->cba", v, y2, precision=highest).reshape(R, bs * R), "lat")
    b2 = jnp.einsum("bja,cba->cj", y2, proj.reshape(R, bs, R), precision=highest)
    b2 = total(b2.reshape(R * m // 128, 128), "lon").reshape(R, m)
    g2 = dot(b2, b2, 1, 1)
    lonp = jnp.einsum("ia,ijr->ajr", new_lon, t, precision=highest)
    parts = jnp.einsum("ajr,bj->arb", lonp, b2, precision=highest)
    parts = parts.reshape(lon, (R // lon) * layers * R // 128, 128)
    got = scatter_sum(parts, "lon")
    size = got.shape[0]
    got = total(jnp.concatenate([got, g2.reshape(R * R // 128, 128)], 0), "lat")
    y3 = gather(got[:size], "lon").reshape(R * layers, R)
    inv2 = inverse(got[size:].reshape(R, R))
    new_lat = dot(b2, inv2, 0, 1)
    y3 = dot(y3, inv2, 1, 1).reshape(R, layers, R)
    proj = jnp.einsum("arb,rc->cab", y3, w, precision=highest)
    b3 = jnp.einsum("arb,cab->rc", y3, proj, precision=highest)
    inv3 = inverse(dot(b3, b3, 0, 0))
    new_rad = dot(b3, inv3, 1, 1)
    core = jnp.einsum("arb,rc->abc", y3, new_rad, precision=highest)
    first = jnp.einsum("abc,rc->abr", core, new_rad, precision=highest)
    second = jnp.einsum("abr,jb->ajr", first, new_lat, precision=highest)
    recon = dot(new_lon, second.reshape(R, m * layers), 1, 0).reshape(n, m, layers)
    return (t, t - recon, new_lon, new_lat, new_rad, core)


def solution(mesh):
    grid = P("lon", "lat", None)
    return jax.shard_map(
        local,
        mesh=mesh,
        in_specs=(grid, grid, grid, P("lon", None), P("lat", None), P()),
        out_specs=(grid, grid, P("lon", None), P("lat", None), P(), P()),
        check_vma=False,
    )
```

time: 840 us -> 236 us (0.28); the launches traced: 830 us -> 235 us
  waiting for transfers between devices: 565 us -> 40.1 us
  other arithmetic: 52.1 us -> 4.69 us
  Pallas kernels: 0 us -> 44.1 us
  starting transfers between devices: 67.7 us -> 34.8 us
  blocking collectives: 83.9 us -> 60.3 us
  between operations: 14.5 us -> 1.2 us
    psum x5 -> x0, waiting for transfers between devices: 557 us -> none  [the longest x1 152 us: local(): modes = lax.psum(local_modes.reshape(SHELL_LAYERS, R * R), ('lon', 'lat'))]
    psum x2 -> x0, blocking collectives: 83.9 us -> none  [the longest x1 52.8 us: local(): gram = lax.psum(jnp.dot(block.T, block, precision=highest), 'lon')]
    all_to_all x0 -> x5, blocking collectives: none -> 60.3 us  [the longest x3 33.4 us: gather(): lax.all_to_all(jnp.broadcast_to(part[None], (count,) + part.shape), axis,...]
    pallas_call x0 -> x4, Pallas kernels: none -> 44.1 us  [the longest x1 32 us: conduct(): pl.pallas_call(functools.partial(conduct_kernel, n, m), out_shape=jax.Sha...]
    ppermute x20 -> x6, starting transfers between devices: 57.5 us -> 16.7 us  [the longest x1 5.5 us: conduct(): lax.ppermute(jnp.concatenate([high_s[:half], high_s[half:]], 1), 'lat', n...]
    add x4 -> x0, other arithmetic: 32 us -> none  [advance(): return centre + time_step * change]
    all_to_all x0 -> x4, waiting for transfers between devices: none -> 23 us  [the longest x3 13.6 us: gather(): lax.all_to_all(jnp.broadcast_to(part[None], (count,) + part.shape), axis,...]
    another operation x15 -> x0, other arithmetic: 20 us -> none  [the longest x9 10.8 us: orthonormal(): factor_l = jnp.linalg.cholesky(gram)]
  transfers between devices with their start and end apart: 25 -> 10, of which waited for: 15 -> 7; matrix products, arithmetic and copies ran while one was open for 1% -> 3% of each run, Pallas kernels for 0% -> 2%
where the time goes in v1:
time: 236 us; the launch traced here: 235 us
  blocking collectives  60.3 us (26%)
  Pallas kernels  44.1 us (19%)
  waiting for transfers between devices  40.1 us (17%)
  starting transfers between devices  34.8 us (15%)
  matrix products  34.3 us (15%)
  local copies, waits for them, and re-layouts  15.4 us (7%)
  other arithmetic  4.69 us (2%)
    all_to_all x3, blocking collectives, gather(): lax.all_to_all(jnp.broadcast_to(part[None], (count,) + part.shape), axis,...  33.4 us
    pallas_call x1, Pallas kernels, conduct(): pl.pallas_call(functools.partial(conduct_kernel, n, m), out_shape=jax.Sha...  32 us
    all_to_all x2, blocking collectives, scatter_sum(): return jnp.sum(lax.all_to_all(parts, axis, 0, 0, tiled=True), axis=0)  26.9 us
    dot_general x12, matrix products, dot(): lax.dot_general(a, b, (((ca,), (cb,)), ((), ())), precision=highest, pref...  18.6 us
    all_to_all x3, starting transfers between devices, gather(): lax.all_to_all(jnp.broadcast_to(part[None], (count,) + part.shape), axis,...  14.3 us
    all_to_all x3, waiting for transfers between devices, gather(): lax.all_to_all(jnp.broadcast_to(part[None], (count,) + part.shape), axis,...  13.6 us
    pallas_call x3, Pallas kernels, inverse(): pl.pallas_call(inverse_kernel, out_shape=jax.ShapeDtypeStruct(gram.shape,...  12.1 us
    all_to_all x1, waiting for transfers between devices, scatter_sum(): return jnp.sum(lax.all_to_all(parts, axis, 0, 0, tiled=True), axis=0)  9.39 us
  transfers between devices with their start and end apart: 10, of which 7 were waited for; matrix products, arithmetic and copies ran while one was open for 3% of the time, Pallas kernels for 2%

profile of v1, /device:TPU:1, one launch (start us, length us, event | category | flops | bytes accessed | tf_op | source)
XLA Modules:
  0.0 235.0 jit_solution(9659408805862636089)
XLA Ops:
  0.7 1.1 fusion.36
  1.8 1.1 fusion.34
  3.0 3.1 %collective-permute-start = (f32[12,64,128]{2,1,0:T(8,128)S(1)}, f32[12,64,128]{2,1,0:T(8,128)S(1)}, u32[]{:S(2)}, u32[]{:S(2)}) collective-permute-start(f32[12,64,128]{2,1,0:T(8,128)S(1)} %pad_maximum_fusion), channel_id=1, source_target_pairs={{0,8},{8,16},{16,24},{24,32},{32,40},{40,48},{48,56},{56,64},{64,7... | collective-permute-start | bytes 1179656 | tf_op jit(solution)/shard_map/ppermute | solution.py:109
  6.2 1.3 fusion.32
  7.5 1.1 fusion.31
  8.5 6.5 %collective-permute-done.below_ref = f32[12,64,128]{2,1,0:T(8,128)S(1)} collective-permute-done((f32[12,64,128]{2,1,0:T(8,128)S(1)}, f32[12,64,128]{2,1,0:T(8,128)S(1)}, u32[]{:S(2)}, u32[]{:S(2)}) %collective-permute-start) | collective-permute-done | bytes 393248 | tf_op jit(solution)/shard_map/ppermute | solution.py:109
  15.0 2.3 collective-permute-done.1.above_ref
  17.4 5.5 %collective-permute-start.2 = (f32[72,8,128]{2,1,0:T(8,128)S(1)}, f32[72,8,128]{2,1,0:T(8,128)S(1)}, u32[]{:S(2)}, u32[]{:S(2)}) collective-permute-start(f32[72,8,128]{2,1,0:T(8,128)S(1)} %maximum_maximum_fusion), channel_id=1, source_target_pairs={{0,1},{1,2},{2,3},{3,4},{4,5},{5,6},{6,7},{8,9},{9,10},{10,11},{11... | collective-permute-start | bytes 884744 | tf_op jit(solution)/shard_map/ppermute | solution.py:122
  23.0 1.3 collective-permute-start.3
  24.3 5.5 %collective-permute-start.4 = (f32[36,8,128]{2,1,0:T(8,128)S(1)}, f32[36,8,128]{2,1,0:T(8,128)S(1)}, u32[]{:S(2)}, u32[]{:S(2)}) collective-permute-start(f32[36,8,128]{2,1,0:T(8,128)S(1)} %fusion.10), channel_id=1, source_target_pairs={{0,1},{1,2},{2,3},{3,4},{4,5},{5,6},{6,7},{8,9},{9,10},{10,11},{11... | collective-permute-start | bytes 442376 | tf_op jit(solution)/shard_map/ppermute | solution.py:124
  29.9 1.3 collective-permute-start.5
  31.2 8.3 %collective-permute-done.4.ssouth_ref = f32[36,8,128]{2,1,0:T(8,128)S(1)} collective-permute-done((f32[36,8,128]{2,1,0:T(8,128)S(1)}, f32[36,8,128]{2,1,0:T(8,128)S(1)}, u32[]{:S(2)}, u32[]{:S(2)}) %collective-permute-start.4) | collective-permute-done | bytes 147488 | tf_op jit(solution)/shard_map/ppermute | solution.py:124
  39.5 32.0 %conduct.1 = f32[64,64,128]{2,1,0:T(8,128)} custom-call(f32[64,64,128]{2,1,0:T(8,128)S(1)} %copy-done.1, f32[64,64,128]{2,1,0:T(8,128)S(1)} %copy-done.2, f32[64,64,128]{2,1,0:T(8,128)} %s_ref.1, f32[12,64,128]{2,1,0:T(8,128)S(1)} %collective-permute-done.below_ref, f32[12,64,128]{2,1,0:T(8,128)S(1)} %collective-permute-done.1.above_ref, ...), custom_call_target="tpu_custom_call" | custom-call | tf_op jit(solution)/shard_map/conduct/pallas_call | solution.py:127
  71.5 7.4 %fusion.29 = f32[64,64,32]{1,2,0:T(8,128)S(1)} fusion(f32[64,64,128]{2,1,0:T(8,128)} %conduct.1, f32[128,32]{0,1:T(8,128)S(1)} %copy-done), kind=kOutput, calls=%fused_computation.47 | convolution fusion | flops 201326592 | bytes 2637824 | tf_op jit(solution)/shard_map/dot_general | solution.py:19
  78.9 3.1 %convolution_bitcast_fusion.2 = f32[64,32,32]{0,1,2:T(8,128)S(1)} fusion(f32[64,64,32]{1,2,0:T(8,128)S(1)} %fusion.29, f32[64,32]{0,1:T(8,128)S(1)} %copy-done.8), kind=kOutput, calls=%fused_computation.5 | convolution fusion | flops 50331648 | bytes 794624 | tf_op jit(solution)/shard_map/ijb,ja->iab/dot_general | solution.py:186
  82.6 14.5 %all_to_all.45 = f32[8,64,128]{2,1,0:T(8,128)S(1)} all-to-all(f32[8,64,128]{2,1,0:T(8,128)S(1)} %copy.47), channel_id=1, replica_groups=mesh['lon'=16,'lat'=8] {'lat'}, dimensions={0} | all-to-all | bytes 524288 | tf_op jit(solution)/shard_map/all_to_all | solution.py:167
  97.2 13.2 %all_to_all.46 = f32[16,32,128]{2,1,0:T(8,128)S(1)} all-to-all(f32[16,32,128]{2,1,0:T(8,128)S(1)} %broadcast_in_dim.20), channel_id=1, replica_groups=mesh['lon'=16,'lat'=8] {'lon'}, dimensions={0} | all-to-all | bytes 524288 | tf_op jit(solution)/shard_map/all_to_all | solution.py:172
  110.7 9.8 %all_to_all.47 = f32[8,1,2048]{2,1,0:T(1,128)S(1)} all-to-all(f32[8,1,2048]{2,1,0:T(1,128)S(1)} %reshape.82), channel_id=1, replica_groups=mesh['lon'=16,'lat'=8] {'lat'}, dimensions={0} | all-to-all | bytes 131072 | tf_op jit(solution)/shard_map/all_to_all | solution.py:172
  121.1 0.8 reduce
  122.0 1.2 convolution_bitcast_fusion.1
  124.2 12.5 %all_to_all.48 = f32[16,40,128]{2,1,0:T(8,128)S(1)} all-to-all(f32[16,40,128]{2,1,0:T(8,128)S(1)} %pad_maximum_fusion.2), channel_id=1, replica_groups=mesh['lon'=16,'lat'=8] {'lon'}, dimensions={0} | all-to-all | bytes 655360 | tf_op jit(solution)/shard_map/all_to_all | solution.py:167
  137.3 4.0 %inverse.3 = f32[32,32]{1,0:T(8,128)} custom-call(f32[32,32]{1,0:T(8,128)} %reshape.63.g_ref), custom_call_target="tpu_custom_call" | custom-call | tf_op jit(solution)/shard_map/inverse/pallas_call | solution.py:161
  141.5 1.0 fusion.20
  143.5 3.4 %all-to-all-start.4 = ((f32[8,1,2048]{2,1,0:T(1,128)}), f32[8,1,2048]{2,1,0:T(1,128)S(1)}, u32[]{:S(2)}, u32[]{:S(2)}) async-start(f32[8,1,2048]{2,1,0:T(1,128)} %reshape.84), calls=%async_computation.4 | async-start | bytes 131072 | tf_op jit(solution)/shard_map/all_to_all | solution.py:172
  146.9 0.9 fusion.41
  147.7 5.7 %all-to-all-done.4 = f32[8,1,2048]{2,1,0:T(1,128)S(1)} async-done(((f32[8,1,2048]{2,1,0:T(1,128)}), f32[8,1,2048]{2,1,0:T(1,128)S(1)}, u32[]{:S(2)}, u32[]{:S(2)}) %all-to-all-start.4) | async-done | bytes 65568 | tf_op jit(solution)/shard_map/all_to_all | solution.py:172
  153.4 0.8 reduce.1
  155.4 5.0 %all-to-all-start.5 = ((f32[16,16,128]{2,1,0:T(8,128)}), f32[16,16,128]{2,1,0:T(8,128)S(1)}, u32[]{:S(2)}, u32[]{:S(2)}) async-start(f32[16,16,128]{2,1,0:T(8,128)} %broadcast_in_dim.52), calls=%async_computation.5 | async-start | bytes 262144 | tf_op jit(solution)/shard_map/all_to_all | solution.py:172
  160.4 2.3 fusion
  162.7 3.9 %all-to-all-done.5 = f32[16,16,128]{2,1,0:T(8,128)S(1)} async-done(((f32[16,16,128]{2,1,0:T(8,128)}), f32[16,16,128]{2,1,0:T(8,128)S(1)}, u32[]{:S(2)}, u32[]{:S(2)}) %all-to-all-start.5) | async-done | bytes 131104 | tf_op jit(solution)/shard_map/all_to_all | solution.py:172
  166.7 5.0 %fusion.5 = f32[32,128,32]{2,1,0:T(8,128)} fusion(f32[32,64,1]{1,0,2:T(8,128)S(1)} %reshape.76, f32[32,64,128]{2,0,1:T(8,128)S(1)} %fusion), kind=kOutput, calls=%fused_computation.13 | convolution fusion | flops 100663296 | bytes 1581056 | tf_op jit(solution)/shard_map/ajr,bj->arb/dot_general | solution.py:207
  171.7 2.7 %reshape.66 = f32[16,64,128]{2,1,0:T(8,128)} reshape(f32[32,128,32]{2,1,0:T(8,128)} %fusion.5) | data formatting | bytes 1048576 | tf_op jit(solution)/shard_map/reshape | solution.py:208
  174.4 3.8 %all-to-all-start.6 = ((f32[16,64,128]{2,1,0:T(8,128)}), f32[16,64,128]{2,1,0:T(8,128)S(1)}, u32[]{:S(2)}, u32[]{:S(2)}) async-start(f32[16,64,128]{2,1,0:T(8,128)} %reshape.66), calls=%async_computation.6 | async-start | bytes 1048576 | tf_op jit(solution)/shard_map/all_to_all | solution.py:167
  178.5 9.4 %all-to-all-done.6 = f32[16,64,128]{2,1,0:T(8,128)S(1)} async-done(((f32[16,64,128]{2,1,0:T(8,128)}), f32[16,64,128]{2,1,0:T(8,128)S(1)}, u32[]{:S(2)}, u32[]{:S(2)}) %all-to-all-start.6) | async-done | bytes 524320 | tf_op jit(solution)/shard_map/all_to_all | solution.py:167
  187.9 10.4 %all_to_all.49 = f32[8,72,128]{2,1,0:T(8,128)S(1)} all-to-all(f32[8,72,128]{2,1,0:T(8,128)S(1)} %broadcast_in_dim.53), channel_id=1, replica_groups=mesh['lon'=16,'lat'=8] {'lat'}, dimensions={0} | all-to-all | bytes 589824 | tf_op jit(solution)/shard_map/all_to_all | solution.py:172
  198.4 0.8 broadcast_in_dim.54
  199.2 5.9 %all-to-all-start.8 = ((f32[16,64,128]{2,1,0:T(8,128)}), f32[16,64,128]{2,1,0:T(8,128)S(1)}, u32[]{:S(2)}, u32[]{:S(2)}) async-start(f32[16,64,128]{2,1,0:T(8,128)} %broadcast_in_dim.54), calls=%async_computation.8 | async-start | bytes 1048576 | tf_op jit(solution)/shard_map/all_to_all | solution.py:172
  205.8 4.0 %inverse.4 = f32[32,32]{1,0:T(8,128)} custom-call(f32[32,32]{1,0:T(8,128)} %reshape.68.g_ref), custom_call_target="tpu_custom_call" | custom-call | tf_op jit(solution)/shard_map/inverse/pallas_call | solution.py:161
  209.9 0.9 fusion.43
  210.8 4.0 %all-to-all-done.8 = f32[16,64,128]{2,1,0:T(8,128)S(1)} async-done(((f32[16,64,128]{2,1,0:T(8,128)}), f32[16,64,128]{2,1,0:T(8,128)S(1)}, u32[]{:S(2)}, u32[]{:S(2)}) %all-to-all-start.8) | async-done | bytes 524320 | tf_op jit(solution)/shard_map/all_to_all | solution.py:172
  214.8 1.8 dot_general.100
  216.6 3.9 %fusion.16 = f32[32,128,32]{1,2,0:T(8,128)S(1)} fusion(f32[32,128,32]{2,1,0:T(8,128)} %dot_general.100, f32[32,32]{1,0:T(8,128)S(1)} %copy-done.7), kind=kOutput, calls=%fused_computation.34 | convolution fusion | flops 50331648 | bytes 1052672 | tf_op jit(solution)/shard_map/dot_general | solution.py:19
  221.1 1.0 convolution_bitcast_fusion.3
  222.9 4.0 %inverse.5 = f32[32,32]{1,0:T(8,128)} custom-call(f32[32,32]{1,0:T(8,128)} %fusion.44.g_ref), custom_call_target="tpu_custom_call" | custom-call | tf_op jit(solution)/shard_map/inverse/pallas_call | solution.py:161
  226.9 0.8 fusion.45
  228.9 1.0 fusion.18
  230.0 2.3 fusion.2
  232.3 2.6 %copy_subtract_fusion = f32[64,64,128]{2,1,0:T(8,128)} fusion(f32[64,64,128]{2,1,0:T(8,128)S(1)} %copy-done.3, f32[64,64,128]{2,0,1:T(8,128)S(1)} %fusion.2), kind=kLoop, calls=%fused_computation | loop fusion | flops 524288 | bytes 6291456 | tf_op jit(solution)/shard_map/sub | solution.py:224
  (83 shorter events, 9.4 us)
Async XLA Ops:
  0.6 70.9 %copy-start = (f32[128,32]{0,1:T(8,128)S(1)}, f32[128,32]{0,1:T(8,128)}, u32[]{:S(2)}) copy-start(f32[128,32]{0,1:T(8,128)} %param.11) | copy-start | bytes 49156
  0.6 5.5 %copy-start.1 = (f32[64,64,128]{2,1,0:T(8,128)S(1)}, f32[64,64,128]{2,1,0:T(8,128)}, u32[]{:S(2)}) copy-start(f32[64,64,128]{2,1,0:T(8,128)} %t_ref.1) | copy-start | bytes 6291460
  3.0 12.0 %collective-permute-start = (f32[12,64,128]{2,1,0:T(8,128)S(1)}, f32[12,64,128]{2,1,0:T(8,128)S(1)}, u32[]{:S(2)}, u32[]{:S(2)}) collective-permute-start(f32[12,64,128]{2,1,0:T(8,128)S(1)} %pad_maximum_fusion), channel_id=1, source_target_pairs={{0,8},{8,16},{16,24},{24,32},{32,40},{40,48},{48,56},{56,64},{64,7... | collective-permute-start | bytes 1179656 | tf_op jit(solution)/shard_map/ppermute | solution.py:109
  6.1 33.4 %copy-start.2 = (f32[64,64,128]{2,1,0:T(8,128)S(1)}, f32[64,64,128]{2,1,0:T(8,128)}, u32[]{:S(2)}) copy-start(f32[64,64,128]{2,1,0:T(8,128)} %k_ref.1) | copy-start | bytes 6291460
  6.1 11.2 %collective-permute-start.1 = (f32[12,64,128]{2,1,0:T(8,128)S(1)}, f32[12,64,128]{2,1,0:T(8,128)S(1)}, u32[]{:S(2)}, u32[]{:S(2)}) collective-permute-start(f32[12,64,128]{2,1,0:T(8,128)S(1)} %pad_maximum_fusion.1), channel_id=1, source_target_pairs={{8,0},{16,8},{24,16},{32,24},{40,32},{48,40},{56,48},{64,56},{72,6... | collective-permute-start | bytes 1179656 | tf_op jit(solution)/shard_map/ppermute | solution.py:110
  17.4 22.1 %collective-permute-start.2 = (f32[72,8,128]{2,1,0:T(8,128)S(1)}, f32[72,8,128]{2,1,0:T(8,128)S(1)}, u32[]{:S(2)}, u32[]{:S(2)}) collective-permute-start(f32[72,8,128]{2,1,0:T(8,128)S(1)} %maximum_maximum_fusion), channel_id=1, source_target_pairs={{0,1},{1,2},{2,3},{3,4},{4,5},{5,6},{6,7},{8,9},{9,10},{10,11},{11... | collective-permute-start | bytes 884744 | tf_op jit(solution)/shard_map/ppermute | solution.py:122
  23.0 16.5 %collective-permute-start.3 = (f32[72,8,128]{2,1,0:T(8,128)S(1)}, f32[72,8,128]{2,1,0:T(8,128)S(1)}, u32[]{:S(2)}, u32[]{:S(2)}) collective-permute-start(f32[72,8,128]{2,1,0:T(8,128)S(1)} %maximum_maximum_fusion.1), channel_id=1, source_target_pairs={{1,0},{2,1},{3,2},{4,3},{5,4},{6,5},{7,6},{9,8},{10,9},{11,10},{12... | collective-permute-start | bytes 884744 | tf_op jit(solution)/shard_map/ppermute | solution.py:123
  24.3 15.2 %collective-permute-start.4 = (f32[36,8,128]{2,1,0:T(8,128)S(1)}, f32[36,8,128]{2,1,0:T(8,128)S(1)}, u32[]{:S(2)}, u32[]{:S(2)}) collective-permute-start(f32[36,8,128]{2,1,0:T(8,128)S(1)} %fusion.10), channel_id=1, source_target_pairs={{0,1},{1,2},{2,3},{3,4},{4,5},{5,6},{6,7},{8,9},{9,10},{10,11},{11... | collective-permute-start | bytes 442376 | tf_op jit(solution)/shard_map/ppermute | solution.py:124
  29.9 9.6 %collective-permute-start.5 = (f32[36,8,128]{2,1,0:T(8,128)S(1)}, f32[36,8,128]{2,1,0:T(8,128)S(1)}, u32[]{:S(2)}, u32[]{:S(2)}) collective-permute-start(f32[36,8,128]{2,1,0:T(8,128)S(1)} %fusion.9), channel_id=1, source_target_pairs={{1,0},{2,1},{3,2},{4,3},{5,4},{6,5},{7,6},{9,8},{10,9},{11,10},{12... | collective-permute-start | bytes 442376 | tf_op jit(solution)/shard_map/ppermute | solution.py:125
  71.5 7.4 %copy-start.8 = (f32[64,32]{0,1:T(8,128)S(1)}, f32[64,32]{0,1:T(8,128)}, u32[]{:S(2)}) copy-start(f32[64,32]{0,1:T(8,128)} %param.10) | copy-start | bytes 24580
  78.9 18.1 %copy-start.10 = (f32[64,32]{0,1:T(8,128)S(1)}, f32[64,32]{0,1:T(8,128)}, u32[]{:S(2)}) copy-start(f32[64,32]{0,1:T(8,128)} %param.9) | copy-start | bytes 24580
  124.1 36.3 %copy-start.3 = (f32[64,64,128]{2,1,0:T(8,128)S(1)}, f32[64,64,128]{2,1,0:T(8,128)}, u32[]{:S(2)}) copy-start(f32[64,64,128]{2,1,0:T(8,128)} %conduct.1) | copy-start | bytes 6291460
  143.5 9.9 %all-to-all-start.4 = ((f32[8,1,2048]{2,1,0:T(1,128)}), f32[8,1,2048]{2,1,0:T(1,128)S(1)}, u32[]{:S(2)}, u32[]{:S(2)}) async-start(f32[8,1,2048]{2,1,0:T(1,128)} %reshape.84), calls=%async_computation.4 | async-start | bytes 131072 | tf_op jit(solution)/shard_map/all_to_all | solution.py:172
  147.7 82.2 %copy-start.5 = (f32[64,32]{0,1:T(8,128)}, f32[64,32]{0,1:T(8,128)S(1)}, u32[]{:S(2)}) copy-start(f32[64,32]{0,1:T(8,128)S(1)} %fusion.41) | copy-start | bytes 24580
  155.4 11.2 %all-to-all-start.5 = ((f32[16,16,128]{2,1,0:T(8,128)}), f32[16,16,128]{2,1,0:T(8,128)S(1)}, u32[]{:S(2)}, u32[]{:S(2)}) async-start(f32[16,16,128]{2,1,0:T(8,128)} %broadcast_in_dim.52), calls=%async_computation.5 | async-start | bytes 262144 | tf_op jit(solution)/shard_map/all_to_all | solution.py:172
  174.4 13.5 %all-to-all-start.6 = ((f32[16,64,128]{2,1,0:T(8,128)}), f32[16,64,128]{2,1,0:T(8,128)S(1)}, u32[]{:S(2)}, u32[]{:S(2)}) async-start(f32[16,64,128]{2,1,0:T(8,128)} %reshape.66), calls=%async_computation.6 | async-start | bytes 1048576 | tf_op jit(solution)/shard_map/all_to_all | solution.py:167
  199.2 15.6 %all-to-all-start.8 = ((f32[16,64,128]{2,1,0:T(8,128)}), f32[16,64,128]{2,1,0:T(8,128)S(1)}, u32[]{:S(2)}, u32[]{:S(2)}) async-start(f32[16,64,128]{2,1,0:T(8,128)} %broadcast_in_dim.54), calls=%async_computation.8 | async-start | bytes 1048576 | tf_op jit(solution)/shard_map/all_to_all | solution.py:172
  209.9 6.8 %copy-start.7 = (f32[32,32]{1,0:T(8,128)S(1)}, f32[32,32]{1,0:T(8,128)}, u32[]{:S(2)}) copy-start(f32[32,32]{1,0:T(8,128)} %inverse.4) | copy-start | bytes 12292
  210.8 18.1 %copy-start.9 = (f32[64,32]{0,1:T(8,128)}, f32[64,32]{0,1:T(8,128)S(1)}, u32[]{:S(2)}) copy-start(f32[64,32]{0,1:T(8,128)S(1)} %fusion.43) | copy-start | bytes 24580
  227.8 4.5 %copy-start.6 = (f32[128,32]{0,1:T(8,128)}, f32[128,32]{0,1:T(8,128)S(1)}, u32[]{:S(2)}) copy-start(f32[128,32]{0,1:T(8,128)S(1)} %fusion.45) | copy-start | bytes 49156
  228.3 4.0 %copy-start.4 = (f32[32,32,32]{2,1,0:T(8,128)}, f32[32,32,32]{2,1,0:T(8,128)S(1)}, u32[]{:S(2)}) copy-start(f32[32,32,32]{2,1,0:T(8,128)S(1)} %fusion.14) | copy-start | bytes 393220

commit v2 on v1

v2 whole, which is shorter than its diff:
```python
import functools

import jax
import jax.numpy as jnp
from jax import lax
from jax.experimental import pallas as pl
from jax.experimental.pallas import tpu as pltpu
from jax.sharding import PartitionSpec as P

SHELL_LAYERS = 128
R = 32
STEPS = 4
time_step = 0.15
highest = lax.Precision.HIGHEST
W = STEPS


def dot(a, b, ca, cb):
    return lax.dot_general(
        a, b, (((ca,), (cb,)), ((), ())), precision=highest, preferred_element_type=jnp.float32
    )


def halves(x):
    high = x.astype(jnp.bfloat16)
    return high, (x - high.astype(jnp.float32)).astype(jnp.bfloat16)


def dot3(a, b, ca=1, cb=0):
    ah, al = halves(a) if not isinstance(a, tuple) else a
    bh, bl = halves(b) if not isinstance(b, tuple) else b

    def one(x, y):
        return lax.dot_general(
            x, y, (((ca,), (cb,)), ((), ())), preferred_element_type=jnp.float32
        )

    return one(ah, bh) + (one(ah, bl) + one(al, bh))


PAD = 4
TILE = PAD + W
SENT = 3 * W - 1


def pack_lat_kernel(t0, k0, s0, t1, k1, s1, low_ref, high_ref):
    n = t0.shape[0]
    for q in range(W):
        low_ref[q] = t0[:, q, :]
        low_ref[W + q] = k0[:, q, :]
        high_ref[q] = t1[:, TILE - W + q, :]
        high_ref[W + q] = k1[:, TILE - W + q, :]
    for q in range(W - 1):
        low_ref[2 * W + q] = s0[:, q, :]
        high_ref[2 * W + q] = s1[:, TILE - W + 1 + q, :]


def pack_lon_kernel(t0, k0, s0, t1, k1, s1, low_ref, high_ref):
    low_ref[0:W] = t0[...]
    low_ref[W:2 * W] = k0[...]
    low_ref[2 * W:] = s0[0:W - 1]
    high_ref[0:W] = t1[...]
    high_ref[W:2 * W] = k1[...]
    high_ref[2 * W:] = s1[1:W]


def pack(kernel, block, dim, t, k, s, slab, name):
    count = t.shape[dim] // block[dim]

    def spec(place):
        return pl.BlockSpec(block, lambda g: tuple(place if d == dim else 0 for d in range(3)))

    shape = jax.ShapeDtypeStruct((SENT,) + slab, jnp.float32)
    return pl.pallas_call(
        kernel,
        grid=(1,),
        out_shape=(shape, shape),
        in_specs=[spec(0)] * 3 + [spec(count - 1)] * 3,
        out_specs=[pl.BlockSpec(shape.shape, lambda g: (0, 0, 0))] * 2,
        name=name,
    )(t, k, s, t, k, s)


def face(p, q):
    summed = p + q
    return (2.0 * time_step) * p * q / jnp.where(summed > 0.0, summed, 1.0)


def conduct_kernel(n, m, lat, t_ref, k_ref, s_ref, below_ref, above_ref, south_ref, north_ref,
                   csouth_ref, cnorth_ref, v_ref, w_ref, out_ref, parts_ref,
                   ta, tb, k, s, hx, hy, hz, z, sems):
    layers = t_ref.shape[2]
    planes = n + 2 * W
    end = TILE + m
    copies = [
        pltpu.make_async_copy(src, dst.at[W:n + W, TILE:end, :], sems.at[i])
        for i, (src, dst) in enumerate(((t_ref, ta), (k_ref, k), (s_ref, s)))
    ]
    for copy in copies:
        copy.start()
    for q in range(SENT):
        arr, at = ((ta, q), (k, q - W), (s, q - 2 * W))[q // W]
        late = q // W == 2
        low_row = PAD + at + (1 if late else 0)
        arr[W:n + W, low_row, :] = south_ref[q]
        arr[W:n + W, end + at, :] = north_ref[q]
        low_plane = at + (1 if late else 0)
        high_plane = n + W + at
        arr[low_plane, TILE:end, :] = below_ref[q]
        arr[high_plane, TILE:end, :] = above_ref[q]
        arr[low_plane, PAD:TILE, :] = csouth_ref[q, 0:W]
        arr[high_plane, PAD:TILE, :] = csouth_ref[q, W:2 * W]
        arr[low_plane, end:end + W, :] = cnorth_ref[q, 0:W]
        arr[high_plane, end:end + W, :] = cnorth_ref[q, W:2 * W]
    for copy in copies:
        copy.wait()

    rows = slice(PAD, end + W)
    count = m + 2 * W
    inside = lax.broadcasted_iota(jnp.int32, (count, layers), 1) < layers - 1

    def faces(i, kc):
        kn = k[i + 1, rows, :]
        hx[i, rows, :] = face(kc, kn)
        hy[i, rows, :] = face(kc, k[i, PAD + 1:PAD + 1 + count, :])
        hz[i, rows, :] = jnp.where(inside, face(kc, pltpu.roll(kc, layers - 1, 1)), 0.0)
        return kn

    lax.fori_loop(0, planes - 1, faces, k[0, rows, :], unroll=4)

    for step in range(STEPS):
        last = step == STEPS - 1
        src, dst = (ta, tb) if step % 2 == 0 else (tb, ta)
        lo, num = (TILE, m) if last else (PAD, count)

        def body(p, carry):
            tc, before = carry
            tn = src[p + 1, lo:lo + num, :]
            fx = hx[p, lo:lo + num, :] * (tn - tc)
            fn = hy[p, lo:lo + num, :] * (src[p, lo + 1:lo + 1 + num, :] - tc)
            fs = hy[p, lo - 1:lo - 1 + num, :] * (src[p, lo - 1:lo - 1 + num, :] - tc)
            up = hz[p, lo:lo + num, :]
            fu = up * (pltpu.roll(tc, layers - 1, 1) - tc)
            fd = pltpu.roll(up, 1, 1) * (pltpu.roll(tc, 1, 1) - tc)
            new = tc + ((s[p, lo:lo + num, :] * time_step + (fx - before)) + ((fn + fs) + (fu + fd)))
            if last:
                out_ref[p - W] = new
            else:
                dst[p, lo:lo + num, :] = new
            return tn, fx

        tc = src[step + 1, lo:lo + num, :]
        start = hx[step, lo:lo + num, :] * (tc - src[step, lo:lo + num, :])
        lax.fori_loop(step + 1, planes - 1 - step, body, (tc, start), unroll=8)

    share = R // lat
    vh, vl = halves(v_ref[...])
    lhs = jnp.concatenate([vh, vh, vl], axis=1)

    def project(i, c):
        pair = jnp.concatenate([out_ref[2 * i], out_ref[2 * i + 1]], axis=1)
        high, low = halves(pair)
        got = lax.dot_general(
            lhs, jnp.concatenate([high, low, high], axis=0), (((1,), (0,)), ((), ())),
            preferred_element_type=jnp.float32,
        )
        for e in range(2):
            for a in range(share):
                z[a, pl.ds(2 * i + e, lat, stride=n), :] = got[
                    a * lat:(a + 1) * lat, e * layers:(e + 1) * layers
                ]
        return c

    lax.fori_loop(0, n // 2, project, 0, unroll=4)
    lane = lax.broadcasted_iota(jnp.int32, w_ref.shape, 1) // R
    total = None
    for a in range(share):
        part = dot3(z[a], jnp.where(lane == a, w_ref[...], 0.0))
        total = part if total is None else total + part
    parts_ref[...] = total


def conduct(t, k, s, v, w):
    n, m, layers = t.shape
    lon, lat = lax.axis_size("lon"), lax.axis_size("lat")
    north_to = [(i, i + 1) for i in range(lat - 1)]
    south_to = [(j, i) for i, j in north_to]
    up = [(i, (i + 1) % lon) for i in range(lon)]
    down = [(j, i) for i, j in up]
    low, high = pack(pack_lat_kernel, (n, TILE, layers), 1, t, k, s, (n, layers), "pack_lat")
    south = lax.ppermute(high, "lat", north_to)
    north = lax.ppermute(low, "lat", south_to)
    low, high = pack(pack_lon_kernel, (W, m, layers), 0, t, k, s, (m, layers), "pack_lon")
    below = lax.ppermute(high, "lon", up)
    above = lax.ppermute(low, "lon", down)
    csouth = lax.ppermute(jnp.concatenate([below[:, m - W:], above[:, m - W:]], 1), "lat", north_to)
    cnorth = lax.ppermute(jnp.concatenate([below[:, :W], above[:, :W]], 1), "lat", south_to)
    share = R // lat
    vt = v.reshape(m, lat, share).transpose(2, 1, 0).reshape(R, m)
    big = pltpu.VMEM((n + 2 * W, m + 2 * TILE, layers), jnp.float32)
    vmem = pl.BlockSpec(memory_space=pltpu.VMEM)
    return pl.pallas_call(
        functools.partial(conduct_kernel, n, m, lat),
        out_shape=(
            jax.ShapeDtypeStruct(t.shape, jnp.float32),
            jax.ShapeDtypeStruct((lat * n, share * R), jnp.float32),
        ),
        in_specs=[pl.BlockSpec(memory_space=pl.ANY)] * 3 + [vmem] * 8,
        out_specs=[vmem] * 2,
        scratch_shapes=[big] * 7
        + [pltpu.VMEM((share, lat * n, layers), jnp.float32), pltpu.SemaphoreType.DMA((3,))],
        compiler_params=pltpu.CompilerParams(vmem_limit_bytes=52 * 2**20),
        name="conduct",
    )(t, k, s, below, above, south, north, csouth, cnorth, vt, jnp.tile(w, (1, share)))


def inverse_factor(gram):
    n = gram.shape[0]
    row = lax.broadcasted_iota(jnp.int32, (n, n), 0)
    col = lax.broadcasted_iota(jnp.int32, (n, n), 1)
    a = gram
    inv = jnp.where(row == col, 1.0, 0.0).astype(jnp.float32)
    scale = jnp.zeros((n, 1), jnp.float32)
    r1 = lax.broadcasted_iota(jnp.int32, (n, 1), 0)
    for j in range(n):
        column = a[:, j:j + 1]
        pivot = a[j:j + 1, j:j + 1]
        factor = jnp.where(r1 > j, column / pivot, 0.0)
        scale = jnp.where(r1 == j, lax.rsqrt(pivot), scale)
        a = a - factor * a[j:j + 1, :]
        inv = inv - factor * inv[j:j + 1, :]
    return inv * scale


def call(kernel, name, outs, args, scratch=(), cost=None, aliases=None):
    vmem = pl.BlockSpec(memory_space=pltpu.VMEM)
    return pl.pallas_call(
        kernel,
        out_shape=tuple(jax.ShapeDtypeStruct(o, jnp.float32) for o in outs),
        in_specs=[vmem] * len(args),
        out_specs=(vmem,) * len(outs),
        scratch_shapes=list(scratch),
        compiler_params=pltpu.CompilerParams(vmem_limit_bytes=40 * 2**20),
        cost_estimate=cost,
        name=name,
    )(*args)


def cost(us):
    return pl.CostEstimate(flops=0, bytes_accessed=int(us * 3e6), transcendentals=0)


def add_up(ref):
    total = ref[0]
    for i in range(1, ref.shape[0]):
        total = total + ref[i]
    return total


def send_all(ref, x):
    for i in range(ref.shape[0]):
        ref[i] = x


def widen(x, n):
    k = x.shape[0] // n
    return jnp.concatenate([x[i * k:(i + 1) * k] for i in range(n)], axis=1)


def narrow(x, n):
    c = x.shape[1] // n
    return jnp.concatenate([x[:, i * c:(i + 1) * c] for i in range(n)], axis=0)


def eye(n):
    row = lax.broadcasted_iota(jnp.int32, (n, n), 0)
    return jnp.where(row == lax.broadcasted_iota(jnp.int32, (n, n), 1), 1.0, 0.0).astype(jnp.float32)


def flip(x):
    return dot(eye(x.shape[1]), x, 1, 1)


def diagonal(x, n):
    k = x.shape[0]
    wide = jnp.concatenate([x] * n, axis=1)
    wide = jnp.concatenate([wide] * n, axis=0)
    row = lax.broadcasted_iota(jnp.int32, wide.shape, 0) // k
    col = lax.broadcasted_iota(jnp.int32, wide.shape, 1) // k
    return jnp.where(row == col, wide, 0.0)


def stack_left(x):
    high, low = halves(x)
    return jnp.concatenate([high, high, low], axis=1)


def stack_right(x):
    high, low = halves(x)
    return jnp.concatenate([high, low, high], axis=0)


def product(left, right):
    return lax.dot_general(
        left, right, (((1,), (0,)), ((), ())), preferred_element_type=jnp.float32
    )


def lon_project_kernel(got, ut, y1, out):
    y = add_up(got)
    y1[...] = y
    send_all(out, dot(ut[...], y, 1, 0))


def lon_block_kernel(got, y1, out):
    send_all(out, widen(dot(add_up(got), y1[...], 1, 1), 2))


def radial_kernel(m, t, wt, out):
    n = t.shape[0] // m
    half = m // 2
    share = out.shape[0]
    peers = R // share
    w = halves(wt[...])

    def body(j, c):
        x = jnp.concatenate(
            [t[pl.ds(j + h * half, n, stride=m), :] for h in range(2)], axis=0
        )
        got = dot3(w, x, 1, 1)
        for b in range(share):
            out[b, pl.ds(j, peers, stride=half), :] = got[b * peers:(b + 1) * peers]
        return c

    lax.fori_loop(0, half, body, 0, unroll=4)


def lat_modes_kernel(got, rt, out, b1):
    block = narrow(add_up(got), 2)
    b1[...] = block
    gram = widen(dot(block, block, 1, 1), 4)
    wide = jnp.concatenate([block, block], axis=1)
    wide = jnp.concatenate([wide] * 4, axis=0)
    row = lax.broadcasted_iota(jnp.int32, wide.shape, 0) // R
    half = lax.broadcasted_iota(jnp.int32, wide.shape, 1) // block.shape[1]
    total = None
    for b in range(rt.shape[0]):
        part = dot3(rt[b], jnp.where(row == 2 * b + half, wide, 0.0), 1, 1)
        total = part if total is None else total + part
    rows = total.shape[0] // out.shape[0]
    for i in range(out.shape[0]):
        out[i, 0:rows] = total[i * rows:(i + 1) * rows]
        out[i, rows:] = gram


def lat_project_kernel(got, b1, vt, out, y2, lon, lont):
    total = add_up(got)
    gram = narrow(total[total.shape[0] - R // 4:], 4)
    inv = inverse_factor(gram)
    block = b1[...]
    lont[...] = dot(inv, block, 1, 0)
    lon[...] = dot(flip(block), inv, 1, 1)
    y = dot(total[:total.shape[0] - R // 4], diagonal(inv, 4), 1, 1)
    y2[...] = y
    half = vt.shape[1] // 2
    lane = lax.broadcasted_iota(jnp.int32, (R, y.shape[1]), 1) // R % 2
    send_all(
        out,
        jnp.where(
            lane == 0, dot(vt[:, 0:half], y, 1, 0), dot(vt[:, half:], y, 1, 0)
        ),
    )


def lon_sums_kernel(m, t, lont, out):
    n = t.shape[0] // m
    layers = t.shape[1]
    left = stack_left(lont[...])

    def body(j, c):
        x = jnp.concatenate([t[pl.ds(2 * j + e, n, stride=m), :] for e in range(2)], axis=1)
        got = product(left, stack_right(x))
        for e in range(2):
            out[pl.ds(2 * j + e, R, stride=m), :] = got[:, e * layers:(e + 1) * layers]
        return c

    lax.fori_loop(0, m // 2, body, 0, unroll=4)


def lat_block_kernel(got, y2, out):
    q = add_up(got)
    y = y2[...]
    lane = lax.broadcasted_iota(jnp.int32, q.shape, 1) // R % 2
    width = q.shape[1]
    both = q + jnp.where(lane == 0, pltpu.roll(q, width - R, 1), pltpu.roll(q, R, 1))
    side = lax.broadcasted_iota(jnp.int32, y.shape, 1) // R % 2
    rows = jnp.concatenate([jnp.where(side == 0, y, 0.0), jnp.where(side == 1, y, 0.0)], axis=0)
    send_all(out, widen(dot(both, rows, 1, 1), 2))


def radial_modes_kernel(got, lp, out, b2, g2):
    block = narrow(add_up(got), 2)
    b2[...] = block
    g2[...] = widen(dot(block, block, 1, 1), 4)
    left = stack_left(block)
    m = block.shape[1]
    layers = lp.shape[1]

    def body(a, c):
        x = jnp.concatenate(
            [lp[pl.ds(pl.multiple_of((2 * a + e) * m, m), m), :] for e in range(2)], axis=1
        )
        y = product(left, stack_right(x))
        for e in range(2):
            out[a, e * R:(e + 1) * R, :] = y[:, e * layers:(e + 1) * layers]
        return c

    lax.fori_loop(0, R // 2, body, 0, unroll=4)


def radial_sum_kernel(got, g2, out):
    total = add_up(got)
    for i in range(out.shape[0]):
        out[i, 0:total.shape[0]] = total
        out[i, total.shape[0]:] = g2[...]


def radial_spread_kernel(got, out, g2):
    total = add_up(got)
    rows = out.shape[1]
    send_all(out, total[:rows])
    g2[...] = total[rows:]


def lat_factor_kernel(g2, b2, inv, lat):
    inverse = inverse_factor(narrow(g2[...], 4))
    inv[...] = inverse
    lat[...] = dot(flip(b2[...]), inverse, 1, 1)


def last_kernel(m, y3_ref, inv2, lat, lon, wt, t, err, rad, core_ref, y3, first, second):
    layers = y3.shape[1]
    n = t.shape[0] // m
    mix = halves(diagonal(inv2[...], layers // R))
    for i in range(y3.shape[0] // layers):
        y3[i * layers:(i + 1) * layers] = dot3(mix, y3_ref[i * layers:(i + 1) * layers])
    y = halves(y3[...])
    proj = dot3(wt[...], y, 1, 1)
    block = dot3(proj, y)
    inv = inverse_factor(dot(block, block, 1, 1))
    radt = dot(inv, block, 1, 0)
    rad[...] = flip(radt)
    radh = halves(radt)
    core = dot3(y, radh, 1, 1)
    core_ref[...] = core
    first[...] = dot3(core, radh)
    left = stack_left(lat[...])

    def widen_lat(a, c):
        x = jnp.concatenate(
            [first[pl.ds(pl.multiple_of((2 * a + e) * R, R), R), :] for e in range(2)], axis=1
        )
        got = product(left, stack_right(x))
        for e in range(2):
            at = pl.multiple_of((2 * a + e) * m, m)
            second[pl.ds(at, m), :] = got[:, e * layers:(e + 1) * layers]
        return c

    lax.fori_loop(0, R // 2, widen_lat, 0, unroll=4)
    lonl = stack_left(lon[...])

    def widen_lon(j, c):
        x = jnp.concatenate(
            [second[pl.ds(2 * j + e, R, stride=m), :] for e in range(2)], axis=1
        )
        got = product(lonl, stack_right(x))
        for e in range(2):
            at = pl.ds(2 * j + e, n, stride=m)
            err[at, :] = t[at, :] - got[:, e * layers:(e + 1) * layers]
        return c

    lax.fori_loop(0, m // 2, widen_lon, 0, unroll=4)


def exchange(parts, axis):
    return lax.all_to_all(parts, axis, 0, 0, tiled=True)


def local(t0, k, s, u, v, w):
    n, m, layers = t0.shape
    lon, lat = lax.axis_size("lon"), lax.axis_size("lat")
    t, parts = conduct(t0, k, s, v, w)
    flat = t.reshape(n * m, layers)
    share = R // lon
    wt = w.T
    vt = v.T
    wide = R // lat * R
    got = exchange(parts.reshape(lat, n, wide), "lat")
    (rt,) = call(
        functools.partial(radial_kernel, m), "radial",
        [(share, lon * m // 2, 2 * n)],
        [flat, wt.reshape(lon, share, layers).transpose(1, 0, 2).reshape(R, layers)],
        cost=cost(4),
    )
    y1, parts = call(
        lon_project_kernel, "lon_project", [(n, wide), (lon, R, wide)], [got, u.T]
    )
    (parts,) = call(
        lon_block_kernel, "lon_block", [(lat, R // 2, 2 * n)], [exchange(parts, "lon"), y1]
    )
    parts, b1 = call(
        lat_modes_kernel, "lat_modes", [(lon, m // 2 + R // 4, 2 * share * R), (R, n)],
        [exchange(parts, "lat"), rt],
    )
    parts, y2, new_lon, lont = call(
        lat_project_kernel, "lat_project",
        [(lat, R, 2 * share * R), (m // 2, 2 * share * R), (n, R), (R, n)],
        [exchange(parts, "lon"), b1, vt],
    )
    got = exchange(parts, "lat")
    (lp,) = call(
        functools.partial(lon_sums_kernel, m), "lon_sums", [(R * m, layers)], [flat, lont],
        cost=cost(4),
    )
    (parts,) = call(lat_block_kernel, "lat_block", [(lon, R // 2, 2 * m)], [got, y2])
    parts, b2, g2 = call(
        radial_modes_kernel, "radial_modes",
        [(lon, share * R, layers), (R, m), (R // 4, 4 * R)],
        [exchange(parts, "lon"), lp],
    )
    (parts,) = call(
        radial_sum_kernel, "radial_sum", [(lat, share * R + R // 4, layers)],
        [exchange(parts, "lon"), g2],
    )
    parts, g2 = call(
        radial_spread_kernel, "radial_spread", [(lon, share * R, layers), (R // 4, 4 * R)],
        [exchange(parts, "lat")],
    )
    got = exchange(parts, "lon")
    inv2, new_lat = call(
        lat_factor_kernel, "lat_factor", [(R, R), (m, R)], [g2, b2], cost=cost(4)
    )
    err, new_rad, core = call(
        functools.partial(last_kernel, m), "last",
        [(n * m, layers), (layers, R), (R * R, R)],
        [got.reshape(R * R, layers), inv2, new_lat, new_lon, wt, flat],
        scratch=[
            pltpu.VMEM((R * R, layers), jnp.float32),
            pltpu.VMEM((R * R, layers), jnp.float32),
            pltpu.VMEM((R * m, layers), jnp.float32),
        ],
    )
    return (t, err.reshape(n, m, layers), new_lon, new_lat, new_rad, core.reshape(R, R, R))


def solution(mesh):
    grid = P("lon", "lat", None)
    return jax.shard_map(
        local,
        mesh=mesh,
        in_specs=(grid, grid, grid, P("lon", None), P("lat", None), P()),
        out_specs=(grid, grid, P("lon", None), P("lat", None), P(), P()),
        check_vma=False,
    )
```

time: 236 us -> 186 us (0.79)
  matrix products: 34.3 us -> 0 us
  waiting for transfers between devices: 40.1 us -> 18.5 us
  blocking collectives: 60.3 us -> 81 us
  local copies, waits for them, and re-layouts: 15.4 us -> 3.77 us
  Pallas kernels: 44.1 us -> 51.3 us
  starting transfers between devices: 34.8 us -> 29.6 us
  other arithmetic: 4.69 us -> 0.03 us
    dot_general x23 -> x0, matrix products: 34.3 us -> none  [the longest x12 18.6 us: dot(): lax.dot_general(a, b, (((ca,), (cb,)), ((), ())), precision=highest, pref...]
    all_to_all x5 -> x6, blocking collectives: 60.3 us -> 81 us  [exchange(): return lax.all_to_all(parts, axis, 0, 0, tiled=True)]
    all_to_all x4 -> x3, waiting for transfers between devices: 23 us -> 10.8 us  [exchange(): return lax.all_to_all(parts, axis, 0, 0, tiled=True)]
    ppermute x6, waiting for transfers between devices: 17.1 us -> 7.64 us  [the longest x1 3.32 us: conduct(): south = lax.ppermute(high, 'lat', north_to)]
    pallas_call x4 -> x15, Pallas kernels: 44.1 us -> 51.3 us  [the longest x12 26.8 us: call(): pl.pallas_call(kernel, out_shape=tuple((jax.ShapeDtypeStruct(o, jnp.float...]
    slice x10 -> x2, local copies, waits for them, and re-layouts: 4.64 us -> 0.02 us  [the longest x1 0.01 us: conduct(): below[:, :W]]
    reshape x8 -> x1, local copies, waits for them, and re-layouts: 4.6 us -> 0.01 us  [conduct(): vt = v.reshape(m, lat, share).transpose(2, 1, 0).reshape(R, m)]
    all_to_all x4 -> x3, starting transfers between devices: 18.1 us -> 14.6 us  [exchange(): return lax.all_to_all(parts, axis, 0, 0, tiled=True)]
  transfers between devices with their start and end apart: 10 -> 9, of which waited for: 7 -> 7; matrix products, arithmetic and copies ran while one was open for 3% -> 1% of each run, Pallas kernels for 2% -> 6%
where the time goes in v2:
time: 186 us; the launch traced here: 185 us
  blocking collectives  81 us (44%)
  Pallas kernels  51.3 us (28%)
  starting transfers between devices  29.6 us (16%)
  waiting for transfers between devices  18.5 us (10%)
  local copies, waits for them, and re-layouts  3.77 us (2%)
    all_to_all x6, blocking collectives, exchange(): return lax.all_to_all(parts, axis, 0, 0, tiled=True)  81 us
    pallas_call x12, Pallas kernels, call(): pl.pallas_call(kernel, out_shape=tuple((jax.ShapeDtypeStruct(o, jnp.float...  26.8 us
    pallas_call x1, Pallas kernels, conduct(): pl.pallas_call(functools.partial(conduct_kernel, n, m, lat), out_shape=(j...  19.9 us
    all_to_all x3, starting transfers between devices, exchange(): return lax.all_to_all(parts, axis, 0, 0, tiled=True)  14.6 us
    all_to_all x3, waiting for transfers between devices, exchange(): return lax.all_to_all(parts, axis, 0, 0, tiled=True)  10.8 us
    ppermute x1, starting transfers between devices, conduct(): south = lax.ppermute(high, 'lat', north_to)  5.22 us
    pallas_call x2, Pallas kernels, pack(): pl.pallas_call(kernel, grid=(1,), out_shape=(shape, shape), in_specs=[spe...  4.72 us
    ppermute x1, starting transfers between devices, conduct(): lax.ppermute(jnp.concatenate([below[:, m - W:], above[:, m - W:]], 1), 'l...  4.16 us
  transfers between devices with their start and end apart: 9, of which 7 were waited for; matrix products, arithmetic and copies ran while one was open for 1% of the time, Pallas kernels for 6%

profile of v2, /device:TPU:1, one launch (start us, length us, event | category | flops | bytes accessed | tf_op | source)
XLA Modules:
  0.0 185.1 jit_solution(15852191096104217191)
XLA Ops:
  0.6 2.1 %pack_lon.1 = (f32[11,64,128]{2,1,0:T(8,128)}, f32[11,64,128]{2,1,0:T(8,128)}) custom-call(f32[64,64,128]{2,1,0:T(8,128)} %t_ref.1, f32[64,64,128]{2,1,0:T(8,128)} %k_ref.1, f32[64,64,128]{2,1,0:T(8,128)} %s_ref.1, f32[64,64,128]{2,1,0:T(8,128)} %t_ref.1, f32[64,64,128]{2,1,0:T(8,128)} %k_ref.1, f32[64,64,128]{2,1,0:T(8,128)} %s_ref.1), custom_call_target="tpu_custom_call" | custom-call | tf_op jit(solution)/shard_map/pack_lon/pallas_call | solution.py:74
  2.7 3.0 %collective-permute-start = (f32[11,64,128]{2,1,0:T(8,128)}, f32[11,64,128]{2,1,0:T(8,128)S(1)}, u32[]{:S(2)}, u32[]{:S(2)}) collective-permute-start(f32[11,64,128]{2,1,0:T(8,128)} %get-tuple-element.30), channel_id=1, source_target_pairs={{0,8},{8,16},{16,24},{24,32},{32,40},{40,48},{48,56},{56,64},{64,7... | collective-permute-start | bytes 1081352 | tf_op jit(solution)/shard_map/ppermute | solution.py:194
  5.8 0.0 collective-permute-start.1
  5.8 2.6 %pack_lat.1 = (f32[11,64,128]{2,1,0:T(8,128)}, f32[11,64,128]{2,1,0:T(8,128)}) custom-call(f32[64,64,128]{2,1,0:T(8,128)} %t_ref.1, f32[64,64,128]{2,1,0:T(8,128)} %k_ref.1, f32[64,64,128]{2,1,0:T(8,128)} %s_ref.1, f32[64,64,128]{2,1,0:T(8,128)} %t_ref.1, f32[64,64,128]{2,1,0:T(8,128)} %k_ref.1, f32[64,64,128]{2,1,0:T(8,128)} %s_ref.1), custom_call_target="tpu_custom_call" | custom-call | tf_op jit(solution)/shard_map/pack_lat/pallas_call | solution.py:74
  8.4 5.2 %collective-permute-start.2 = (f32[11,64,128]{2,1,0:T(8,128)}, f32[11,64,128]{2,1,0:T(8,128)S(1)}, u32[]{:S(2)}, u32[]{:S(2)}) collective-permute-start(f32[11,64,128]{2,1,0:T(8,128)} %get-tuple-element.32), channel_id=1, source_target_pairs={{0,1},{1,2},{2,3},{3,4},{4,5},{5,6},{6,7},{8,9},{9,10},{10,11},{11... | collective-permute-start | bytes 1081352 | tf_op jit(solution)/shard_map/ppermute | solution.py:191
  13.6 1.3 collective-permute-start.3
  14.9 0.0 collective-permute-done.below_ref
  14.9 2.8 %collective-permute-done.1.above_ref = f32[11,64,128]{2,1,0:T(8,128)S(1)} collective-permute-done((f32[11,64,128]{2,1,0:T(8,128)}, f32[11,64,128]{2,1,0:T(8,128)S(1)}, u32[]{:S(2)}, u32[]{:S(2)}) %collective-permute-start.1) | collective-permute-done | bytes 360480 | tf_op jit(solution)/shard_map/ppermute | solution.py:195
  17.8 4.2 %collective-permute-start.4 = (f32[11,8,128]{2,1,0:T(8,128)S(1)}, f32[11,8,128]{2,1,0:T(8,128)S(1)}, u32[]{:S(2)}, u32[]{:S(2)}) collective-permute-start(f32[11,8,128]{2,1,0:T(8,128)S(1)} %pad_maximum_fusion), channel_id=1, source_target_pairs={{0,1},{1,2},{2,3},{3,4},{4,5},{5,6},{6,7},{8,9},{9,10},{10,11},{11... | collective-permute-start | bytes 135176 | tf_op jit(solution)/shard_map/ppermute | solution.py:196
  22.0 1.3 collective-permute-start.5
  23.3 0.0 copy-done.2
  23.3 0.1 copy.19.w_ref
  23.4 0.0 copy-done.3
  23.4 3.3 %collective-permute-done.2.south_ref = f32[11,64,128]{2,1,0:T(8,128)S(1)} collective-permute-done((f32[11,64,128]{2,1,0:T(8,128)}, f32[11,64,128]{2,1,0:T(8,128)S(1)}, u32[]{:S(2)}, u32[]{:S(2)}) %collective-permute-start.2) | collective-permute-done | bytes 360480 | tf_op jit(solution)/shard_map/ppermute | solution.py:191
  26.7 0.0 collective-permute-done.3.north_ref
  26.7 0.9 collective-permute-done.4.csouth_ref
  27.6 0.7 collective-permute-done.5.cnorth_ref
  28.3 19.9 %conduct.1 = (f32[64,64,128]{2,1,0:T(8,128)}, f32[512,128]{1,0:T(8,128)S(1)}) custom-call(f32[64,64,128]{2,1,0:T(8,128)} %t_ref.1, f32[64,64,128]{2,1,0:T(8,128)} %k_ref.1, f32[64,64,128]{2,1,0:T(8,128)} %s_ref.1, f32[11,64,128]{2,1,0:T(8,128)S(1)} %collective-permute-done.below_ref, f32[11,64,128]{2,1,0:T(8,128)S(1)} %collective-permute-done.1.above_ref, ...), custom_call_target="tpu_custom_call" | custom-call | tf_op jit(solution)/shard_map/conduct/pallas_call | solution.py:202
  48.1 23.4 %all_to_all.45.got = f32[8,64,128]{2,1,0:T(8,128)S(1)} all-to-all(f32[8,64,128]{2,1,0:T(8,128)S(1)} %bitcast.24), channel_id=1, replica_groups=mesh['lon'=16,'lat'=8] {'lat'}, dimensions={0} | all-to-all | bytes 524288 | tf_op jit(solution)/shard_map/all_to_all | solution.py:486
  71.5 0.0 copy-done.4
  71.5 0.2 lon_project.1
  71.7 11.5 %all_to_all.46.got = f32[16,32,128]{2,1,0:T(8,128)S(1)} all-to-all(f32[16,32,128]{2,1,0:T(8,128)S(1)} %get-tuple-element.36), channel_id=1, replica_groups=mesh['lon'=16,'lat'=8] {'lon'}, dimensions={0} | all-to-all | bytes 524288 | tf_op jit(solution)/shard_map/all_to_all | solution.py:486
  83.2 0.9 lon_block.1
  84.1 3.4 %all-to-all-start.2 = ((f32[8,16,128]{2,1,0:T(8,128)}), f32[8,16,128]{2,1,0:T(8,128)S(1)}, u32[]{:S(2)}, u32[]{:S(2)}) async-start(f32[8,16,128]{2,1,0:T(8,128)} %lon_block.1), calls=%async_computation.2 | async-start | bytes 131072 | tf_op jit(solution)/shard_map/all_to_all | solution.py:486
  87.5 0.0 copy-start
  87.5 1.6 copy-done
  89.1 3.1 %radial.1.rt = f32[2,512,128]{2,1,0:T(8,128)S(1)} custom-call(f32[4096,128]{1,0:T(8,128)S(1)} %bitcast.20, f32[32,128]{1,0:T(8,128)S(1)} %bitcast.28), custom_call_target="tpu_custom_call" | custom-call | bytes 12000000 | tf_op jit(solution)/shard_map/radial/pallas_call | solution.py:237
  92.2 1.9 %all-to-all-done.2.got = f32[8,16,128]{2,1,0:T(8,128)S(1)} async-done(((f32[8,16,128]{2,1,0:T(8,128)}), f32[8,16,128]{2,1,0:T(8,128)S(1)}, u32[]{:S(2)}, u32[]{:S(2)}) %all-to-all-start.2) | async-done | bytes 65568 | tf_op jit(solution)/shard_map/all_to_all | solution.py:486
  94.1 0.6 lat_modes.1
  94.6 12.3 %all_to_all.47.got = f32[16,40,128]{2,1,0:T(8,128)S(1)} all-to-all(f32[16,40,128]{2,1,0:T(8,128)S(1)} %get-tuple-element.38), channel_id=1, replica_groups=mesh['lon'=16,'lat'=8] {'lon'}, dimensions={0} | all-to-all | bytes 655360 | tf_op jit(solution)/shard_map/all_to_all | solution.py:486
  107.0 3.4 %lat_project.1 = (f32[8,32,128]{2,1,0:T(8,128)S(1)}, f32[32,128]{1,0:T(8,128)S(1)}, f32[64,32]{1,0:T(8,128)S(1)}, f32[32,64]{1,0:T(8,128)S(1)}) custom-call(f32[16,40,128]{2,1,0:T(8,128)S(1)} %all_to_all.47.got, f32[32,64]{1,0:T(8,128)S(1)} %get-tuple-element.39.b1, f32[32,64]{1,0:T(8,128)S(1)} %bitcast.30), custom_call_target="tpu_custom_call" | custom-call | tf_op jit(solution)/shard_map/lat_project/pallas_call | solution.py:237
  110.4 10.8 %all_to_all.48.got = f32[8,32,128]{2,1,0:T(8,128)S(1)} all-to-all(f32[8,32,128]{2,1,0:T(8,128)S(1)} %get-tuple-element.40), channel_id=1, replica_groups=mesh['lon'=16,'lat'=8] {'lat'}, dimensions={0} | all-to-all | bytes 262144 | tf_op jit(solution)/shard_map/all_to_all | solution.py:486
  121.1 1.0 lat_block.1
  122.1 5.1 %all-to-all-start.5 = ((f32[16,16,128]{2,1,0:T(8,128)}), f32[16,16,128]{2,1,0:T(8,128)S(1)}, u32[]{:S(2)}, u32[]{:S(2)}) async-start(f32[16,16,128]{2,1,0:T(8,128)} %lat_block.1), calls=%async_computation.5 | async-start | bytes 262144 | tf_op jit(solution)/shard_map/all_to_all | solution.py:486
  127.2 0.0 copy-done.1
  127.2 2.6 %lon_sums.1.lp = f32[2048,128]{1,0:T(8,128)S(1)} custom-call(f32[4096,128]{1,0:T(8,128)S(1)} %bitcast.21, f32[32,64]{1,0:T(8,128)S(1)} %get-tuple-element.42.lont), custom_call_target="tpu_custom_call" | custom-call | bytes 12000000 | tf_op jit(solution)/shard_map/lon_sums/pallas_call | solution.py:237
  129.9 3.6 %all-to-all-done.5.got = f32[16,16,128]{2,1,0:T(8,128)S(1)} async-done(((f32[16,16,128]{2,1,0:T(8,128)}), f32[16,16,128]{2,1,0:T(8,128)S(1)}, u32[]{:S(2)}, u32[]{:S(2)}) %all-to-all-start.5) | async-done | bytes 131104 | tf_op jit(solution)/shard_map/all_to_all | solution.py:486
  133.4 1.0 radial_modes.1
  134.5 12.6 %all_to_all.49.got = f32[16,64,128]{2,1,0:T(8,128)S(1)} all-to-all(f32[16,64,128]{2,1,0:T(8,128)S(1)} %get-tuple-element.43), channel_id=1, replica_groups=mesh['lon'=16,'lat'=8] {'lon'}, dimensions={0} | all-to-all | bytes 1048576 | tf_op jit(solution)/shard_map/all_to_all | solution.py:486
  147.1 10.4 %all_to_all.50.got = f32[8,72,128]{2,1,0:T(8,128)S(1)} all-to-all(f32[8,72,128]{2,1,0:T(8,128)S(1)} %radial_sum.1), channel_id=1, replica_groups=mesh['lon'=16,'lat'=8] {'lat'}, dimensions={0} | all-to-all | bytes 589824 | tf_op jit(solution)/shard_map/all_to_all | solution.py:486
  157.5 0.9 radial_spread.1
  158.4 6.1 %all-to-all-start.8 = ((f32[16,64,128]{2,1,0:T(8,128)}), f32[16,64,128]{2,1,0:T(8,128)S(1)}, u32[]{:S(2)}, u32[]{:S(2)}) async-start(f32[16,64,128]{2,1,0:T(8,128)} %get-tuple-element.45), calls=%async_computation.8 | async-start | bytes 1048576 | tf_op jit(solution)/shard_map/all_to_all | solution.py:486
  164.5 0.7 copy.21
  165.2 2.9 %lat_factor.1 = (f32[32,32]{1,0:T(8,128)S(1)}, f32[64,32]{1,0:T(8,128)S(1)}) custom-call(f32[8,128]{1,0:T(8,128)S(1)} %get-tuple-element.46.g2, f32[32,64]{1,0:T(8,128)S(1)} %get-tuple-element.47.b2), custom_call_target="tpu_custom_call" | custom-call | bytes 12000000 | tf_op jit(solution)/shard_map/lat_factor/pallas_call | solution.py:237
  168.1 0.7 copy.22
  168.8 5.4 %all-to-all-done.8 = f32[16,64,128]{2,1,0:T(8,128)S(1)} async-done(((f32[16,64,128]{2,1,0:T(8,128)}), f32[16,64,128]{2,1,0:T(8,128)S(1)}, u32[]{:S(2)}, u32[]{:S(2)}) %all-to-all-start.8) | async-done | bytes 524320 | tf_op jit(solution)/shard_map/all_to_all | solution.py:486
  174.2 10.2 %last.1 = (f32[4096,128]{1,0:T(8,128)}, f32[128,32]{1,0:T(8,128)S(1)}, f32[1024,32]{1,0:T(8,128)}) custom-call(f32[1024,128]{1,0:T(8,128)S(1)} %bitcast.23, f32[32,32]{1,0:T(8,128)S(1)} %get-tuple-element.48.inv2, f32[64,32]{1,0:T(8,128)S(1)} %get-tuple-element.63.lat, f32[64,32]{1,0:T(8,128)S(1)} %get-tuple-element.62.lon, f32[32,128]{1,0:T(8,128)S(1)} %bitcast.26, ...), custom_call_target="tpu_custom_call" | custom-call | tf_op jit(solution)/shard_map/last/pallas_call | solution.py:237
  184.4 0.7 copy.23
  (12 shorter events, 0.1 us)
Async XLA Ops:
  2.7 12.2 %collective-permute-start = (f32[11,64,128]{2,1,0:T(8,128)}, f32[11,64,128]{2,1,0:T(8,128)S(1)}, u32[]{:S(2)}, u32[]{:S(2)}) collective-permute-start(f32[11,64,128]{2,1,0:T(8,128)} %get-tuple-element.30), channel_id=1, source_target_pairs={{0,8},{8,16},{16,24},{24,32},{32,40},{40,48},{48,56},{56,64},{64,7... | collective-permute-start | bytes 1081352 | tf_op jit(solution)/shard_map/ppermute | solution.py:194
  5.8 17.5 %copy-start.2 = (f32[128,32]{0,1:T(8,128)S(1)}, f32[128,32]{0,1:T(8,128)}, u32[]{:S(2)}) copy-start(f32[128,32]{0,1:T(8,128)} %param.11) | copy-start | bytes 49156
  5.8 17.6 %copy-start.3 = (f32[64,32]{0,1:T(8,128)S(1)}, f32[64,32]{0,1:T(8,128)}, u32[]{:S(2)}) copy-start(f32[64,32]{0,1:T(8,128)} %param.10) | copy-start | bytes 24580
  5.8 12.0 %collective-permute-start.1 = (f32[11,64,128]{2,1,0:T(8,128)}, f32[11,64,128]{2,1,0:T(8,128)S(1)}, u32[]{:S(2)}, u32[]{:S(2)}) collective-permute-start(f32[11,64,128]{2,1,0:T(8,128)} %get-tuple-element.31), channel_id=1, source_target_pairs={{8,0},{16,8},{24,16},{32,24},{40,32},{48,40},{56,48},{64,56},{72,6... | collective-permute-start | bytes 1081352 | tf_op jit(solution)/shard_map/ppermute | solution.py:195
  8.4 18.3 %collective-permute-start.2 = (f32[11,64,128]{2,1,0:T(8,128)}, f32[11,64,128]{2,1,0:T(8,128)S(1)}, u32[]{:S(2)}, u32[]{:S(2)}) collective-permute-start(f32[11,64,128]{2,1,0:T(8,128)} %get-tuple-element.32), channel_id=1, source_target_pairs={{0,1},{1,2},{2,3},{3,4},{4,5},{5,6},{6,7},{8,9},{9,10},{10,11},{11... | collective-permute-start | bytes 1081352 | tf_op jit(solution)/shard_map/ppermute | solution.py:191
  13.6 13.1 %collective-permute-start.3 = (f32[11,64,128]{2,1,0:T(8,128)}, f32[11,64,128]{2,1,0:T(8,128)S(1)}, u32[]{:S(2)}, u32[]{:S(2)}) collective-permute-start(f32[11,64,128]{2,1,0:T(8,128)} %get-tuple-element.33), channel_id=1, source_target_pairs={{1,0},{2,1},{3,2},{4,3},{5,4},{6,5},{7,6},{9,8},{10,9},{11,10},{12... | collective-permute-start | bytes 1081352 | tf_op jit(solution)/shard_map/ppermute | solution.py:192
  17.8 9.8 %collective-permute-start.4 = (f32[11,8,128]{2,1,0:T(8,128)S(1)}, f32[11,8,128]{2,1,0:T(8,128)S(1)}, u32[]{:S(2)}, u32[]{:S(2)}) collective-permute-start(f32[11,8,128]{2,1,0:T(8,128)S(1)} %pad_maximum_fusion), channel_id=1, source_target_pairs={{0,1},{1,2},{2,3},{3,4},{4,5},{5,6},{6,7},{8,9},{9,10},{10,11},{11... | collective-permute-start | bytes 135176 | tf_op jit(solution)/shard_map/ppermute | solution.py:196
  22.0 6.3 %collective-permute-start.5 = (f32[11,8,128]{2,1,0:T(8,128)S(1)}, f32[11,8,128]{2,1,0:T(8,128)S(1)}, u32[]{:S(2)}, u32[]{:S(2)}) collective-permute-start(f32[11,8,128]{2,1,0:T(8,128)S(1)} %pad_maximum_fusion.1), channel_id=1, source_target_pairs={{1,0},{2,1},{3,2},{4,3},{5,4},{6,5},{7,6},{9,8},{10,9},{11,10},{12... | collective-permute-start | bytes 135176 | tf_op jit(solution)/shard_map/ppermute | solution.py:197
  28.2 43.2 %copy-start.4 = (f32[64,32]{0,1:T(8,128)S(1)}, f32[64,32]{0,1:T(8,128)}, u32[]{:S(2)}) copy-start(f32[64,32]{0,1:T(8,128)} %param.9) | copy-start | bytes 24580
  84.1 10.0 %all-to-all-start.2 = ((f32[8,16,128]{2,1,0:T(8,128)}), f32[8,16,128]{2,1,0:T(8,128)S(1)}, u32[]{:S(2)}, u32[]{:S(2)}) async-start(f32[8,16,128]{2,1,0:T(8,128)} %lon_block.1), calls=%async_computation.2 | async-start | bytes 131072 | tf_op jit(solution)/shard_map/all_to_all | solution.py:486
  87.5 1.6 copy-start
  89.1 38.2 %copy-start.1 = (f32[64,64,128]{2,1,0:T(8,128)S(1)}, f32[64,64,128]{2,1,0:T(8,128)}, u32[]{:S(2)}) copy-start(f32[64,64,128]{2,1,0:T(8,128)} %get-tuple-element.60) | copy-start | bytes 6291460
  122.1 11.3 %all-to-all-start.5 = ((f32[16,16,128]{2,1,0:T(8,128)}), f32[16,16,128]{2,1,0:T(8,128)S(1)}, u32[]{:S(2)}, u32[]{:S(2)}) async-start(f32[16,16,128]{2,1,0:T(8,128)} %lat_block.1), calls=%async_computation.5 | async-start | bytes 262144 | tf_op jit(solution)/shard_map/all_to_all | solution.py:486
  158.4 15.8 %all-to-all-start.8 = ((f32[16,64,128]{2,1,0:T(8,128)}), f32[16,64,128]{2,1,0:T(8,128)S(1)}, u32[]{:S(2)}, u32[]{:S(2)}) async-start(f32[16,64,128]{2,1,0:T(8,128)} %get-tuple-element.45), calls=%async_computation.8 | async-start | bytes 1048576 | tf_op jit(solution)/shard_map/all_to_all | solution.py:486

commit v3 on v2

--- a/solution.py
+++ b/solution.py
@@ -88,13 +88,13 @@
 
 def conduct_kernel(n, m, lat, t_ref, k_ref, s_ref, below_ref, above_ref, south_ref, north_ref,
                    csouth_ref, cnorth_ref, v_ref, w_ref, out_ref, parts_ref,
-                   ta, tb, k, s, hx, hy, hz, z, sems):
+                   ta, tb, k, s, hx, hy, hz, hd, full, z, sems):
     layers = t_ref.shape[2]
     planes = n + 2 * W
     end = TILE + m
     copies = [
         pltpu.make_async_copy(src, dst.at[W:n + W, TILE:end, :], sems.at[i])
-        for i, (src, dst) in enumerate(((t_ref, ta), (k_ref, k), (s_ref, s)))
+        for i, (src, dst) in enumerate(((k_ref, k), (t_ref, ta), (s_ref, s)))
     ]
     for copy in copies:
         copy.start()
@@ -112,8 +112,7 @@
         arr[high_plane, PAD:TILE, :] = csouth_ref[q, W:2 * W]
         arr[low_plane, end:end + W, :] = cnorth_ref[q, 0:W]
         arr[high_plane, end:end + W, :] = cnorth_ref[q, W:2 * W]
-    for copy in copies:
-        copy.wait()
+    copies[0].wait()
 
     rows = slice(PAD, end + W)
     count = m + 2 * W
@@ -123,11 +122,15 @@
         kn = k[i + 1, rows, :]
         hx[i, rows, :] = face(kc, kn)
         hy[i, rows, :] = face(kc, k[i, PAD + 1:PAD + 1 + count, :])
-        hz[i, rows, :] = jnp.where(inside, face(kc, pltpu.roll(kc, layers - 1, 1)), 0.0)
+        up = jnp.where(inside, face(kc, pltpu.roll(kc, layers - 1, 1)), 0.0)
+        hz[i, rows, :] = up
+        hd[i, rows, :] = pltpu.roll(up, 1, 1)
         return kn
 
     lax.fori_loop(0, planes - 1, faces, k[0, rows, :], unroll=4)
 
+    copies[1].wait()
+    copies[2].wait()
     for step in range(STEPS):
         last = step == STEPS - 1
         src, dst = (ta, tb) if step % 2 == 0 else (tb, ta)
@@ -139,26 +142,34 @@
             fx = hx[p, lo:lo + num, :] * (tn - tc)
             fn = hy[p, lo:lo + num, :] * (src[p, lo + 1:lo + 1 + num, :] - tc)
             fs = hy[p, lo - 1:lo - 1 + num, :] * (src[p, lo - 1:lo - 1 + num, :] - tc)
-            up = hz[p, lo:lo + num, :]
-            fu = up * (pltpu.roll(tc, layers - 1, 1) - tc)
-            fd = pltpu.roll(up, 1, 1) * (pltpu.roll(tc, 1, 1) - tc)
-            new = tc + ((s[p, lo:lo + num, :] * time_step + (fx - before)) + ((fn + fs) + (fu + fd)))
+            fu = hz[p, lo:lo + num, :] * (pltpu.roll(tc, layers - 1, 1) - tc)
+            fd = hd[p, lo:lo + num, :] * (pltpu.roll(tc, 1, 1) - tc)
+            gain = s[p, lo:lo + num, :]
+            if step == 0:
+                gain = gain * time_step
+                s[p, lo:lo + num, :] = gain
+            new = tc + ((gain + (fx - before)) + ((fn + fs) + (fu + fd)))
             if last:
-                out_ref[p - W] = new
+                full[p - W] = new
             else:
                 dst[p, lo:lo + num, :] = new
             return tn, fx
 
         tc = src[step + 1, lo:lo + num, :]
         start = hx[step, lo:lo + num, :] * (tc - src[step, lo:lo + num, :])
-        lax.fori_loop(step + 1, planes - 1 - step, body, (tc, start), unroll=8)
-
+        lax.fori_loop(step + 1, planes - 1 - step, body, (tc, start), unroll=16)
+
+    written = pltpu.make_async_copy(full, out_ref, sems.at[0])
+    written.start()
     share = R // lat
-    vh, vl = halves(v_ref[...])
+    row = lax.broadcasted_iota(jnp.int32, (R, R), 0)
+    col = lax.broadcasted_iota(jnp.int32, (R, R), 1)
+    order = jnp.where(row % lat * share + row // lat == col, 1.0, 0.0).astype(jnp.float32)
+    vh, vl = halves(dot(order, v_ref[...], 1, 0))
     lhs = jnp.concatenate([vh, vh, vl], axis=1)
 
     def project(i, c):
-        pair = jnp.concatenate([out_ref[2 * i], out_ref[2 * i + 1]], axis=1)
+        pair = jnp.concatenate([full[2 * i], full[2 * i + 1]], axis=1)
         high, low = halves(pair)
         got = lax.dot_general(
             lhs, jnp.concatenate([high, low, high], axis=0), (((1,), (0,)), ((), ())),
@@ -172,12 +183,14 @@
         return c
 
     lax.fori_loop(0, n // 2, project, 0, unroll=4)
-    lane = lax.broadcasted_iota(jnp.int32, w_ref.shape, 1) // R
+    tiled = jnp.concatenate([w_ref[...]] * share, axis=0)
+    block = lax.broadcasted_iota(jnp.int32, tiled.shape, 0) // R
     total = None
     for a in range(share):
-        part = dot3(z[a], jnp.where(lane == a, w_ref[...], 0.0))
+        part = dot3(z[a], jnp.where(block == a, tiled, 0.0), 1, 1)
         total = part if total is None else total + part
     parts_ref[...] = total
+    written.wait()
 
 
 def conduct(t, k, s, v, w):
@@ -196,7 +209,6 @@
     csouth = lax.ppermute(jnp.concatenate([below[:, m - W:], above[:, m - W:]], 1), "lat", north_to)
     cnorth = lax.ppermute(jnp.concatenate([below[:, :W], above[:, :W]], 1), "lat", south_to)
     share = R // lat
-    vt = v.reshape(m, lat, share).transpose(2, 1, 0).reshape(R, m)
     big = pltpu.VMEM((n + 2 * W, m + 2 * TILE, layers), jnp.float32)
     vmem = pl.BlockSpec(memory_space=pltpu.VMEM)
     return pl.pallas_call(
@@ -206,12 +218,12 @@
             jax.ShapeDtypeStruct((lat * n, share * R), jnp.float32),
         ),
         in_specs=[pl.BlockSpec(memory_space=pl.ANY)] * 3 + [vmem] * 8,
-        out_specs=[vmem] * 2,
-        scratch_shapes=[big] * 7
-        + [pltpu.VMEM((share, lat * n, layers), jnp.float32), pltpu.SemaphoreType.DMA((3,))],
-        compiler_params=pltpu.CompilerParams(vmem_limit_bytes=52 * 2**20),
+        out_specs=[pl.BlockSpec(memory_space=pl.ANY), vmem],
+        scratch_shapes=[big] * 8
+        + [pltpu.VMEM(t.shape, jnp.float32), pltpu.VMEM((share, lat * n, layers), jnp.float32), pltpu.SemaphoreType.DMA((3,))],
+        compiler_params=pltpu.CompilerParams(vmem_limit_bytes=56 * 2**20),
         name="conduct",
-    )(t, k, s, below, above, south, north, csouth, cnorth, vt, jnp.tile(w, (1, share)))
+    )(t, k, s, below, above, south, north, csouth, cnorth, v.T, w.T)
 
 
 def inverse_factor(gram):
@@ -449,7 +461,7 @@
     block = dot3(proj, y)
     inv = inverse_factor(dot(block, block, 1, 1))
     radt = dot(inv, block, 1, 0)
-    rad[...] = flip(radt)
+    rad[...] = radt
     radh = halves(radt)
     core = dot3(y, radh, 1, 1)
     core_ref[...] = core
@@ -542,7 +554,7 @@
     )
     err, new_rad, core = call(
         functools.partial(last_kernel, m), "last",
-        [(n * m, layers), (layers, R), (R * R, R)],
+        [(n * m, layers), (R, layers), (R * R, R)],
         [got.reshape(R * R, layers), inv2, new_lat, new_lon, wt, flat],
         scratch=[
             pltpu.VMEM((R * R, layers), jnp.float32),
@@ -550,7 +562,7 @@
             pltpu.VMEM((R * m, layers), jnp.float32),
         ],
     )
-    return (t, err.reshape(n, m, layers), new_lon, new_lat, new_rad, core.reshape(R, R, R))
+    return (t, err.reshape(n, m, layers), new_lon, new_lat, new_rad.T, core.reshape(R, R, R))
 
 
 def solution(mesh):

time: 186 us -> 185 us (level)
  no operation moved by 1% of the time
where the time goes in v3:
time: 185 us; the launch traced here: 184 us
  blocking collectives  81.3 us (44%)
  Pallas kernels  49.7 us (27%)
  starting transfers between devices  29.7 us (16%)
  waiting for transfers between devices  18.7 us (10%)
  local copies, waits for them, and re-layouts  3.6 us (2%)
    all_to_all x6, blocking collectives, exchange(): return lax.all_to_all(parts, axis, 0, 0, tiled=True)  81.3 us
    pallas_call x12, Pallas kernels, call(): pl.pallas_call(kernel, out_shape=tuple((jax.ShapeDtypeStruct(o, jnp.float...  26.7 us
    pallas_call x1, Pallas kernels, conduct(): pl.pallas_call(functools.partial(conduct_kernel, n, m, lat), out_shape=(j...  18.3 us
    all_to_all x3, starting transfers between devices, exchange(): return lax.all_to_all(parts, axis, 0, 0, tiled=True)  14.8 us
    all_to_all x3, waiting for transfers between devices, exchange(): return lax.all_to_all(parts, axis, 0, 0, tiled=True)  10.8 us
    ppermute x1, starting transfers between devices, conduct(): south = lax.ppermute(high, 'lat', north_to)  5.22 us
    pallas_call x2, Pallas kernels, pack(): pl.pallas_call(kernel, grid=(1,), out_shape=(shape, shape), in_specs=[spe...  4.69 us
    ppermute x1, starting transfers between devices, conduct(): lax.ppermute(jnp.concatenate([below[:, m - W:], above[:, m - W:]], 1), 'l...  4.12 us
  transfers between devices with their start and end apart: 9, of which 7 were waited for; matrix products, arithmetic and copies ran while one was open for 1% of the time, Pallas kernels for 6%

profile of v3, /device:TPU:1, one launch (start us, length us, event | category | flops | bytes accessed | tf_op | source)
XLA Modules:
  0.0 183.9 jit_solution(3964981903421675187)
XLA Ops:
  0.6 2.1 %pack_lon.1 = (f32[11,64,128]{2,1,0:T(8,128)}, f32[11,64,128]{2,1,0:T(8,128)}) custom-call(f32[64,64,128]{2,1,0:T(8,128)} %t_ref.1, f32[64,64,128]{2,1,0:T(8,128)} %k_ref.1, f32[64,64,128]{2,1,0:T(8,128)} %s_ref.1, f32[64,64,128]{2,1,0:T(8,128)} %t_ref.1, f32[64,64,128]{2,1,0:T(8,128)} %k_ref.1, f32[64,64,128]{2,1,0:T(8,128)} %s_ref.1), custom_call_target="tpu_custom_call" | custom-call | tf_op jit(solution)/shard_map/pack_lon/pallas_call | solution.py:74
  2.7 3.0 %collective-permute-start = (f32[11,64,128]{2,1,0:T(8,128)}, f32[11,64,128]{2,1,0:T(8,128)S(1)}, u32[]{:S(2)}, u32[]{:S(2)}) collective-permute-start(f32[11,64,128]{2,1,0:T(8,128)} %get-tuple-element.30), channel_id=1, source_target_pairs={{0,8},{8,16},{16,24},{24,32},{32,40},{40,48},{48,56},{56,64},{64,7... | collective-permute-start | bytes 1081352 | tf_op jit(solution)/shard_map/ppermute | solution.py:207
  5.8 0.0 collective-permute-start.1
  5.8 2.6 %pack_lat.1 = (f32[11,64,128]{2,1,0:T(8,128)}, f32[11,64,128]{2,1,0:T(8,128)}) custom-call(f32[64,64,128]{2,1,0:T(8,128)} %t_ref.1, f32[64,64,128]{2,1,0:T(8,128)} %k_ref.1, f32[64,64,128]{2,1,0:T(8,128)} %s_ref.1, f32[64,64,128]{2,1,0:T(8,128)} %t_ref.1, f32[64,64,128]{2,1,0:T(8,128)} %k_ref.1, f32[64,64,128]{2,1,0:T(8,128)} %s_ref.1), custom_call_target="tpu_custom_call" | custom-call | tf_op jit(solution)/shard_map/pack_lat/pallas_call | solution.py:74
  8.4 5.2 %collective-permute-start.2 = (f32[11,64,128]{2,1,0:T(8,128)}, f32[11,64,128]{2,1,0:T(8,128)S(1)}, u32[]{:S(2)}, u32[]{:S(2)}) collective-permute-start(f32[11,64,128]{2,1,0:T(8,128)} %get-tuple-element.32), channel_id=1, source_target_pairs={{0,1},{1,2},{2,3},{3,4},{4,5},{5,6},{6,7},{8,9},{9,10},{10,11},{11... | collective-permute-start | bytes 1081352 | tf_op jit(solution)/shard_map/ppermute | solution.py:204
  13.6 1.3 collective-permute-start.3
  14.9 0.0 collective-permute-done.below_ref
  14.9 0.0 copy-start.5
  14.9 2.8 %collective-permute-done.1.above_ref = f32[11,64,128]{2,1,0:T(8,128)S(1)} collective-permute-done((f32[11,64,128]{2,1,0:T(8,128)}, f32[11,64,128]{2,1,0:T(8,128)S(1)}, u32[]{:S(2)}, u32[]{:S(2)}) %collective-permute-start.1) | collective-permute-done | bytes 360480 | tf_op jit(solution)/shard_map/ppermute | solution.py:208
  17.8 4.1 %collective-permute-start.4 = (f32[11,8,128]{2,1,0:T(8,128)S(1)}, f32[11,8,128]{2,1,0:T(8,128)S(1)}, u32[]{:S(2)}, u32[]{:S(2)}) collective-permute-start(f32[11,8,128]{2,1,0:T(8,128)S(1)} %pad_maximum_fusion), channel_id=1, source_target_pairs={{0,1},{1,2},{2,3},{3,4},{4,5},{5,6},{6,7},{8,9},{9,10},{10,11},{11... | collective-permute-start | bytes 135176 | tf_op jit(solution)/shard_map/ppermute | solution.py:209
  22.0 1.3 collective-permute-start.5
  23.3 3.4 %collective-permute-done.2.south_ref = f32[11,64,128]{2,1,0:T(8,128)S(1)} collective-permute-done((f32[11,64,128]{2,1,0:T(8,128)}, f32[11,64,128]{2,1,0:T(8,128)S(1)}, u32[]{:S(2)}, u32[]{:S(2)}) %collective-permute-start.2) | collective-permute-done | bytes 360480 | tf_op jit(solution)/shard_map/ppermute | solution.py:204
  26.7 0.0 collective-permute-done.3.north_ref
  26.7 0.9 collective-permute-done.4.csouth_ref
  27.5 0.7 collective-permute-done.5.cnorth_ref
  28.2 0.0 copy-done.5
  28.3 0.0 copy-done.6
  28.3 0.0 copy-done.7
  28.3 0.0 copy-done.8
  28.3 0.6 copy-done.10
  28.9 18.3 %conduct.1 = (f32[64,64,128]{2,1,0:T(8,128)}, f32[512,128]{1,0:T(8,128)}) custom-call(f32[64,64,128]{2,1,0:T(8,128)} %t_ref.1, f32[64,64,128]{2,1,0:T(8,128)} %k_ref.1, f32[64,64,128]{2,1,0:T(8,128)} %s_ref.1, f32[11,64,128]{2,1,0:T(8,128)} %copy-done.5, f32[11,64,128]{2,1,0:T(8,128)} %copy-done.6, f32[11,64,128]{2,1,0:T(8,128)} %copy-done.7, ...), custom_call_target="tpu_custom_call" | custom-call | tf_op jit(solution)/shard_map/conduct/pallas_call | solution.py:214
  47.2 23.6 %all_to_all.45.got = f32[8,64,128]{2,1,0:T(8,128)S(1)} all-to-all(f32[8,64,128]{2,1,0:T(8,128)} %bitcast.25), channel_id=1, replica_groups=mesh['lon'=16,'lat'=8] {'lat'}, dimensions={0} | all-to-all | bytes 524288 | tf_op jit(solution)/shard_map/all_to_all | solution.py:498
  70.8 0.2 lon_project.1
  71.0 11.6 %all_to_all.46.got = f32[16,32,128]{2,1,0:T(8,128)S(1)} all-to-all(f32[16,32,128]{2,1,0:T(8,128)S(1)} %get-tuple-element.36), channel_id=1, replica_groups=mesh['lon'=16,'lat'=8] {'lon'}, dimensions={0} | all-to-all | bytes 524288 | tf_op jit(solution)/shard_map/all_to_all | solution.py:498
  82.6 0.9 lon_block.1
  83.4 3.5 %all-to-all-start.2 = ((f32[8,16,128]{2,1,0:T(8,128)}), f32[8,16,128]{2,1,0:T(8,128)S(1)}, u32[]{:S(2)}, u32[]{:S(2)}) async-start(f32[8,16,128]{2,1,0:T(8,128)} %lon_block.1), calls=%async_computation.2 | async-start | bytes 131072 | tf_op jit(solution)/shard_map/all_to_all | solution.py:498
  87.0 0.0 copy-start
  87.0 1.6 copy-done
  88.6 3.1 %radial.1.rt = f32[2,512,128]{2,1,0:T(8,128)S(1)} custom-call(f32[4096,128]{1,0:T(8,128)S(1)} %bitcast.14, f32[32,128]{1,0:T(8,128)S(1)} %bitcast.23), custom_call_target="tpu_custom_call" | custom-call | bytes 12000000 | tf_op jit(solution)/shard_map/radial/pallas_call | solution.py:249
  91.7 1.9 %all-to-all-done.2.got = f32[8,16,128]{2,1,0:T(8,128)S(1)} async-done(((f32[8,16,128]{2,1,0:T(8,128)}), f32[8,16,128]{2,1,0:T(8,128)S(1)}, u32[]{:S(2)}, u32[]{:S(2)}) %all-to-all-start.2) | async-done | bytes 65568 | tf_op jit(solution)/shard_map/all_to_all | solution.py:498
  93.6 0.5 lat_modes.1
  94.2 12.3 %all_to_all.47.got = f32[16,40,128]{2,1,0:T(8,128)S(1)} all-to-all(f32[16,40,128]{2,1,0:T(8,128)S(1)} %get-tuple-element.38), channel_id=1, replica_groups=mesh['lon'=16,'lat'=8] {'lon'}, dimensions={0} | all-to-all | bytes 655360 | tf_op jit(solution)/shard_map/all_to_all | solution.py:498
  106.5 3.4 %lat_project.1 = (f32[8,32,128]{2,1,0:T(8,128)S(1)}, f32[32,128]{1,0:T(8,128)S(1)}, f32[64,32]{1,0:T(8,128)S(1)}, f32[32,64]{1,0:T(8,128)S(1)}) custom-call(f32[16,40,128]{2,1,0:T(8,128)S(1)} %all_to_all.47.got, f32[32,64]{1,0:T(8,128)S(1)} %get-tuple-element.39.b1, f32[32,64]{1,0:T(8,128)S(1)} %bitcast.22), custom_call_target="tpu_custom_call" | custom-call | tf_op jit(solution)/shard_map/lat_project/pallas_call | solution.py:249
  109.9 10.8 %all_to_all.48.got = f32[8,32,128]{2,1,0:T(8,128)S(1)} all-to-all(f32[8,32,128]{2,1,0:T(8,128)S(1)} %get-tuple-element.40), channel_id=1, replica_groups=mesh['lon'=16,'lat'=8] {'lat'}, dimensions={0} | all-to-all | bytes 262144 | tf_op jit(solution)/shard_map/all_to_all | solution.py:498
  120.7 1.0 lat_block.1
  121.6 5.1 %all-to-all-start.5 = ((f32[16,16,128]{2,1,0:T(8,128)}), f32[16,16,128]{2,1,0:T(8,128)S(1)}, u32[]{:S(2)}, u32[]{:S(2)}) async-start(f32[16,16,128]{2,1,0:T(8,128)} %lat_block.1), calls=%async_computation.5 | async-start | bytes 262144 | tf_op jit(solution)/shard_map/all_to_all | solution.py:498
  126.8 2.6 %lon_sums.1.lp = f32[2048,128]{1,0:T(8,128)S(1)} custom-call(f32[4096,128]{1,0:T(8,128)S(1)} %bitcast.15, f32[32,64]{1,0:T(8,128)S(1)} %get-tuple-element.42.lont), custom_call_target="tpu_custom_call" | custom-call | bytes 12000000 | tf_op jit(solution)/shard_map/lon_sums/pallas_call | solution.py:249
  129.4 3.6 %all-to-all-done.5.got = f32[16,16,128]{2,1,0:T(8,128)S(1)} async-done(((f32[16,16,128]{2,1,0:T(8,128)}), f32[16,16,128]{2,1,0:T(8,128)S(1)}, u32[]{:S(2)}, u32[]{:S(2)}) %all-to-all-start.5) | async-done | bytes 131104 | tf_op jit(solution)/shard_map/all_to_all | solution.py:498
  133.0 1.0 radial_modes.1
  134.0 12.6 %all_to_all.49.got = f32[16,64,128]{2,1,0:T(8,128)S(1)} all-to-all(f32[16,64,128]{2,1,0:T(8,128)S(1)} %get-tuple-element.43), channel_id=1, replica_groups=mesh['lon'=16,'lat'=8] {'lon'}, dimensions={0} | all-to-all | bytes 1048576 | tf_op jit(solution)/shard_map/all_to_all | solution.py:498
  146.6 10.4 %all_to_all.50.got = f32[8,72,128]{2,1,0:T(8,128)S(1)} all-to-all(f32[8,72,128]{2,1,0:T(8,128)S(1)} %radial_sum.1), channel_id=1, replica_groups=mesh['lon'=16,'lat'=8] {'lat'}, dimensions={0} | all-to-all | bytes 589824 | tf_op jit(solution)/shard_map/all_to_all | solution.py:498
  157.1 0.9 radial_spread.1
  157.9 6.1 %all-to-all-start.8 = ((f32[16,64,128]{2,1,0:T(8,128)}), f32[16,64,128]{2,1,0:T(8,128)S(1)}, u32[]{:S(2)}, u32[]{:S(2)}) async-start(f32[16,64,128]{2,1,0:T(8,128)} %get-tuple-element.45), calls=%async_computation.8 | async-start | bytes 1048576 | tf_op jit(solution)/shard_map/all_to_all | solution.py:498
  164.0 0.7 copy.13
  164.7 2.9 %lat_factor.1 = (f32[32,32]{1,0:T(8,128)S(1)}, f32[64,32]{1,0:T(8,128)S(1)}) custom-call(f32[8,128]{1,0:T(8,128)S(1)} %get-tuple-element.46.g2, f32[32,64]{1,0:T(8,128)S(1)} %get-tuple-element.47.b2), custom_call_target="tpu_custom_call" | custom-call | bytes 12000000 | tf_op jit(solution)/shard_map/lat_factor/pallas_call | solution.py:249
  167.6 0.7 copy.14
  168.3 5.4 %all-to-all-done.8 = f32[16,64,128]{2,1,0:T(8,128)S(1)} async-done(((f32[16,64,128]{2,1,0:T(8,128)}), f32[16,64,128]{2,1,0:T(8,128)S(1)}, u32[]{:S(2)}, u32[]{:S(2)}) %all-to-all-start.8) | async-done | bytes 524320 | tf_op jit(solution)/shard_map/all_to_all | solution.py:498
  173.7 10.2 %last.1 = (f32[4096,128]{1,0:T(8,128)}, f32[32,128]{1,0:T(8,128)}, f32[1024,32]{1,0:T(8,128)}) custom-call(f32[1024,128]{1,0:T(8,128)S(1)} %bitcast.17, f32[32,32]{1,0:T(8,128)S(1)} %get-tuple-element.48.inv2, f32[64,32]{1,0:T(8,128)S(1)} %get-tuple-element.57.lat, f32[64,32]{1,0:T(8,128)S(1)} %get-tuple-element.56.lon, f32[32,128]{1,0:T(8,128)S(1)} %bitcast.20, ...), custom_call_target="tpu_custom_call" | custom-call | tf_op jit(solution)/shard_map/last/pallas_call | solution.py:249
  (20 shorter events, 0.1 us)
Async XLA Ops:
  2.7 12.2 %collective-permute-start = (f32[11,64,128]{2,1,0:T(8,128)}, f32[11,64,128]{2,1,0:T(8,128)S(1)}, u32[]{:S(2)}, u32[]{:S(2)}) collective-permute-start(f32[11,64,128]{2,1,0:T(8,128)} %get-tuple-element.30), channel_id=1, source_target_pairs={{0,8},{8,16},{16,24},{24,32},{32,40},{40,48},{48,56},{56,64},{64,7... | collective-permute-start | bytes 1081352 | tf_op jit(solution)/shard_map/ppermute | solution.py:207
  5.8 12.0 %collective-permute-start.1 = (f32[11,64,128]{2,1,0:T(8,128)}, f32[11,64,128]{2,1,0:T(8,128)S(1)}, u32[]{:S(2)}, u32[]{:S(2)}) collective-permute-start(f32[11,64,128]{2,1,0:T(8,128)} %get-tuple-element.31), channel_id=1, source_target_pairs={{8,0},{16,8},{24,16},{32,24},{40,32},{48,40},{56,48},{64,56},{72,6... | collective-permute-start | bytes 1081352 | tf_op jit(solution)/shard_map/ppermute | solution.py:208
  8.4 18.3 %collective-permute-start.2 = (f32[11,64,128]{2,1,0:T(8,128)}, f32[11,64,128]{2,1,0:T(8,128)S(1)}, u32[]{:S(2)}, u32[]{:S(2)}) collective-permute-start(f32[11,64,128]{2,1,0:T(8,128)} %get-tuple-element.32), channel_id=1, source_target_pairs={{0,1},{1,2},{2,3},{3,4},{4,5},{5,6},{6,7},{8,9},{9,10},{10,11},{11... | collective-permute-start | bytes 1081352 | tf_op jit(solution)/shard_map/ppermute | solution.py:204
  13.6 13.1 %collective-permute-start.3 = (f32[11,64,128]{2,1,0:T(8,128)}, f32[11,64,128]{2,1,0:T(8,128)S(1)}, u32[]{:S(2)}, u32[]{:S(2)}) collective-permute-start(f32[11,64,128]{2,1,0:T(8,128)} %get-tuple-element.33), channel_id=1, source_target_pairs={{1,0},{2,1},{3,2},{4,3},{5,4},{6,5},{7,6},{9,8},{10,9},{11,10},{12... | collective-permute-start | bytes 1081352 | tf_op jit(solution)/shard_map/ppermute | solution.py:205
  14.9 13.4 %copy-start.5 = (f32[11,64,128]{2,1,0:T(8,128)}, f32[11,64,128]{2,1,0:T(8,128)S(1)}, u32[]{:S(2)}) copy-start(f32[11,64,128]{2,1,0:T(8,128)S(1)} %collective-permute-done.below_ref) | copy-start | bytes 1081348
  17.8 10.5 %copy-start.6 = (f32[11,64,128]{2,1,0:T(8,128)}, f32[11,64,128]{2,1,0:T(8,128)S(1)}, u32[]{:S(2)}) copy-start(f32[11,64,128]{2,1,0:T(8,128)S(1)} %collective-permute-done.1.above_ref) | copy-start | bytes 1081348
  17.8 9.7 %collective-permute-start.4 = (f32[11,8,128]{2,1,0:T(8,128)S(1)}, f32[11,8,128]{2,1,0:T(8,128)S(1)}, u32[]{:S(2)}, u32[]{:S(2)}) collective-permute-start(f32[11,8,128]{2,1,0:T(8,128)S(1)} %pad_maximum_fusion), channel_id=1, source_target_pairs={{0,1},{1,2},{2,3},{3,4},{4,5},{5,6},{6,7},{8,9},{9,10},{10,11},{11... | collective-permute-start | bytes 135176 | tf_op jit(solution)/shard_map/ppermute | solution.py:209
  22.0 6.3 %collective-permute-start.5 = (f32[11,8,128]{2,1,0:T(8,128)S(1)}, f32[11,8,128]{2,1,0:T(8,128)S(1)}, u32[]{:S(2)}, u32[]{:S(2)}) collective-permute-start(f32[11,8,128]{2,1,0:T(8,128)S(1)} %pad_maximum_fusion.1), channel_id=1, source_target_pairs={{1,0},{2,1},{3,2},{4,3},{5,4},{6,5},{7,6},{9,8},{10,9},{11,10},{12... | collective-permute-start | bytes 135176 | tf_op jit(solution)/shard_map/ppermute | solution.py:210
  26.7 1.6 copy-start.7
  26.7 1.6 copy-start.8
  27.5 0.8 copy-start.9
  28.2 0.6 copy-start.10
  28.9 41.9 %copy-start.4 = (f32[64,32]{0,1:T(8,128)S(1)}, f32[64,32]{0,1:T(8,128)}, u32[]{:S(2)}) copy-start(f32[64,32]{0,1:T(8,128)} %param.9) | copy-start | bytes 24580
  28.9 58.1 %copy-start.2 = (f32[128,32]{0,1:T(8,128)S(1)}, f32[128,32]{0,1:T(8,128)}, u32[]{:S(2)}) copy-start(f32[128,32]{0,1:T(8,128)} %param.11) | copy-start | bytes 49156
  83.4 23.0 %copy-start.3 = (f32[64,32]{0,1:T(8,128)S(1)}, f32[64,32]{0,1:T(8,128)}, u32[]{:S(2)}) copy-start(f32[64,32]{0,1:T(8,128)} %param.10) | copy-start | bytes 24580
  83.4 10.2 %all-to-all-start.2 = ((f32[8,16,128]{2,1,0:T(8,128)}), f32[8,16,128]{2,1,0:T(8,128)S(1)}, u32[]{:S(2)}, u32[]{:S(2)}) async-start(f32[8,16,128]{2,1,0:T(8,128)} %lon_block.1), calls=%async_computation.2 | async-start | bytes 131072 | tf_op jit(solution)/shard_map/all_to_all | solution.py:498
  87.0 1.6 copy-start
  88.6 38.2 %copy-start.1 = (f32[64,64,128]{2,1,0:T(8,128)S(1)}, f32[64,64,128]{2,1,0:T(8,128)}, u32[]{:S(2)}) copy-start(f32[64,64,128]{2,1,0:T(8,128)} %get-tuple-element.54) | copy-start | bytes 6291460
  121.6 11.3 %all-to-all-start.5 = ((f32[16,16,128]{2,1,0:T(8,128)}), f32[16,16,128]{2,1,0:T(8,128)S(1)}, u32[]{:S(2)}, u32[]{:S(2)}) async-start(f32[16,16,128]{2,1,0:T(8,128)} %lat_block.1), calls=%async_computation.5 | async-start | bytes 262144 | tf_op jit(solution)/shard_map/all_to_all | solution.py:498
  157.9 15.8 %all-to-all-start.8 = ((f32[16,64,128]{2,1,0:T(8,128)}), f32[16,64,128]{2,1,0:T(8,128)S(1)}, u32[]{:S(2)}, u32[]{:S(2)}) async-start(f32[16,64,128]{2,1,0:T(8,128)} %get-tuple-element.45), calls=%async_computation.8 | async-start | bytes 1048576 | tf_op jit(solution)/shard_map/all_to_all | solution.py:498

commit v4 on v3

--- a/solution.py
+++ b/solution.py
@@ -229,18 +229,22 @@
 def inverse_factor(gram):
     n = gram.shape[0]
     row = lax.broadcasted_iota(jnp.int32, (n, n), 0)
-    col = lax.broadcasted_iota(jnp.int32, (n, n), 1)
-    a = gram
-    inv = jnp.where(row == col, 1.0, 0.0).astype(jnp.float32)
-    scale = jnp.zeros((n, 1), jnp.float32)
-    r1 = lax.broadcasted_iota(jnp.int32, (n, 1), 0)
+    inv = jnp.where(row == lax.broadcasted_iota(jnp.int32, (n, n), 1), 1.0, 0.0)
+    scale = jnp.zeros((n, n), jnp.float32)
+    columns = [jnp.broadcast_to(gram[:, k:k + 1], (n, n)) for k in range(n)]
     for j in range(n):
-        column = a[:, j:j + 1]
-        pivot = a[j:j + 1, j:j + 1]
-        factor = jnp.where(r1 > j, column / pivot, 0.0)
-        scale = jnp.where(r1 == j, lax.rsqrt(pivot), scale)
-        a = a - factor * a[j:j + 1, :]
-        inv = inv - factor * inv[j:j + 1, :]
+        top, at = j // 8 * 8, j % 8
+        if at == 0 and j:
+            columns = [c if c is None else c[8:] for c in columns]
+        column = columns[j]
+        pivot = column[at:at + 1]
+        factor = jnp.where(row[top:] > j, column, 0.0) * (1.0 / pivot)
+        for k in range(j + 1, n):
+            columns[k] = columns[k] - factor * columns[k][at:at + 1]
+        columns[j] = None
+        scale = jnp.where(row == j, lax.rsqrt(pivot), scale)
+        below = inv[top:] - factor * inv[j:j + 1]
+        inv = below if top == 0 else jnp.concatenate([inv[:top], below], axis=0)
     return inv * scale
 
 

time: 185 us -> 181 us (0.978)
  Pallas kernels: 49.7 us -> 43.9 us
  waiting for transfers between devices: 18.7 us -> 20.6 us
    pallas_call x12, Pallas kernels: 26.7 us -> 20.8 us  [call(): pl.pallas_call(kernel, out_shape=tuple((jax.ShapeDtypeStruct(o, jnp.float...]
    all_to_all x3, waiting for transfers between devices: 10.8 us -> 12.8 us  [exchange(): return lax.all_to_all(parts, axis, 0, 0, tiled=True)]
  transfers between devices with their start and end apart: 9 -> 9, of which waited for: 7 -> 7; matrix products, arithmetic and copies ran while one was open for 1% -> 1% of each run, Pallas kernels for 6% -> 5%
where the time goes in v4:
time: 181 us; the launch traced here: 180 us
  blocking collectives  81.3 us (45%)
  Pallas kernels  43.9 us (24%)
  starting transfers between devices  29.7 us (16%)
  waiting for transfers between devices  20.6 us (11%)
  local copies, waits for them, and re-layouts  3.6 us (2%)
    all_to_all x6, blocking collectives, exchange(): return lax.all_to_all(parts, axis, 0, 0, tiled=True)  81.3 us
    pallas_call x12, Pallas kernels, call(): pl.pallas_call(kernel, out_shape=tuple((jax.ShapeDtypeStruct(o, jnp.float...  20.8 us
    pallas_call x1, Pallas kernels, conduct(): pl.pallas_call(functools.partial(conduct_kernel, n, m, lat), out_shape=(j...  18.3 us
    all_to_all x3, starting transfers between devices, exchange(): return lax.all_to_all(parts, axis, 0, 0, tiled=True)  14.8 us
    all_to_all x3, waiting for transfers between devices, exchange(): return lax.all_to_all(parts, axis, 0, 0, tiled=True)  12.8 us
    ppermute x1, starting transfers between devices, conduct(): south = lax.ppermute(high, 'lat', north_to)  5.22 us
    pallas_call x2, Pallas kernels, pack(): pl.pallas_call(kernel, grid=(1,), out_shape=(shape, shape), in_specs=[spe...  4.69 us
    ppermute x1, starting transfers between devices, conduct(): lax.ppermute(jnp.concatenate([below[:, m - W:], above[:, m - W:]], 1), 'l...  4.12 us
  transfers between devices with their start and end apart: 9, of which 7 were waited for; matrix products, arithmetic and copies ran while one was open for 1% of the time, Pallas kernels for 5%

profile of v4, /device:TPU:1, one launch (start us, length us, event | category | flops | bytes accessed | tf_op | source)
XLA Modules:
  0.0 180.0 jit_solution(1183473769741406144)
XLA Ops:
  0.6 2.1 %pack_lon.1 = (f32[11,64,128]{2,1,0:T(8,128)}, f32[11,64,128]{2,1,0:T(8,128)}) custom-call(f32[64,64,128]{2,1,0:T(8,128)} %t_ref.1, f32[64,64,128]{2,1,0:T(8,128)} %k_ref.1, f32[64,64,128]{2,1,0:T(8,128)} %s_ref.1, f32[64,64,128]{2,1,0:T(8,128)} %t_ref.1, f32[64,64,128]{2,1,0:T(8,128)} %k_ref.1, f32[64,64,128]{2,1,0:T(8,128)} %s_ref.1), custom_call_target="tpu_custom_call" | custom-call | tf_op jit(solution)/shard_map/pack_lon/pallas_call | solution.py:74
  2.7 3.0 %collective-permute-start = (f32[11,64,128]{2,1,0:T(8,128)}, f32[11,64,128]{2,1,0:T(8,128)S(1)}, u32[]{:S(2)}, u32[]{:S(2)}) collective-permute-start(f32[11,64,128]{2,1,0:T(8,128)} %get-tuple-element.30), channel_id=1, source_target_pairs={{0,8},{8,16},{16,24},{24,32},{32,40},{40,48},{48,56},{56,64},{64,7... | collective-permute-start | bytes 1081352 | tf_op jit(solution)/shard_map/ppermute | solution.py:207
  5.8 0.0 collective-permute-start.1
  5.8 2.6 %pack_lat.1 = (f32[11,64,128]{2,1,0:T(8,128)}, f32[11,64,128]{2,1,0:T(8,128)}) custom-call(f32[64,64,128]{2,1,0:T(8,128)} %t_ref.1, f32[64,64,128]{2,1,0:T(8,128)} %k_ref.1, f32[64,64,128]{2,1,0:T(8,128)} %s_ref.1, f32[64,64,128]{2,1,0:T(8,128)} %t_ref.1, f32[64,64,128]{2,1,0:T(8,128)} %k_ref.1, f32[64,64,128]{2,1,0:T(8,128)} %s_ref.1), custom_call_target="tpu_custom_call" | custom-call | tf_op jit(solution)/shard_map/pack_lat/pallas_call | solution.py:74
  8.4 5.2 %collective-permute-start.2 = (f32[11,64,128]{2,1,0:T(8,128)}, f32[11,64,128]{2,1,0:T(8,128)S(1)}, u32[]{:S(2)}, u32[]{:S(2)}) collective-permute-start(f32[11,64,128]{2,1,0:T(8,128)} %get-tuple-element.32), channel_id=1, source_target_pairs={{0,1},{1,2},{2,3},{3,4},{4,5},{5,6},{6,7},{8,9},{9,10},{10,11},{11... | collective-permute-start | bytes 1081352 | tf_op jit(solution)/shard_map/ppermute | solution.py:204
  13.6 1.3 collective-permute-start.3
  14.9 0.0 collective-permute-done.below_ref
  14.9 0.0 copy-start.5
  14.9 2.8 %collective-permute-done.1.above_ref = f32[11,64,128]{2,1,0:T(8,128)S(1)} collective-permute-done((f32[11,64,128]{2,1,0:T(8,128)}, f32[11,64,128]{2,1,0:T(8,128)S(1)}, u32[]{:S(2)}, u32[]{:S(2)}) %collective-permute-start.1) | collective-permute-done | bytes 360480 | tf_op jit(solution)/shard_map/ppermute | solution.py:208
  17.8 4.1 %collective-permute-start.4 = (f32[11,8,128]{2,1,0:T(8,128)S(1)}, f32[11,8,128]{2,1,0:T(8,128)S(1)}, u32[]{:S(2)}, u32[]{:S(2)}) collective-permute-start(f32[11,8,128]{2,1,0:T(8,128)S(1)} %pad_maximum_fusion), channel_id=1, source_target_pairs={{0,1},{1,2},{2,3},{3,4},{4,5},{5,6},{6,7},{8,9},{9,10},{10,11},{11... | collective-permute-start | bytes 135176 | tf_op jit(solution)/shard_map/ppermute | solution.py:209
  22.0 1.3 collective-permute-start.5
  23.3 3.4 %collective-permute-done.2.south_ref = f32[11,64,128]{2,1,0:T(8,128)S(1)} collective-permute-done((f32[11,64,128]{2,1,0:T(8,128)}, f32[11,64,128]{2,1,0:T(8,128)S(1)}, u32[]{:S(2)}, u32[]{:S(2)}) %collective-permute-start.2) | collective-permute-done | bytes 360480 | tf_op jit(solution)/shard_map/ppermute | solution.py:204
  26.7 0.0 collective-permute-done.3.north_ref
  26.7 0.9 collective-permute-done.4.csouth_ref
  27.5 0.7 collective-permute-done.5.cnorth_ref
  28.2 0.0 copy-done.5
  28.3 0.0 copy-done.6
  28.3 0.0 copy-done.7
  28.3 0.6 copy-done.10
  28.9 18.3 %conduct.1 = (f32[64,64,128]{2,1,0:T(8,128)}, f32[512,128]{1,0:T(8,128)}) custom-call(f32[64,64,128]{2,1,0:T(8,128)} %t_ref.1, f32[64,64,128]{2,1,0:T(8,128)} %k_ref.1, f32[64,64,128]{2,1,0:T(8,128)} %s_ref.1, f32[11,64,128]{2,1,0:T(8,128)} %copy-done.5, f32[11,64,128]{2,1,0:T(8,128)} %copy-done.6, f32[11,64,128]{2,1,0:T(8,128)} %copy-done.7, ...), custom_call_target="tpu_custom_call" | custom-call | tf_op jit(solution)/shard_map/conduct/pallas_call | solution.py:214
  47.2 23.6 %all_to_all.45.got = f32[8,64,128]{2,1,0:T(8,128)S(1)} all-to-all(f32[8,64,128]{2,1,0:T(8,128)} %bitcast.25), channel_id=1, replica_groups=mesh['lon'=16,'lat'=8] {'lat'}, dimensions={0} | all-to-all | bytes 524288 | tf_op jit(solution)/shard_map/all_to_all | solution.py:502
  70.8 0.2 lon_project.1
  71.0 11.6 %all_to_all.46.got = f32[16,32,128]{2,1,0:T(8,128)S(1)} all-to-all(f32[16,32,128]{2,1,0:T(8,128)S(1)} %get-tuple-element.36), channel_id=1, replica_groups=mesh['lon'=16,'lat'=8] {'lon'}, dimensions={0} | all-to-all | bytes 524288 | tf_op jit(solution)/shard_map/all_to_all | solution.py:502
  82.6 0.9 lon_block.1
  83.5 3.5 %all-to-all-start.2 = ((f32[8,16,128]{2,1,0:T(8,128)}), f32[8,16,128]{2,1,0:T(8,128)S(1)}, u32[]{:S(2)}, u32[]{:S(2)}) async-start(f32[8,16,128]{2,1,0:T(8,128)} %lon_block.1), calls=%async_computation.2 | async-start | bytes 131072 | tf_op jit(solution)/shard_map/all_to_all | solution.py:502
  87.0 0.0 copy-done.2
  87.0 0.0 copy-start
  87.0 1.6 copy-done
  88.6 3.1 %radial.1.rt = f32[2,512,128]{2,1,0:T(8,128)S(1)} custom-call(f32[4096,128]{1,0:T(8,128)S(1)} %bitcast.14, f32[32,128]{1,0:T(8,128)S(1)} %bitcast.23), custom_call_target="tpu_custom_call" | custom-call | bytes 12000000 | tf_op jit(solution)/shard_map/radial/pallas_call | solution.py:253
  91.7 1.9 %all-to-all-done.2.got = f32[8,16,128]{2,1,0:T(8,128)S(1)} async-done(((f32[8,16,128]{2,1,0:T(8,128)}), f32[8,16,128]{2,1,0:T(8,128)S(1)}, u32[]{:S(2)}, u32[]{:S(2)}) %all-to-all-start.2) | async-done | bytes 65568 | tf_op jit(solution)/shard_map/all_to_all | solution.py:502
  93.6 0.6 lat_modes.1
  94.2 12.3 %all_to_all.47.got = f32[16,40,128]{2,1,0:T(8,128)S(1)} all-to-all(f32[16,40,128]{2,1,0:T(8,128)S(1)} %get-tuple-element.38), channel_id=1, replica_groups=mesh['lon'=16,'lat'=8] {'lon'}, dimensions={0} | all-to-all | bytes 655360 | tf_op jit(solution)/shard_map/all_to_all | solution.py:502
  106.5 1.4 lat_project.1
  107.9 10.8 %all_to_all.48.got = f32[8,32,128]{2,1,0:T(8,128)S(1)} all-to-all(f32[8,32,128]{2,1,0:T(8,128)S(1)} %get-tuple-element.40), channel_id=1, replica_groups=mesh['lon'=16,'lat'=8] {'lat'}, dimensions={0} | all-to-all | bytes 262144 | tf_op jit(solution)/shard_map/all_to_all | solution.py:502
  118.7 1.0 lat_block.1
  119.7 5.1 %all-to-all-start.5 = ((f32[16,16,128]{2,1,0:T(8,128)}), f32[16,16,128]{2,1,0:T(8,128)S(1)}, u32[]{:S(2)}, u32[]{:S(2)}) async-start(f32[16,16,128]{2,1,0:T(8,128)} %lat_block.1), calls=%async_computation.5 | async-start | bytes 262144 | tf_op jit(solution)/shard_map/all_to_all | solution.py:502
  124.8 2.6 %lon_sums.1.lp = f32[2048,128]{1,0:T(8,128)S(1)} custom-call(f32[4096,128]{1,0:T(8,128)S(1)} %bitcast.15, f32[32,64]{1,0:T(8,128)S(1)} %get-tuple-element.42.lont), custom_call_target="tpu_custom_call" | custom-call | bytes 12000000 | tf_op jit(solution)/shard_map/lon_sums/pallas_call | solution.py:253
  127.4 3.6 %all-to-all-done.5.got = f32[16,16,128]{2,1,0:T(8,128)S(1)} async-done(((f32[16,16,128]{2,1,0:T(8,128)}), f32[16,16,128]{2,1,0:T(8,128)S(1)}, u32[]{:S(2)}, u32[]{:S(2)}) %all-to-all-start.5) | async-done | bytes 131104 | tf_op jit(solution)/shard_map/all_to_all | solution.py:502
  131.0 1.0 radial_modes.1
  132.0 12.6 %all_to_all.49.got = f32[16,64,128]{2,1,0:T(8,128)S(1)} all-to-all(f32[16,64,128]{2,1,0:T(8,128)S(1)} %get-tuple-element.43), channel_id=1, replica_groups=mesh['lon'=16,'lat'=8] {'lon'}, dimensions={0} | all-to-all | bytes 1048576 | tf_op jit(solution)/shard_map/all_to_all | solution.py:502
  144.6 10.4 %all_to_all.50.got = f32[8,72,128]{2,1,0:T(8,128)S(1)} all-to-all(f32[8,72,128]{2,1,0:T(8,128)S(1)} %radial_sum.1), channel_id=1, replica_groups=mesh['lon'=16,'lat'=8] {'lat'}, dimensions={0} | all-to-all | bytes 589824 | tf_op jit(solution)/shard_map/all_to_all | solution.py:502
  155.1 0.9 radial_spread.1
  155.9 6.1 %all-to-all-start.8 = ((f32[16,64,128]{2,1,0:T(8,128)}), f32[16,64,128]{2,1,0:T(8,128)S(1)}, u32[]{:S(2)}, u32[]{:S(2)}) async-start(f32[16,64,128]{2,1,0:T(8,128)} %get-tuple-element.45), calls=%async_computation.8 | async-start | bytes 1048576 | tf_op jit(solution)/shard_map/all_to_all | solution.py:502
  162.0 0.7 copy.13
  162.7 1.0 lat_factor.1
  163.7 0.7 copy.14
  164.4 7.3 %all-to-all-done.8 = f32[16,64,128]{2,1,0:T(8,128)S(1)} async-done(((f32[16,64,128]{2,1,0:T(8,128)}), f32[16,64,128]{2,1,0:T(8,128)S(1)}, u32[]{:S(2)}, u32[]{:S(2)}) %all-to-all-start.8) | async-done | bytes 524320 | tf_op jit(solution)/shard_map/all_to_all | solution.py:502
  171.7 8.2 %last.1 = (f32[4096,128]{1,0:T(8,128)}, f32[32,128]{1,0:T(8,128)}, f32[1024,32]{1,0:T(8,128)}) custom-call(f32[1024,128]{1,0:T(8,128)S(1)} %bitcast.17, f32[32,32]{1,0:T(8,128)S(1)} %get-tuple-element.48.inv2, f32[64,32]{1,0:T(8,128)S(1)} %get-tuple-element.57.lat, f32[64,32]{1,0:T(8,128)S(1)} %get-tuple-element.56.lon, f32[32,128]{1,0:T(8,128)S(1)} %bitcast.20, ...), custom_call_target="tpu_custom_call" | custom-call | tf_op jit(solution)/shard_map/last/pallas_call | solution.py:253
  (20 shorter events, 0.1 us)
Async XLA Ops:
  2.7 12.2 %collective-permute-start = (f32[11,64,128]{2,1,0:T(8,128)}, f32[11,64,128]{2,1,0:T(8,128)S(1)}, u32[]{:S(2)}, u32[]{:S(2)}) collective-permute-start(f32[11,64,128]{2,1,0:T(8,128)} %get-tuple-element.30), channel_id=1, source_target_pairs={{0,8},{8,16},{16,24},{24,32},{32,40},{40,48},{48,56},{56,64},{64,7... | collective-permute-start | bytes 1081352 | tf_op jit(solution)/shard_map/ppermute | solution.py:207
  5.8 12.0 %collective-permute-start.1 = (f32[11,64,128]{2,1,0:T(8,128)}, f32[11,64,128]{2,1,0:T(8,128)S(1)}, u32[]{:S(2)}, u32[]{:S(2)}) collective-permute-start(f32[11,64,128]{2,1,0:T(8,128)} %get-tuple-element.31), channel_id=1, source_target_pairs={{8,0},{16,8},{24,16},{32,24},{40,32},{48,40},{56,48},{64,56},{72,6... | collective-permute-start | bytes 1081352 | tf_op jit(solution)/shard_map/ppermute | solution.py:208
  8.4 18.3 %collective-permute-start.2 = (f32[11,64,128]{2,1,0:T(8,128)}, f32[11,64,128]{2,1,0:T(8,128)S(1)}, u32[]{:S(2)}, u32[]{:S(2)}) collective-permute-start(f32[11,64,128]{2,1,0:T(8,128)} %get-tuple-element.32), channel_id=1, source_target_pairs={{0,1},{1,2},{2,3},{3,4},{4,5},{5,6},{6,7},{8,9},{9,10},{10,11},{11... | collective-permute-start | bytes 1081352 | tf_op jit(solution)/shard_map/ppermute | solution.py:204
  13.6 13.1 %collective-permute-start.3 = (f32[11,64,128]{2,1,0:T(8,128)}, f32[11,64,128]{2,1,0:T(8,128)S(1)}, u32[]{:S(2)}, u32[]{:S(2)}) collective-permute-start(f32[11,64,128]{2,1,0:T(8,128)} %get-tuple-element.33), channel_id=1, source_target_pairs={{1,0},{2,1},{3,2},{4,3},{5,4},{6,5},{7,6},{9,8},{10,9},{11,10},{12... | collective-permute-start | bytes 1081352 | tf_op jit(solution)/shard_map/ppermute | solution.py:205
  14.9 13.4 %copy-start.5 = (f32[11,64,128]{2,1,0:T(8,128)}, f32[11,64,128]{2,1,0:T(8,128)S(1)}, u32[]{:S(2)}) copy-start(f32[11,64,128]{2,1,0:T(8,128)S(1)} %collective-permute-done.below_ref) | copy-start | bytes 1081348
  17.8 10.5 %copy-start.6 = (f32[11,64,128]{2,1,0:T(8,128)}, f32[11,64,128]{2,1,0:T(8,128)S(1)}, u32[]{:S(2)}) copy-start(f32[11,64,128]{2,1,0:T(8,128)S(1)} %collective-permute-done.1.above_ref) | copy-start | bytes 1081348
  17.8 9.7 %collective-permute-start.4 = (f32[11,8,128]{2,1,0:T(8,128)S(1)}, f32[11,8,128]{2,1,0:T(8,128)S(1)}, u32[]{:S(2)}, u32[]{:S(2)}) collective-permute-start(f32[11,8,128]{2,1,0:T(8,128)S(1)} %pad_maximum_fusion), channel_id=1, source_target_pairs={{0,1},{1,2},{2,3},{3,4},{4,5},{5,6},{6,7},{8,9},{9,10},{10,11},{11... | collective-permute-start | bytes 135176 | tf_op jit(solution)/shard_map/ppermute | solution.py:209
  22.0 6.3 %collective-permute-start.5 = (f32[11,8,128]{2,1,0:T(8,128)S(1)}, f32[11,8,128]{2,1,0:T(8,128)S(1)}, u32[]{:S(2)}, u32[]{:S(2)}) collective-permute-start(f32[11,8,128]{2,1,0:T(8,128)S(1)} %pad_maximum_fusion.1), channel_id=1, source_target_pairs={{1,0},{2,1},{3,2},{4,3},{5,4},{6,5},{7,6},{9,8},{10,9},{11,10},{12... | collective-permute-start | bytes 135176 | tf_op jit(solution)/shard_map/ppermute | solution.py:210
  26.7 1.6 copy-start.7
  26.7 1.6 copy-start.8
  27.5 0.8 copy-start.9
  28.2 0.6 copy-start.10
  28.9 41.9 %copy-start.4 = (f32[64,32]{0,1:T(8,128)S(1)}, f32[64,32]{0,1:T(8,128)}, u32[]{:S(2)}) copy-start(f32[64,32]{0,1:T(8,128)} %param.9) | copy-start | bytes 24580
  28.9 58.1 %copy-start.2 = (f32[128,32]{0,1:T(8,128)S(1)}, f32[128,32]{0,1:T(8,128)}, u32[]{:S(2)}) copy-start(f32[128,32]{0,1:T(8,128)} %param.11) | copy-start | bytes 49156
  83.5 23.0 %copy-start.3 = (f32[64,32]{0,1:T(8,128)S(1)}, f32[64,32]{0,1:T(8,128)}, u32[]{:S(2)}) copy-start(f32[64,32]{0,1:T(8,128)} %param.10) | copy-start | bytes 24580
  83.5 10.2 %all-to-all-start.2 = ((f32[8,16,128]{2,1,0:T(8,128)}), f32[8,16,128]{2,1,0:T(8,128)S(1)}, u32[]{:S(2)}, u32[]{:S(2)}) async-start(f32[8,16,128]{2,1,0:T(8,128)} %lon_block.1), calls=%async_computation.2 | async-start | bytes 131072 | tf_op jit(solution)/shard_map/all_to_all | solution.py:502
  87.0 1.6 copy-start
  88.6 36.2 %copy-start.1 = (f32[64,64,128]{2,1,0:T(8,128)S(1)}, f32[64,64,128]{2,1,0:T(8,128)}, u32[]{:S(2)}) copy-start(f32[64,64,128]{2,1,0:T(8,128)} %get-tuple-element.54) | copy-start | bytes 6291460
  119.7 11.3 %all-to-all-start.5 = ((f32[16,16,128]{2,1,0:T(8,128)}), f32[16,16,128]{2,1,0:T(8,128)S(1)}, u32[]{:S(2)}, u32[]{:S(2)}) async-start(f32[16,16,128]{2,1,0:T(8,128)} %lat_block.1), calls=%async_computation.5 | async-start | bytes 262144 | tf_op jit(solution)/shard_map/all_to_all | solution.py:502
  155.9 15.8 %all-to-all-start.8 = ((f32[16,64,128]{2,1,0:T(8,128)}), f32[16,64,128]{2,1,0:T(8,128)S(1)}, u32[]{:S(2)}, u32[]{:S(2)}) async-start(f32[16,64,128]{2,1,0:T(8,128)} %get-tuple-element.45), calls=%async_computation.8 | async-start | bytes 1048576 | tf_op jit(solution)/shard_map/all_to_all | solution.py:502

commit v5 on v4

--- a/solution.py
+++ b/solution.py
@@ -127,7 +127,7 @@
         hd[i, rows, :] = pltpu.roll(up, 1, 1)
         return kn
 
-    lax.fori_loop(0, planes - 1, faces, k[0, rows, :], unroll=4)
+    lax.fori_loop(0, planes - 1, faces, k[0, rows, :], unroll=8)
 
     copies[1].wait()
     copies[2].wait()
@@ -182,7 +182,7 @@
                 ]
         return c
 
-    lax.fori_loop(0, n // 2, project, 0, unroll=4)
+    lax.fori_loop(0, n // 2, project, 0, unroll=8)
     tiled = jnp.concatenate([w_ref[...]] * share, axis=0)
     block = lax.broadcasted_iota(jnp.int32, tiled.shape, 0) // R
     total = None
@@ -431,7 +431,7 @@
             out[a, e * R:(e + 1) * R, :] = y[:, e * layers:(e + 1) * layers]
         return c
 
-    lax.fori_loop(0, R // 2, body, 0, unroll=4)
+    lax.fori_loop(0, R // 2, body, 0, unroll=16)
 
 
 def radial_sum_kernel(got, g2, out):
@@ -482,7 +482,7 @@
             second[pl.ds(at, m), :] = got[:, e * layers:(e + 1) * layers]
         return c
 
-    lax.fori_loop(0, R // 2, widen_lat, 0, unroll=4)
+    lax.fori_loop(0, R // 2, widen_lat, 0, unroll=16)
     lonl = stack_left(lon[...])
 
     def widen_lon(j, c):
@@ -495,7 +495,7 @@
             err[at, :] = t[at, :] - got[:, e * layers:(e + 1) * layers]
         return c
 
-    lax.fori_loop(0, m // 2, widen_lon, 0, unroll=4)
+    lax.fori_loop(0, m // 2, widen_lon, 0, unroll=16)
 
 
 def exchange(parts, axis):

time: 181 us -> 179 us (0.989)
  Pallas kernels: 43.9 us -> 42 us
where the time goes in v5:
time: 179 us; the launch traced here: 178 us
  blocking collectives  81.3 us (45%)
  Pallas kernels  42 us (23%)
  starting transfers between devices  29.7 us (17%)
  waiting for transfers between devices  20.6 us (12%)
  local copies, waits for them, and re-layouts  3.6 us (2%)
    all_to_all x6, blocking collectives, exchange(): return lax.all_to_all(parts, axis, 0, 0, tiled=True)  81.3 us
    pallas_call x12, Pallas kernels, call(): pl.pallas_call(kernel, out_shape=tuple((jax.ShapeDtypeStruct(o, jnp.float...  19.6 us
    pallas_call x1, Pallas kernels, conduct(): pl.pallas_call(functools.partial(conduct_kernel, n, m, lat), out_shape=(j...  17.7 us
    all_to_all x3, starting transfers between devices, exchange(): return lax.all_to_all(parts, axis, 0, 0, tiled=True)  14.8 us
    all_to_all x3, waiting for transfers between devices, exchange(): return lax.all_to_all(parts, axis, 0, 0, tiled=True)  12.8 us
    ppermute x1, starting transfers between devices, conduct(): south = lax.ppermute(high, 'lat', north_to)  5.22 us
    pallas_call x2, Pallas kernels, pack(): pl.pallas_call(kernel, grid=(1,), out_shape=(shape, shape), in_specs=[spe...  4.69 us
    ppermute x1, starting transfers between devices, conduct(): lax.ppermute(jnp.concatenate([below[:, m - W:], above[:, m - W:]], 1), 'l...  4.12 us
  transfers between devices with their start and end apart: 9, of which 7 were waited for; matrix products, arithmetic and copies ran while one was open for 1% of the time, Pallas kernels for 5%

profile of v5, /device:TPU:1, one launch (start us, length us, event | category | flops | bytes accessed | tf_op | source)
XLA Modules:
  0.0 178.1 jit_solution(12024283278672528812)
XLA Ops:
  0.6 2.1 %pack_lon.1 = (f32[11,64,128]{2,1,0:T(8,128)}, f32[11,64,128]{2,1,0:T(8,128)}) custom-call(f32[64,64,128]{2,1,0:T(8,128)} %t_ref.1, f32[64,64,128]{2,1,0:T(8,128)} %k_ref.1, f32[64,64,128]{2,1,0:T(8,128)} %s_ref.1, f32[64,64,128]{2,1,0:T(8,128)} %t_ref.1, f32[64,64,128]{2,1,0:T(8,128)} %k_ref.1, f32[64,64,128]{2,1,0:T(8,128)} %s_ref.1), custom_call_target="tpu_custom_call" | custom-call | tf_op jit(solution)/shard_map/pack_lon/pallas_call | solution.py:74
  2.7 3.0 %collective-permute-start = (f32[11,64,128]{2,1,0:T(8,128)}, f32[11,64,128]{2,1,0:T(8,128)S(1)}, u32[]{:S(2)}, u32[]{:S(2)}) collective-permute-start(f32[11,64,128]{2,1,0:T(8,128)} %get-tuple-element.30), channel_id=1, source_target_pairs={{0,8},{8,16},{16,24},{24,32},{32,40},{40,48},{48,56},{56,64},{64,7... | collective-permute-start | bytes 1081352 | tf_op jit(solution)/shard_map/ppermute | solution.py:207
  5.8 0.0 collective-permute-start.1
  5.8 2.6 %pack_lat.1 = (f32[11,64,128]{2,1,0:T(8,128)}, f32[11,64,128]{2,1,0:T(8,128)}) custom-call(f32[64,64,128]{2,1,0:T(8,128)} %t_ref.1, f32[64,64,128]{2,1,0:T(8,128)} %k_ref.1, f32[64,64,128]{2,1,0:T(8,128)} %s_ref.1, f32[64,64,128]{2,1,0:T(8,128)} %t_ref.1, f32[64,64,128]{2,1,0:T(8,128)} %k_ref.1, f32[64,64,128]{2,1,0:T(8,128)} %s_ref.1), custom_call_target="tpu_custom_call" | custom-call | tf_op jit(solution)/shard_map/pack_lat/pallas_call | solution.py:74
  8.4 5.2 %collective-permute-start.2 = (f32[11,64,128]{2,1,0:T(8,128)}, f32[11,64,128]{2,1,0:T(8,128)S(1)}, u32[]{:S(2)}, u32[]{:S(2)}) collective-permute-start(f32[11,64,128]{2,1,0:T(8,128)} %get-tuple-element.32), channel_id=1, source_target_pairs={{0,1},{1,2},{2,3},{3,4},{4,5},{5,6},{6,7},{8,9},{9,10},{10,11},{11... | collective-permute-start | bytes 1081352 | tf_op jit(solution)/shard_map/ppermute | solution.py:204
  13.6 1.3 collective-permute-start.3
  14.9 0.0 collective-permute-done.below_ref
  14.9 0.0 copy-start.5
  14.9 2.8 %collective-permute-done.1.above_ref = f32[11,64,128]{2,1,0:T(8,128)S(1)} collective-permute-done((f32[11,64,128]{2,1,0:T(8,128)}, f32[11,64,128]{2,1,0:T(8,128)S(1)}, u32[]{:S(2)}, u32[]{:S(2)}) %collective-permute-start.1) | collective-permute-done | bytes 360480 | tf_op jit(solution)/shard_map/ppermute | solution.py:208
  17.8 4.1 %collective-permute-start.4 = (f32[11,8,128]{2,1,0:T(8,128)S(1)}, f32[11,8,128]{2,1,0:T(8,128)S(1)}, u32[]{:S(2)}, u32[]{:S(2)}) collective-permute-start(f32[11,8,128]{2,1,0:T(8,128)S(1)} %pad_maximum_fusion), channel_id=1, source_target_pairs={{0,1},{1,2},{2,3},{3,4},{4,5},{5,6},{6,7},{8,9},{9,10},{10,11},{11... | collective-permute-start | bytes 135176 | tf_op jit(solution)/shard_map/ppermute | solution.py:209
  22.0 1.3 collective-permute-start.5
  23.3 3.4 %collective-permute-done.2.south_ref = f32[11,64,128]{2,1,0:T(8,128)S(1)} collective-permute-done((f32[11,64,128]{2,1,0:T(8,128)}, f32[11,64,128]{2,1,0:T(8,128)S(1)}, u32[]{:S(2)}, u32[]{:S(2)}) %collective-permute-start.2) | collective-permute-done | bytes 360480 | tf_op jit(solution)/shard_map/ppermute | solution.py:204
  26.7 0.0 collective-permute-done.3.north_ref
  26.7 0.9 collective-permute-done.4.csouth_ref
  27.5 0.7 collective-permute-done.5.cnorth_ref
  28.2 0.0 copy-done.5
  28.3 0.0 copy-done.7
  28.3 0.6 copy-done.10
  28.9 17.7 %conduct.1 = (f32[64,64,128]{2,1,0:T(8,128)}, f32[512,128]{1,0:T(8,128)}) custom-call(f32[64,64,128]{2,1,0:T(8,128)} %t_ref.1, f32[64,64,128]{2,1,0:T(8,128)} %k_ref.1, f32[64,64,128]{2,1,0:T(8,128)} %s_ref.1, f32[11,64,128]{2,1,0:T(8,128)} %copy-done.5, f32[11,64,128]{2,1,0:T(8,128)} %copy-done.6, f32[11,64,128]{2,1,0:T(8,128)} %copy-done.7, ...), custom_call_target="tpu_custom_call" | custom-call | tf_op jit(solution)/shard_map/conduct/pallas_call | solution.py:214
  46.6 23.6 %all_to_all.45.got = f32[8,64,128]{2,1,0:T(8,128)S(1)} all-to-all(f32[8,64,128]{2,1,0:T(8,128)} %bitcast.25), channel_id=1, replica_groups=mesh['lon'=16,'lat'=8] {'lat'}, dimensions={0} | all-to-all | bytes 524288 | tf_op jit(solution)/shard_map/all_to_all | solution.py:502
  70.2 0.2 lon_project.1
  70.3 11.6 %all_to_all.46.got = f32[16,32,128]{2,1,0:T(8,128)S(1)} all-to-all(f32[16,32,128]{2,1,0:T(8,128)S(1)} %get-tuple-element.36), channel_id=1, replica_groups=mesh['lon'=16,'lat'=8] {'lon'}, dimensions={0} | all-to-all | bytes 524288 | tf_op jit(solution)/shard_map/all_to_all | solution.py:502
  81.9 0.9 lon_block.1
  82.8 3.5 %all-to-all-start.2 = ((f32[8,16,128]{2,1,0:T(8,128)}), f32[8,16,128]{2,1,0:T(8,128)S(1)}, u32[]{:S(2)}, u32[]{:S(2)}) async-start(f32[8,16,128]{2,1,0:T(8,128)} %lon_block.1), calls=%async_computation.2 | async-start | bytes 131072 | tf_op jit(solution)/shard_map/all_to_all | solution.py:502
  86.4 0.0 copy-done.2
  86.4 0.0 copy-start
  86.4 1.6 copy-done
  88.0 3.1 %radial.1.rt = f32[2,512,128]{2,1,0:T(8,128)S(1)} custom-call(f32[4096,128]{1,0:T(8,128)S(1)} %bitcast.14, f32[32,128]{1,0:T(8,128)S(1)} %bitcast.23), custom_call_target="tpu_custom_call" | custom-call | bytes 12000000 | tf_op jit(solution)/shard_map/radial/pallas_call | solution.py:253
  91.1 1.9 %all-to-all-done.2.got = f32[8,16,128]{2,1,0:T(8,128)S(1)} async-done(((f32[8,16,128]{2,1,0:T(8,128)}), f32[8,16,128]{2,1,0:T(8,128)S(1)}, u32[]{:S(2)}, u32[]{:S(2)}) %all-to-all-start.2) | async-done | bytes 65568 | tf_op jit(solution)/shard_map/all_to_all | solution.py:502
  93.0 0.6 lat_modes.1
  93.5 12.3 %all_to_all.47.got = f32[16,40,128]{2,1,0:T(8,128)S(1)} all-to-all(f32[16,40,128]{2,1,0:T(8,128)S(1)} %get-tuple-element.38), channel_id=1, replica_groups=mesh['lon'=16,'lat'=8] {'lon'}, dimensions={0} | all-to-all | bytes 655360 | tf_op jit(solution)/shard_map/all_to_all | solution.py:502
  105.8 1.4 lat_project.1
  107.3 10.8 %all_to_all.48.got = f32[8,32,128]{2,1,0:T(8,128)S(1)} all-to-all(f32[8,32,128]{2,1,0:T(8,128)S(1)} %get-tuple-element.40), channel_id=1, replica_groups=mesh['lon'=16,'lat'=8] {'lat'}, dimensions={0} | all-to-all | bytes 262144 | tf_op jit(solution)/shard_map/all_to_all | solution.py:502
  118.1 1.0 lat_block.1
  119.0 5.1 %all-to-all-start.5 = ((f32[16,16,128]{2,1,0:T(8,128)}), f32[16,16,128]{2,1,0:T(8,128)S(1)}, u32[]{:S(2)}, u32[]{:S(2)}) async-start(f32[16,16,128]{2,1,0:T(8,128)} %lat_block.1), calls=%async_computation.5 | async-start | bytes 262144 | tf_op jit(solution)/shard_map/all_to_all | solution.py:502
  124.1 0.0 copy-done.1
  124.1 2.6 %lon_sums.1.lp = f32[2048,128]{1,0:T(8,128)S(1)} custom-call(f32[4096,128]{1,0:T(8,128)S(1)} %bitcast.15, f32[32,64]{1,0:T(8,128)S(1)} %get-tuple-element.42.lont), custom_call_target="tpu_custom_call" | custom-call | bytes 12000000 | tf_op jit(solution)/shard_map/lon_sums/pallas_call | solution.py:253
  126.8 3.6 %all-to-all-done.5.got = f32[16,16,128]{2,1,0:T(8,128)S(1)} async-done(((f32[16,16,128]{2,1,0:T(8,128)}), f32[16,16,128]{2,1,0:T(8,128)S(1)}, u32[]{:S(2)}, u32[]{:S(2)}) %all-to-all-start.5) | async-done | bytes 131104 | tf_op jit(solution)/shard_map/all_to_all | solution.py:502
  130.4 0.5 radial_modes.1
  130.9 12.6 %all_to_all.49.got = f32[16,64,128]{2,1,0:T(8,128)S(1)} all-to-all(f32[16,64,128]{2,1,0:T(8,128)S(1)} %get-tuple-element.43), channel_id=1, replica_groups=mesh['lon'=16,'lat'=8] {'lon'}, dimensions={0} | all-to-all | bytes 1048576 | tf_op jit(solution)/shard_map/all_to_all | solution.py:502
  143.5 10.4 %all_to_all.50.got = f32[8,72,128]{2,1,0:T(8,128)S(1)} all-to-all(f32[8,72,128]{2,1,0:T(8,128)S(1)} %radial_sum.1), channel_id=1, replica_groups=mesh['lon'=16,'lat'=8] {'lat'}, dimensions={0} | all-to-all | bytes 589824 | tf_op jit(solution)/shard_map/all_to_all | solution.py:502
  153.9 0.9 radial_spread.1
  154.8 6.1 %all-to-all-start.8 = ((f32[16,64,128]{2,1,0:T(8,128)}), f32[16,64,128]{2,1,0:T(8,128)S(1)}, u32[]{:S(2)}, u32[]{:S(2)}) async-start(f32[16,64,128]{2,1,0:T(8,128)} %get-tuple-element.45), calls=%async_computation.8 | async-start | bytes 1048576 | tf_op jit(solution)/shard_map/all_to_all | solution.py:502
  160.9 0.7 copy.13
  161.6 1.0 lat_factor.1
  162.6 0.7 copy.14
  163.3 7.3 %all-to-all-done.8 = f32[16,64,128]{2,1,0:T(8,128)S(1)} async-done(((f32[16,64,128]{2,1,0:T(8,128)}), f32[16,64,128]{2,1,0:T(8,128)S(1)}, u32[]{:S(2)}, u32[]{:S(2)}) %all-to-all-start.8) | async-done | bytes 524320 | tf_op jit(solution)/shard_map/all_to_all | solution.py:502
  170.6 7.5 %last.1 = (f32[4096,128]{1,0:T(8,128)}, f32[32,128]{1,0:T(8,128)}, f32[1024,32]{1,0:T(8,128)}) custom-call(f32[1024,128]{1,0:T(8,128)S(1)} %bitcast.17, f32[32,32]{1,0:T(8,128)S(1)} %get-tuple-element.48.inv2, f32[64,32]{1,0:T(8,128)S(1)} %get-tuple-element.57.lat, f32[64,32]{1,0:T(8,128)S(1)} %get-tuple-element.56.lon, f32[32,128]{1,0:T(8,128)S(1)} %bitcast.20, ...), custom_call_target="tpu_custom_call" | custom-call | tf_op jit(solution)/shard_map/last/pallas_call | solution.py:253
  (20 shorter events, 0.1 us)
Async XLA Ops:
  2.7 12.2 %collective-permute-start = (f32[11,64,128]{2,1,0:T(8,128)}, f32[11,64,128]{2,1,0:T(8,128)S(1)}, u32[]{:S(2)}, u32[]{:S(2)}) collective-permute-start(f32[11,64,128]{2,1,0:T(8,128)} %get-tuple-element.30), channel_id=1, source_target_pairs={{0,8},{8,16},{16,24},{24,32},{32,40},{40,48},{48,56},{56,64},{64,7... | collective-permute-start | bytes 1081352 | tf_op jit(solution)/shard_map/ppermute | solution.py:207
  5.8 12.0 %collective-permute-start.1 = (f32[11,64,128]{2,1,0:T(8,128)}, f32[11,64,128]{2,1,0:T(8,128)S(1)}, u32[]{:S(2)}, u32[]{:S(2)}) collective-permute-start(f32[11,64,128]{2,1,0:T(8,128)} %get-tuple-element.31), channel_id=1, source_target_pairs={{8,0},{16,8},{24,16},{32,24},{40,32},{48,40},{56,48},{64,56},{72,6... | collective-permute-start | bytes 1081352 | tf_op jit(solution)/shard_map/ppermute | solution.py:208
  8.4 18.3 %collective-permute-start.2 = (f32[11,64,128]{2,1,0:T(8,128)}, f32[11,64,128]{2,1,0:T(8,128)S(1)}, u32[]{:S(2)}, u32[]{:S(2)}) collective-permute-start(f32[11,64,128]{2,1,0:T(8,128)} %get-tuple-element.32), channel_id=1, source_target_pairs={{0,1},{1,2},{2,3},{3,4},{4,5},{5,6},{6,7},{8,9},{9,10},{10,11},{11... | collective-permute-start | bytes 1081352 | tf_op jit(solution)/shard_map/ppermute | solution.py:204
  13.6 13.1 %collective-permute-start.3 = (f32[11,64,128]{2,1,0:T(8,128)}, f32[11,64,128]{2,1,0:T(8,128)S(1)}, u32[]{:S(2)}, u32[]{:S(2)}) collective-permute-start(f32[11,64,128]{2,1,0:T(8,128)} %get-tuple-element.33), channel_id=1, source_target_pairs={{1,0},{2,1},{3,2},{4,3},{5,4},{6,5},{7,6},{9,8},{10,9},{11,10},{12... | collective-permute-start | bytes 1081352 | tf_op jit(solution)/shard_map/ppermute | solution.py:205
  14.9 13.4 %copy-start.5 = (f32[11,64,128]{2,1,0:T(8,128)}, f32[11,64,128]{2,1,0:T(8,128)S(1)}, u32[]{:S(2)}) copy-start(f32[11,64,128]{2,1,0:T(8,128)S(1)} %collective-permute-done.below_ref) | copy-start | bytes 1081348
  17.8 10.5 %copy-start.6 = (f32[11,64,128]{2,1,0:T(8,128)}, f32[11,64,128]{2,1,0:T(8,128)S(1)}, u32[]{:S(2)}) copy-start(f32[11,64,128]{2,1,0:T(8,128)S(1)} %collective-permute-done.1.above_ref) | copy-start | bytes 1081348
  17.8 9.7 %collective-permute-start.4 = (f32[11,8,128]{2,1,0:T(8,128)S(1)}, f32[11,8,128]{2,1,0:T(8,128)S(1)}, u32[]{:S(2)}, u32[]{:S(2)}) collective-permute-start(f32[11,8,128]{2,1,0:T(8,128)S(1)} %pad_maximum_fusion), channel_id=1, source_target_pairs={{0,1},{1,2},{2,3},{3,4},{4,5},{5,6},{6,7},{8,9},{9,10},{10,11},{11... | collective-permute-start | bytes 135176 | tf_op jit(solution)/shard_map/ppermute | solution.py:209
  22.0 6.3 %collective-permute-start.5 = (f32[11,8,128]{2,1,0:T(8,128)S(1)}, f32[11,8,128]{2,1,0:T(8,128)S(1)}, u32[]{:S(2)}, u32[]{:S(2)}) collective-permute-start(f32[11,8,128]{2,1,0:T(8,128)S(1)} %pad_maximum_fusion.1), channel_id=1, source_target_pairs={{1,0},{2,1},{3,2},{4,3},{5,4},{6,5},{7,6},{9,8},{10,9},{11,10},{12... | collective-permute-start | bytes 135176 | tf_op jit(solution)/shard_map/ppermute | solution.py:210
  26.7 1.6 copy-start.7
  26.7 1.6 copy-start.8
  27.5 0.8 copy-start.9
  28.2 0.6 copy-start.10
  28.9 41.3 %copy-start.4 = (f32[64,32]{0,1:T(8,128)S(1)}, f32[64,32]{0,1:T(8,128)}, u32[]{:S(2)}) copy-start(f32[64,32]{0,1:T(8,128)} %param.9) | copy-start | bytes 24580
  28.9 57.5 %copy-start.2 = (f32[128,32]{0,1:T(8,128)S(1)}, f32[128,32]{0,1:T(8,128)}, u32[]{:S(2)}) copy-start(f32[128,32]{0,1:T(8,128)} %param.11) | copy-start | bytes 49156
  82.8 23.0 %copy-start.3 = (f32[64,32]{0,1:T(8,128)S(1)}, f32[64,32]{0,1:T(8,128)}, u32[]{:S(2)}) copy-start(f32[64,32]{0,1:T(8,128)} %param.10) | copy-start | bytes 24580
  82.8 10.2 %all-to-all-start.2 = ((f32[8,16,128]{2,1,0:T(8,128)}), f32[8,16,128]{2,1,0:T(8,128)S(1)}, u32[]{:S(2)}, u32[]{:S(2)}) async-start(f32[8,16,128]{2,1,0:T(8,128)} %lon_block.1), calls=%async_computation.2 | async-start | bytes 131072 | tf_op jit(solution)/shard_map/all_to_all | solution.py:502
  86.4 1.6 copy-start
  88.0 36.2 %copy-start.1 = (f32[64,64,128]{2,1,0:T(8,128)S(1)}, f32[64,64,128]{2,1,0:T(8,128)}, u32[]{:S(2)}) copy-start(f32[64,64,128]{2,1,0:T(8,128)} %get-tuple-element.54) | copy-start | bytes 6291460
  119.0 11.3 %all-to-all-start.5 = ((f32[16,16,128]{2,1,0:T(8,128)}), f32[16,16,128]{2,1,0:T(8,128)S(1)}, u32[]{:S(2)}, u32[]{:S(2)}) async-start(f32[16,16,128]{2,1,0:T(8,128)} %lat_block.1), calls=%async_computation.5 | async-start | bytes 262144 | tf_op jit(solution)/shard_map/all_to_all | solution.py:502
  154.8 15.8 %all-to-all-start.8 = ((f32[16,64,128]{2,1,0:T(8,128)}), f32[16,64,128]{2,1,0:T(8,128)S(1)}, u32[]{:S(2)}, u32[]{:S(2)}) async-start(f32[16,64,128]{2,1,0:T(8,128)} %get-tuple-element.45), calls=%async_computation.8 | async-start | bytes 1048576 | tf_op jit(solution)/shard_map/all_to_all | solution.py:502

commit v6 on v5

--- a/solution.py
+++ b/solution.py
@@ -434,18 +434,8 @@
     lax.fori_loop(0, R // 2, body, 0, unroll=16)
 
 
-def radial_sum_kernel(got, g2, out):
-    total = add_up(got)
-    for i in range(out.shape[0]):
-        out[i, 0:total.shape[0]] = total
-        out[i, total.shape[0]:] = g2[...]
-
-
-def radial_spread_kernel(got, out, g2):
-    total = add_up(got)
-    rows = out.shape[1]
-    send_all(out, total[:rows])
-    g2[...] = total[rows:]
+def radial_sum_kernel(got, out):
+    send_all(out, add_up(got))
 
 
 def lat_factor_kernel(g2, b2, inv, lat):
@@ -544,15 +534,16 @@
         [(lon, share * R, layers), (R, m), (R // 4, 4 * R)],
         [exchange(parts, "lon"), lp],
     )
-    (parts,) = call(
-        radial_sum_kernel, "radial_sum", [(lat, share * R + R // 4, layers)],
-        [exchange(parts, "lon"), g2],
-    )
-    parts, g2 = call(
-        radial_spread_kernel, "radial_spread", [(lon, share * R, layers), (R // 4, 4 * R)],
-        [exchange(parts, "lat")],
-    )
-    got = exchange(parts, "lon")
+    both = ("lon", "lat")
+    got = exchange(parts.reshape(lon * lat, share * R // lat, layers), both)
+    hop = 1
+    while hop < lat:
+        g2 = g2 + lax.ppermute(g2, "lat", [(i, i ^ hop) for i in range(lat)])
+        hop *= 2
+        if 2 * hop == lat:
+            g2, got = lax.optimization_barrier((g2, got))
+    (parts,) = call(radial_sum_kernel, "radial_sum", [got.shape], [got])
+    got = exchange(parts, both)
     inv2, new_lat = call(
         lat_factor_kernel, "lat_factor", [(R, R), (m, R)], [g2, b2], cost=cost(4)
     )

time: 179 us -> 179 us (level)
  blocking collectives: 81.3 us -> 58.3 us
  starting transfers between devices: 29.7 us -> 41.4 us
  waiting for transfers between devices: 20.6 us -> 31.4 us
    all_to_all x6 -> x4, blocking collectives: 81.3 us -> 58.3 us  [exchange(): return lax.all_to_all(parts, axis, 0, 0, tiled=True)]
    ppermute x0 -> x3, starting transfers between devices: none -> 7.85 us  [local(): g2 = g2 + lax.ppermute(g2, 'lat', [(i, i ^ hop) for i in range(lat)])]
    ppermute x0 -> x3, waiting for transfers between devices: none -> 7.82 us  [local(): g2 = g2 + lax.ppermute(g2, 'lat', [(i, i ^ hop) for i in range(lat)])]
    all_to_all x3 -> x4, starting transfers between devices: 14.8 us -> 18.6 us  [exchange(): return lax.all_to_all(parts, axis, 0, 0, tiled=True)]
    all_to_all x3 -> x4, waiting for transfers between devices: 12.8 us -> 15.7 us  [exchange(): return lax.all_to_all(parts, axis, 0, 0, tiled=True)]
    unnamed x24 -> x26, local copies, waits for them, and re-layouts: 3.58 us -> 4.37 us
    pallas_call x12 -> x11, Pallas kernels: 19.6 us -> 19.7 us  [call(): pl.pallas_call(kernel, out_shape=tuple((jax.ShapeDtypeStruct(o, jnp.float...]
  transfers between devices with their start and end apart: 9 -> 13, of which waited for: 7 -> 11; matrix products, arithmetic and copies ran while one was open for 1% -> 1% of each run, Pallas kernels for 5% -> 5%
where the time goes in v6:
time: 179 us; the launch traced here: 178 us
  blocking collectives  58.3 us (33%)
  Pallas kernels  42 us (23%)
  starting transfers between devices  41.4 us (23%)
  waiting for transfers between devices  31.4 us (18%)
  local copies, waits for them, and re-layouts  4.39 us (2%)
    all_to_all x4, blocking collectives, exchange(): return lax.all_to_all(parts, axis, 0, 0, tiled=True)  58.3 us
    pallas_call x11, Pallas kernels, call(): pl.pallas_call(kernel, out_shape=tuple((jax.ShapeDtypeStruct(o, jnp.float...  19.7 us
    all_to_all x4, starting transfers between devices, exchange(): return lax.all_to_all(parts, axis, 0, 0, tiled=True)  18.6 us
    pallas_call x1, Pallas kernels, conduct(): pl.pallas_call(functools.partial(conduct_kernel, n, m, lat), out_shape=(j...  17.7 us
    all_to_all x4, waiting for transfers between devices, exchange(): return lax.all_to_all(parts, axis, 0, 0, tiled=True)  15.7 us
    ppermute x3, starting transfers between devices, local(): g2 = g2 + lax.ppermute(g2, 'lat', [(i, i ^ hop) for i in range(lat)])  7.85 us
    ppermute x3, waiting for transfers between devices, local(): g2 = g2 + lax.ppermute(g2, 'lat', [(i, i ^ hop) for i in range(lat)])  7.82 us
    ppermute x1, starting transfers between devices, conduct(): south = lax.ppermute(high, 'lat', north_to)  5.22 us
  transfers between devices with their start and end apart: 13, of which 11 were waited for; matrix products, arithmetic and copies ran while one was open for 1% of the time, Pallas kernels for 5%

profile of v6, /device:TPU:1, one launch (start us, length us, event | category | flops | bytes accessed | tf_op | source)
XLA Modules:
  0.0 178.4 jit_solution(17835996876604756972)
XLA Ops:
  0.6 2.1 %pack_lon.1 = (f32[11,64,128]{2,1,0:T(8,128)}, f32[11,64,128]{2,1,0:T(8,128)}) custom-call(f32[64,64,128]{2,1,0:T(8,128)} %t_ref.1, f32[64,64,128]{2,1,0:T(8,128)} %k_ref.1, f32[64,64,128]{2,1,0:T(8,128)} %s_ref.1, f32[64,64,128]{2,1,0:T(8,128)} %t_ref.1, f32[64,64,128]{2,1,0:T(8,128)} %k_ref.1, f32[64,64,128]{2,1,0:T(8,128)} %s_ref.1), custom_call_target="tpu_custom_call" | custom-call | tf_op jit(solution)/shard_map/pack_lon/pallas_call | solution.py:74
  2.7 3.0 %collective-permute-start = (f32[11,64,128]{2,1,0:T(8,128)}, f32[11,64,128]{2,1,0:T(8,128)S(1)}, u32[]{:S(2)}, u32[]{:S(2)}) collective-permute-start(f32[11,64,128]{2,1,0:T(8,128)} %get-tuple-element.30), channel_id=1, source_target_pairs={{0,8},{8,16},{16,24},{24,32},{32,40},{40,48},{48,56},{56,64},{64,7... | collective-permute-start | bytes 1081352 | tf_op jit(solution)/shard_map/ppermute | solution.py:207
  5.8 2.6 %pack_lat.1 = (f32[11,64,128]{2,1,0:T(8,128)}, f32[11,64,128]{2,1,0:T(8,128)}) custom-call(f32[64,64,128]{2,1,0:T(8,128)} %t_ref.1, f32[64,64,128]{2,1,0:T(8,128)} %k_ref.1, f32[64,64,128]{2,1,0:T(8,128)} %s_ref.1, f32[64,64,128]{2,1,0:T(8,128)} %t_ref.1, f32[64,64,128]{2,1,0:T(8,128)} %k_ref.1, f32[64,64,128]{2,1,0:T(8,128)} %s_ref.1), custom_call_target="tpu_custom_call" | custom-call | tf_op jit(solution)/shard_map/pack_lat/pallas_call | solution.py:74
  8.3 5.2 %collective-permute-start.2 = (f32[11,64,128]{2,1,0:T(8,128)}, f32[11,64,128]{2,1,0:T(8,128)S(1)}, u32[]{:S(2)}, u32[]{:S(2)}) collective-permute-start(f32[11,64,128]{2,1,0:T(8,128)} %get-tuple-element.32), channel_id=1, source_target_pairs={{0,1},{1,2},{2,3},{3,4},{4,5},{5,6},{6,7},{8,9},{9,10},{10,11},{11... | collective-permute-start | bytes 1081352 | tf_op jit(solution)/shard_map/ppermute | solution.py:204
  13.6 1.3 collective-permute-start.3
  14.9 0.0 copy-start.6
  14.9 2.9 %collective-permute-done.1.above_ref = f32[11,64,128]{2,1,0:T(8,128)S(1)} collective-permute-done((f32[11,64,128]{2,1,0:T(8,128)}, f32[11,64,128]{2,1,0:T(8,128)S(1)}, u32[]{:S(2)}, u32[]{:S(2)}) %collective-permute-start.1) | collective-permute-done | bytes 360480 | tf_op jit(solution)/shard_map/ppermute | solution.py:208
  17.8 4.1 %collective-permute-start.4 = (f32[11,8,128]{2,1,0:T(8,128)S(1)}, f32[11,8,128]{2,1,0:T(8,128)S(1)}, u32[]{:S(2)}, u32[]{:S(2)}) collective-permute-start(f32[11,8,128]{2,1,0:T(8,128)S(1)} %pad_maximum_fusion), channel_id=1, source_target_pairs={{0,1},{1,2},{2,3},{3,4},{4,5},{5,6},{6,7},{8,9},{9,10},{10,11},{11... | collective-permute-start | bytes 135176 | tf_op jit(solution)/shard_map/ppermute | solution.py:209
  22.0 1.3 collective-permute-start.5
  23.3 3.4 %collective-permute-done.2.south_ref = f32[11,64,128]{2,1,0:T(8,128)S(1)} collective-permute-done((f32[11,64,128]{2,1,0:T(8,128)}, f32[11,64,128]{2,1,0:T(8,128)S(1)}, u32[]{:S(2)}, u32[]{:S(2)}) %collective-permute-start.2) | collective-permute-done | bytes 360480 | tf_op jit(solution)/shard_map/ppermute | solution.py:204
  26.7 0.9 collective-permute-done.4.csouth_ref
  27.5 0.7 collective-permute-done.5.cnorth_ref
  28.3 0.6 copy-done.11
  28.9 17.7 %conduct.1 = (f32[64,64,128]{2,1,0:T(8,128)}, f32[512,128]{1,0:T(8,128)}) custom-call(f32[64,64,128]{2,1,0:T(8,128)} %t_ref.1, f32[64,64,128]{2,1,0:T(8,128)} %k_ref.1, f32[64,64,128]{2,1,0:T(8,128)} %s_ref.1, f32[11,64,128]{2,1,0:T(8,128)} %copy-done.6, f32[11,64,128]{2,1,0:T(8,128)} %copy-done.7, f32[11,64,128]{2,1,0:T(8,128)} %copy-done.8, ...), custom_call_target="tpu_custom_call" | custom-call | tf_op jit(solution)/shard_map/conduct/pallas_call | solution.py:214
  46.6 23.6 %all_to_all.40.got = f32[8,64,128]{2,1,0:T(8,128)S(1)} all-to-all(f32[8,64,128]{2,1,0:T(8,128)} %bitcast.27), channel_id=1, replica_groups=mesh['lon'=16,'lat'=8] {'lat'}, dimensions={0} | all-to-all | bytes 524288 | tf_op jit(solution)/shard_map/all_to_all | solution.py:492
  70.2 0.2 lon_project.1
  70.3 11.6 %all_to_all.41.got = f32[16,32,128]{2,1,0:T(8,128)S(1)} all-to-all(f32[16,32,128]{2,1,0:T(8,128)S(1)} %get-tuple-element.36), channel_id=1, replica_groups=mesh['lon'=16,'lat'=8] {'lon'}, dimensions={0} | all-to-all | bytes 524288 | tf_op jit(solution)/shard_map/all_to_all | solution.py:492
  81.9 0.9 lon_block.1
  82.8 3.5 %all-to-all-start.2 = ((f32[8,16,128]{2,1,0:T(8,128)}), f32[8,16,128]{2,1,0:T(8,128)S(1)}, u32[]{:S(2)}, u32[]{:S(2)}) async-start(f32[8,16,128]{2,1,0:T(8,128)} %lon_block.1), calls=%async_computation.2 | async-start | bytes 131072 | tf_op jit(solution)/shard_map/all_to_all | solution.py:492
  86.4 0.0 copy-start
  86.4 1.6 copy-done
  88.0 3.1 %radial.1.rt = f32[2,512,128]{2,1,0:T(8,128)S(1)} custom-call(f32[4096,128]{1,0:T(8,128)S(1)} %bitcast.15, f32[32,128]{1,0:T(8,128)S(1)} %bitcast.25), custom_call_target="tpu_custom_call" | custom-call | bytes 12000000 | tf_op jit(solution)/shard_map/radial/pallas_call | solution.py:253
  91.1 1.9 %all-to-all-done.2.got = f32[8,16,128]{2,1,0:T(8,128)S(1)} async-done(((f32[8,16,128]{2,1,0:T(8,128)}), f32[8,16,128]{2,1,0:T(8,128)S(1)}, u32[]{:S(2)}, u32[]{:S(2)}) %all-to-all-start.2) | async-done | bytes 65568 | tf_op jit(solution)/shard_map/all_to_all | solution.py:492
  93.0 0.6 lat_modes.1
  93.5 12.3 %all_to_all.42.got = f32[16,40,128]{2,1,0:T(8,128)S(1)} all-to-all(f32[16,40,128]{2,1,0:T(8,128)S(1)} %get-tuple-element.38), channel_id=1, replica_groups=mesh['lon'=16,'lat'=8] {'lon'}, dimensions={0} | all-to-all | bytes 655360 | tf_op jit(solution)/shard_map/all_to_all | solution.py:492
  105.8 1.4 lat_project.1
  107.3 10.8 %all_to_all.43.got = f32[8,32,128]{2,1,0:T(8,128)S(1)} all-to-all(f32[8,32,128]{2,1,0:T(8,128)S(1)} %get-tuple-element.40), channel_id=1, replica_groups=mesh['lon'=16,'lat'=8] {'lat'}, dimensions={0} | all-to-all | bytes 262144 | tf_op jit(solution)/shard_map/all_to_all | solution.py:492
  118.1 1.0 lat_block.1
  119.0 5.1 %all-to-all-start.5 = ((f32[16,16,128]{2,1,0:T(8,128)}), f32[16,16,128]{2,1,0:T(8,128)S(1)}, u32[]{:S(2)}, u32[]{:S(2)}) async-start(f32[16,16,128]{2,1,0:T(8,128)} %lat_block.1), calls=%async_computation.5 | async-start | bytes 262144 | tf_op jit(solution)/shard_map/all_to_all | solution.py:492
  124.1 2.6 %lon_sums.1.lp = f32[2048,128]{1,0:T(8,128)S(1)} custom-call(f32[4096,128]{1,0:T(8,128)S(1)} %bitcast.16, f32[32,64]{1,0:T(8,128)S(1)} %get-tuple-element.42.lont), custom_call_target="tpu_custom_call" | custom-call | bytes 12000000 | tf_op jit(solution)/shard_map/lon_sums/pallas_call | solution.py:253
  126.8 3.6 %all-to-all-done.5.got = f32[16,16,128]{2,1,0:T(8,128)S(1)} async-done(((f32[16,16,128]{2,1,0:T(8,128)}), f32[16,16,128]{2,1,0:T(8,128)S(1)}, u32[]{:S(2)}, u32[]{:S(2)}) %all-to-all-start.5) | async-done | bytes 131104 | tf_op jit(solution)/shard_map/all_to_all | solution.py:492
  130.4 0.5 radial_modes.1
  130.9 0.8 copy-done.2
  131.7 3.9 %all-to-all-start.6 = ((f32[128,8,128]{2,1,0:T(8,128)}), f32[128,8,128]{2,1,0:T(8,128)S(1)}, u32[]{:S(2)}, u32[]{:S(2)}) async-start(f32[128,8,128]{2,1,0:T(8,128)} %bitcast.19), calls=%async_computation.6 | async-start | bytes 1048576 | tf_op jit(solution)/shard_map/all_to_all | solution.py:492
  135.6 3.5 %collective-permute-start.6 = (f32[8,128]{1,0:T(8,128)S(1)}, f32[8,128]{1,0:T(8,128)S(1)}, u32[]{:S(2)}, u32[]{:S(2)}) collective-permute-start(f32[8,128]{1,0:T(8,128)S(1)} %get-tuple-element.43), channel_id=1, source_target_pairs={{0,1},{1,0},{2,3},{3,2},{4,5},{5,4},{6,7},{7,6},{8,9},{9,8},{10,11... | collective-permute-start | bytes 12296 | tf_op jit(solution)/shard_map/ppermute | solution.py:541
  139.0 1.4 collective-permute-done.6
  140.5 1.2 collective-permute-start.7
  141.7 1.6 collective-permute-done.7
  143.2 6.6 %all-to-all-done.6.got = f32[128,8,128]{2,1,0:T(8,128)S(1)} async-done(((f32[128,8,128]{2,1,0:T(8,128)}), f32[128,8,128]{2,1,0:T(8,128)S(1)}, u32[]{:S(2)}, u32[]{:S(2)}) %all-to-all-start.6) | async-done | bytes 524320 | tf_op jit(solution)/shard_map/all_to_all | solution.py:492
  149.8 1.0 radial_sum.1
  150.7 6.1 %all-to-all-start.7 = ((f32[128,8,128]{2,1,0:T(8,128)}), f32[128,8,128]{2,1,0:T(8,128)S(1)}, u32[]{:S(2)}, u32[]{:S(2)}) async-start(f32[128,8,128]{2,1,0:T(8,128)} %radial_sum.1), calls=%async_computation.7 | async-start | bytes 1048576 | tf_op jit(solution)/shard_map/all_to_all | solution.py:492
  156.8 3.2 %collective-permute-start.8 = (f32[8,128]{1,0:T(8,128)S(1)}, f32[8,128]{1,0:T(8,128)S(1)}, u32[]{:S(2)}, u32[]{:S(2)}) collective-permute-start(f32[8,128]{1,0:T(8,128)S(1)} %add.10), channel_id=1, source_target_pairs={{0,4},{1,5},{2,6},{3,7},{4,0},{5,1},{6,2},{7,3},{8,12},{9,13},{10,... | collective-permute-start | bytes 12296 | tf_op jit(solution)/shard_map/ppermute | solution.py:541
  160.0 0.7 copy.13
  160.7 4.9 %collective-permute-done.8 = f32[8,128]{1,0:T(8,128)S(1)} collective-permute-done((f32[8,128]{1,0:T(8,128)S(1)}, f32[8,128]{1,0:T(8,128)S(1)}, u32[]{:S(2)}, u32[]{:S(2)}) %collective-permute-start.8) | collective-permute-done | bytes 4128 | tf_op jit(solution)/shard_map/ppermute | solution.py:541
  165.5 1.0 lat_factor.1
  166.5 0.7 copy.14
  167.2 3.7 %all-to-all-done.7 = f32[128,8,128]{2,1,0:T(8,128)S(1)} async-done(((f32[128,8,128]{2,1,0:T(8,128)}), f32[128,8,128]{2,1,0:T(8,128)S(1)}, u32[]{:S(2)}, u32[]{:S(2)}) %all-to-all-start.7) | async-done | bytes 524320 | tf_op jit(solution)/shard_map/all_to_all | solution.py:492
  170.9 7.5 %last.1 = (f32[4096,128]{1,0:T(8,128)}, f32[32,128]{1,0:T(8,128)}, f32[1024,32]{1,0:T(8,128)}) custom-call(f32[1024,128]{1,0:T(8,128)S(1)} %bitcast.18, f32[32,32]{1,0:T(8,128)S(1)} %get-tuple-element.48.inv2, f32[64,32]{1,0:T(8,128)S(1)} %get-tuple-element.57.lat, f32[64,32]{1,0:T(8,128)S(1)} %get-tuple-element.56.lon, f32[32,128]{1,0:T(8,128)S(1)} %bitcast.22, ...), custom_call_target="tpu_custom_call" | custom-call | tf_op jit(solution)/shard_map/last/pallas_call | solution.py:253
  (30 shorter events, 0.1 us)
Async XLA Ops:
  2.7 12.2 %collective-permute-start = (f32[11,64,128]{2,1,0:T(8,128)}, f32[11,64,128]{2,1,0:T(8,128)S(1)}, u32[]{:S(2)}, u32[]{:S(2)}) collective-permute-start(f32[11,64,128]{2,1,0:T(8,128)} %get-tuple-element.30), channel_id=1, source_target_pairs={{0,8},{8,16},{16,24},{24,32},{32,40},{40,48},{48,56},{56,64},{64,7... | collective-permute-start | bytes 1081352 | tf_op jit(solution)/shard_map/ppermute | solution.py:207
  5.8 12.0 %collective-permute-start.1 = (f32[11,64,128]{2,1,0:T(8,128)}, f32[11,64,128]{2,1,0:T(8,128)S(1)}, u32[]{:S(2)}, u32[]{:S(2)}) collective-permute-start(f32[11,64,128]{2,1,0:T(8,128)} %get-tuple-element.31), channel_id=1, source_target_pairs={{8,0},{16,8},{24,16},{32,24},{40,32},{48,40},{56,48},{64,56},{72,6... | collective-permute-start | bytes 1081352 | tf_op jit(solution)/shard_map/ppermute | solution.py:208
  8.3 18.3 %collective-permute-start.2 = (f32[11,64,128]{2,1,0:T(8,128)}, f32[11,64,128]{2,1,0:T(8,128)S(1)}, u32[]{:S(2)}, u32[]{:S(2)}) collective-permute-start(f32[11,64,128]{2,1,0:T(8,128)} %get-tuple-element.32), channel_id=1, source_target_pairs={{0,1},{1,2},{2,3},{3,4},{4,5},{5,6},{6,7},{8,9},{9,10},{10,11},{11... | collective-permute-start | bytes 1081352 | tf_op jit(solution)/shard_map/ppermute | solution.py:204
  13.6 13.1 %collective-permute-start.3 = (f32[11,64,128]{2,1,0:T(8,128)}, f32[11,64,128]{2,1,0:T(8,128)S(1)}, u32[]{:S(2)}, u32[]{:S(2)}) collective-permute-start(f32[11,64,128]{2,1,0:T(8,128)} %get-tuple-element.33), channel_id=1, source_target_pairs={{1,0},{2,1},{3,2},{4,3},{5,4},{6,5},{7,6},{9,8},{10,9},{11,10},{12... | collective-permute-start | bytes 1081352 | tf_op jit(solution)/shard_map/ppermute | solution.py:205
  14.9 13.4 %copy-start.6 = (f32[11,64,128]{2,1,0:T(8,128)}, f32[11,64,128]{2,1,0:T(8,128)S(1)}, u32[]{:S(2)}) copy-start(f32[11,64,128]{2,1,0:T(8,128)S(1)} %collective-permute-done.below_ref) | copy-start | bytes 1081348
  17.8 10.5 %copy-start.7 = (f32[11,64,128]{2,1,0:T(8,128)}, f32[11,64,128]{2,1,0:T(8,128)S(1)}, u32[]{:S(2)}) copy-start(f32[11,64,128]{2,1,0:T(8,128)S(1)} %collective-permute-done.1.above_ref) | copy-start | bytes 1081348
  17.8 9.7 %collective-permute-start.4 = (f32[11,8,128]{2,1,0:T(8,128)S(1)}, f32[11,8,128]{2,1,0:T(8,128)S(1)}, u32[]{:S(2)}, u32[]{:S(2)}) collective-permute-start(f32[11,8,128]{2,1,0:T(8,128)S(1)} %pad_maximum_fusion), channel_id=1, source_target_pairs={{0,1},{1,2},{2,3},{3,4},{4,5},{5,6},{6,7},{8,9},{9,10},{10,11},{11... | collective-permute-start | bytes 135176 | tf_op jit(solution)/shard_map/ppermute | solution.py:209
  22.0 6.3 %collective-permute-start.5 = (f32[11,8,128]{2,1,0:T(8,128)S(1)}, f32[11,8,128]{2,1,0:T(8,128)S(1)}, u32[]{:S(2)}, u32[]{:S(2)}) collective-permute-start(f32[11,8,128]{2,1,0:T(8,128)S(1)} %pad_maximum_fusion.1), channel_id=1, source_target_pairs={{1,0},{2,1},{3,2},{4,3},{5,4},{6,5},{7,6},{9,8},{10,9},{11,10},{12... | collective-permute-start | bytes 135176 | tf_op jit(solution)/shard_map/ppermute | solution.py:210
  26.7 1.6 copy-start.8
  26.7 1.6 copy-start.9
  27.5 0.8 copy-start.10
  28.2 0.6 copy-start.11
  28.9 41.3 %copy-start.5 = (f32[64,32]{0,1:T(8,128)S(1)}, f32[64,32]{0,1:T(8,128)}, u32[]{:S(2)}) copy-start(f32[64,32]{0,1:T(8,128)} %param.9) | copy-start | bytes 24580
  28.9 57.5 %copy-start.3 = (f32[128,32]{0,1:T(8,128)S(1)}, f32[128,32]{0,1:T(8,128)}, u32[]{:S(2)}) copy-start(f32[128,32]{0,1:T(8,128)} %param.11) | copy-start | bytes 49156
  82.8 23.0 %copy-start.4 = (f32[64,32]{0,1:T(8,128)S(1)}, f32[64,32]{0,1:T(8,128)}, u32[]{:S(2)}) copy-start(f32[64,32]{0,1:T(8,128)} %param.10) | copy-start | bytes 24580
  82.8 10.2 %all-to-all-start.2 = ((f32[8,16,128]{2,1,0:T(8,128)}), f32[8,16,128]{2,1,0:T(8,128)S(1)}, u32[]{:S(2)}, u32[]{:S(2)}) async-start(f32[8,16,128]{2,1,0:T(8,128)} %lon_block.1), calls=%async_computation.2 | async-start | bytes 131072 | tf_op jit(solution)/shard_map/all_to_all | solution.py:492
  86.4 1.6 copy-start
  88.0 36.2 %copy-start.1 = (f32[64,64,128]{2,1,0:T(8,128)S(1)}, f32[64,64,128]{2,1,0:T(8,128)}, u32[]{:S(2)}) copy-start(f32[64,64,128]{2,1,0:T(8,128)} %get-tuple-element.54) | copy-start | bytes 6291460
  119.0 11.3 %all-to-all-start.5 = ((f32[16,16,128]{2,1,0:T(8,128)}), f32[16,16,128]{2,1,0:T(8,128)S(1)}, u32[]{:S(2)}, u32[]{:S(2)}) async-start(f32[16,16,128]{2,1,0:T(8,128)} %lat_block.1), calls=%async_computation.5 | async-start | bytes 262144 | tf_op jit(solution)/shard_map/all_to_all | solution.py:492
  130.9 0.8 copy-start.2
  131.7 18.1 %all-to-all-start.6 = ((f32[128,8,128]{2,1,0:T(8,128)}), f32[128,8,128]{2,1,0:T(8,128)S(1)}, u32[]{:S(2)}, u32[]{:S(2)}) async-start(f32[128,8,128]{2,1,0:T(8,128)} %bitcast.19), calls=%async_computation.6 | async-start | bytes 1048576 | tf_op jit(solution)/shard_map/all_to_all | solution.py:492
  135.6 4.9 %collective-permute-start.6 = (f32[8,128]{1,0:T(8,128)S(1)}, f32[8,128]{1,0:T(8,128)S(1)}, u32[]{:S(2)}, u32[]{:S(2)}) collective-permute-start(f32[8,128]{1,0:T(8,128)S(1)} %get-tuple-element.43), channel_id=1, source_target_pairs={{0,1},{1,0},{2,3},{3,2},{4,5},{5,4},{6,7},{7,6},{8,9},{9,8},{10,11... | collective-permute-start | bytes 12296 | tf_op jit(solution)/shard_map/ppermute | solution.py:541
  140.5 2.8 %collective-permute-start.7 = (f32[8,128]{1,0:T(8,128)S(1)}, f32[8,128]{1,0:T(8,128)S(1)}, u32[]{:S(2)}, u32[]{:S(2)}) collective-permute-start(f32[8,128]{1,0:T(8,128)S(1)} %add.9), channel_id=1, source_target_pairs={{0,2},{1,3},{2,0},{3,1},{4,6},{5,7},{6,4},{7,5},{8,10},{9,11},{10,... | collective-permute-start | bytes 12296 | tf_op jit(solution)/shard_map/ppermute | solution.py:541
  150.7 20.2 %all-to-all-start.7 = ((f32[128,8,128]{2,1,0:T(8,128)}), f32[128,8,128]{2,1,0:T(8,128)S(1)}, u32[]{:S(2)}, u32[]{:S(2)}) async-start(f32[128,8,128]{2,1,0:T(8,128)} %radial_sum.1), calls=%async_computation.7 | async-start | bytes 1048576 | tf_op jit(solution)/shard_map/all_to_all | solution.py:492
  156.8 8.7 %collective-permute-start.8 = (f32[8,128]{1,0:T(8,128)S(1)}, f32[8,128]{1,0:T(8,128)S(1)}, u32[]{:S(2)}, u32[]{:S(2)}) collective-permute-start(f32[8,128]{1,0:T(8,128)S(1)} %add.10), channel_id=1, source_target_pairs={{0,4},{1,5},{2,6},{3,7},{4,0},{5,1},{6,2},{7,3},{8,12},{9,13},{10,... | collective-permute-start | bytes 12296 | tf_op jit(solution)/shard_map/ppermute | solution.py:541
